TPU v7x, 32 devices: a whole 2x2x4 slice. The times are simulated.
32 devices in a mesh: dp: 4 (over y, x), expert: 4 (over z), tensor: 2 (over core).
Axes of the slice: x: 2, y: 2, z: 4, core: 2. Of those that a mesh axis runs over, the one named last changes fastest.
Arguments:
- tokens: bfloat16 [2048, 4096], P(('dp', 'expert')), may hold values from -6 to 6
- cotangent: bfloat16 [2048, 4096], P(('dp', 'expert')), may hold values from -6 to 6
- routes: int32 [2048, 1], P(('dp', 'expert')), may hold values from 0 to 3; in each aligned block of 128 rows (0 to 127, 128 to 255, ...) at most 48 rows name the same one
- cluster: int32 [4, 512], replicated, may hold values from -1 to 1847, as said below
- w_gate: bfloat16 [1848, 4096], P(('expert', 'tensor'), 'dp'), may hold values from -0.09375 to 0.09375
- w_up: bfloat16 [1848, 4096], P(('expert', 'tensor'), 'dp'), may hold values from -0.09375 to 0.09375
- w_down: bfloat16 [1848, 4096], P(('expert', 'tensor'), 'dp'), may hold values from -0.25 to 0.25
Outputs:
- layer_out: bfloat16 [2048, 4096], P(('dp', 'expert'))
- grad_tokens: bfloat16 [2048, 4096], P(('dp', 'expert'))
Inputs may be any that keep to these rules, and one draw needn't show every extreme that they name: `routes`: in each aligned block of 128 rows no expert is named more than 48 times, and some block names one expert exactly 48 times; every expert is named somewhere. `cluster`: every neuron appears exactly once and each expert has 462 live slots. Slot j = q * 256 + s * 32 + k (k below 32) holds -1 or a neuron of source shard s, that is a row from s * 231 to (s + 1) * 231 - 1; shard s fills exactly 32 such slots of some experts' halves and fewer of others.
All inputs are finite; a program needn't handle non-finite values.
Results may differ from a plain program's by a relative error of at most 0.0059.
Values may be sent and summed in bfloat16 or wider, within the bound.
No kernel may reach another device: no remote copies, remote signals or barrier semaphores. Data moves between devices by JAX's collectives and lax.ppermute only.
A program may use at most 128 MiB of HBM per device.

v0:
```python
import jax
import jax.numpy as jnp
from jax import lax
from jax.sharding import PartitionSpec as P


def expert_math(x_rows, dy_rows, gate_w, up_w, down_w):
    contract = (((1,), (1,)), ((), ()))
    pre_gate = lax.dot_general(x_rows, gate_w, contract, preferred_element_type=jnp.float32)
    pre_up = lax.dot_general(x_rows, up_w, contract, preferred_element_type=jnp.float32)
    sig_gate = jax.nn.sigmoid(pre_gate)
    hidden = (pre_gate * sig_gate * pre_up).astype(jnp.bfloat16)
    out_part = jnp.dot(hidden, down_w, preferred_element_type=jnp.float32)
    grad_hidden = lax.dot_general(dy_rows, down_w, contract, preferred_element_type=jnp.float32)
    grad_gate = (grad_hidden * pre_up * sig_gate * (1.0 + pre_gate * (1.0 - sig_gate))).astype(
        jnp.bfloat16
    )
    grad_up = (grad_hidden * pre_gate * sig_gate).astype(jnp.bfloat16)
    grad_part = jnp.dot(grad_gate, gate_w, preferred_element_type=jnp.float32)
    grad_part = grad_part + jnp.dot(grad_up, up_w, preferred_element_type=jnp.float32)
    return (out_part, grad_part)


def to_tokens(dispatch_table, returned):
    contract = (((0,), (0,)), ((), ()))
    merged = lax.dot_general(dispatch_table, returned, contract, preferred_element_type=jnp.float32)
    return merged.astype(jnp.bfloat16)


def per_device(tokens, cotangent, routes, cluster, w_gate, w_up, w_down):
    shards = lax.axis_size(("expert", "tensor"))
    source = lax.axis_index(("expert", "tensor"))
    halves = lax.axis_size("tensor")
    rows_dev = w_gate.shape[0]
    width_part = w_gate.shape[1]
    n_experts = cluster.shape[0]
    half_slots = cluster.shape[1] // halves
    per_shard = half_slots // shards
    picks = cluster.reshape(shards, shards, per_shard)
    my_picks = lax.dynamic_index_in_dim(picks, source, 1, keepdims=False)
    is_live = (my_picks >= 0)[:, :, None]
    row_index = jnp.clip(my_picks - source * rows_dev, 0, rows_dev - 1).reshape(-1)

    def select_rows(weight):
        chosen = jnp.take(weight, row_index, axis=0).reshape(shards, per_shard, width_part)
        return jnp.where(is_live, chosen, jnp.zeros((), jnp.bfloat16))

    sent_gate = select_rows(w_gate)
    sent_up = select_rows(w_up)
    sent_down = select_rows(w_down)
    received = (
        lax.all_to_all(sent_gate, ("expert", "tensor"), split_axis=0, concat_axis=0, tiled=True),
        lax.all_to_all(sent_up, ("expert", "tensor"), split_axis=0, concat_axis=0, tiled=True),
        lax.all_to_all(sent_down, ("expert", "tensor"), split_axis=0, concat_axis=0, tiled=True),
    )
    part_gate = received[0].reshape(half_slots, width_part)
    part_up = received[1].reshape(half_slots, width_part)
    part_down = received[2].reshape(half_slots, width_part)
    gate_w, up_w, down_w = (
        lax.all_gather(part_gate, "dp", axis=1, tiled=True),
        lax.all_gather(part_up, "dp", axis=1, tiled=True),
        lax.all_gather(part_down, "dp", axis=1, tiled=True),
    )
    tok_count = tokens.shape[0]
    width = tokens.shape[1]
    capacity = max(2, 3 * tok_count // (2 * n_experts))
    expert_of = routes[:, 0]
    onehot = (expert_of[:, None] == jnp.arange(n_experts, dtype=jnp.int32)[None, :]).astype(
        jnp.int32
    )
    position = jnp.sum((jnp.cumsum(onehot, axis=0) - 1) * onehot, axis=1)
    slot_id = expert_of * capacity + position
    buffer_rows = n_experts * capacity
    dispatch_table = (slot_id[None, :] == jnp.arange(buffer_rows, dtype=jnp.int32)[:, None]).astype(
        jnp.bfloat16
    )
    sent_tokens = jnp.dot(dispatch_table, tokens, preferred_element_type=jnp.float32).astype(
        jnp.bfloat16
    )
    sent_grads = jnp.dot(dispatch_table, cotangent, preferred_element_type=jnp.float32).astype(
        jnp.bfloat16
    )
    sent_tokens = sent_tokens.reshape(n_experts, capacity, width)
    sent_grads = sent_grads.reshape(n_experts, capacity, width)
    x_rows, dy_rows = (
        lax.all_to_all(sent_tokens, "expert", split_axis=0, concat_axis=0, tiled=True),
        lax.all_to_all(sent_grads, "expert", split_axis=0, concat_axis=0, tiled=True),
    )
    x_rows = x_rows.reshape(buffer_rows, width)
    dy_rows = dy_rows.reshape(buffer_rows, width)
    out_part, grad_part = expert_math(x_rows, dy_rows, gate_w, up_w, down_w)
    out_total, grad_total = (
        lax.psum(out_part.astype(jnp.bfloat16), "tensor").astype(jnp.float32),
        lax.psum(grad_part.astype(jnp.bfloat16), "tensor").astype(jnp.float32),
    )
    out_back = out_total.astype(jnp.bfloat16).reshape(n_experts, capacity, width)
    grad_back = grad_total.astype(jnp.bfloat16).reshape(n_experts, capacity, width)
    out_home, grad_home = (
        lax.all_to_all(out_back, "expert", split_axis=0, concat_axis=0, tiled=True),
        lax.all_to_all(grad_back, "expert", split_axis=0, concat_axis=0, tiled=True),
    )
    layer_out = to_tokens(dispatch_table, out_home.reshape(buffer_rows, width))
    grad_out = to_tokens(dispatch_table, grad_home.reshape(buffer_rows, width))
    return (layer_out, grad_out)


def solution(mesh):
    in_specs = (
        P(("dp", "expert"), None),
        P(("dp", "expert"), None),
        P(("dp", "expert"), None),
        P(),
        P(("expert", "tensor"), "dp"),
        P(("expert", "tensor"), "dp"),
        P(("expert", "tensor"), "dp"),
    )
    out_specs = (P(("dp", "expert"), None), P(("dp", "expert"), None))
    return jax.shard_map(
        per_device, mesh=mesh, in_specs=in_specs, out_specs=out_specs, check_vma=False
    )
```

profile of v0, /device:TPU:0, one launch (start us, length us, event | category | flops | bytes accessed | tf_op | source)
XLA Modules:
  0.0 278.3 jit_solution(1469059670136298073)
XLA Ops:
  7.2 0.0 copy-start
  7.2 0.0 all-gather.4.cloned.1.call-start
  7.2 0.9 reshape.78
  8.1 0.1 min.12
  8.3 0.0 copy-start.1
  8.3 2.7 gather_fusion.2
  11.0 0.0 copy-done.1
  11.0 0.0 copy-start.2
  11.0 1.2 gather_fusion.1
  12.2 0.0 copy-done.2
  12.2 2.0 gather_fusion
  14.1 1.2 broadcast_select_fusion.2
  15.4 1.0 broadcast_select_fusion.5
  16.4 21.7 %all_to_all.35 = bf16[8,32,1024]{2,1,0:T(8,128)(2,1)} all-to-all(bf16[8,32,1024]{2,1,0:T(8,128)(2,1)S(1)} %get-tuple-element.5), channel_id=1, replica_groups=mesh['dp'=4,'expert'=4,'tensor'=2] {'expert','tensor'}, dimensions={0} | all-to-all | bytes 1048576 | tf_op jit(solution)/shard_map/all_to_all | solution.py:52
  38.1 0.0 all-gather.4.cloned.1.call-update
  38.1 0.0 all-gather.6.cloned.1.call-start
  38.1 18.5 %all_to_all.36 = bf16[8,32,1024]{2,1,0:T(8,128)(2,1)} all-to-all(bf16[8,32,1024]{2,1,0:T(8,128)(2,1)S(1)} %get-tuple-element.6), channel_id=1, replica_groups=mesh['dp'=4,'expert'=4,'tensor'=2] {'expert','tensor'}, dimensions={0} | all-to-all | bytes 1048576 | tf_op jit(solution)/shard_map/all_to_all | solution.py:53
  56.6 0.0 all-gather.6.cloned.1.call-update
  56.6 3.5 %all-to-all-start.3 = ((bf16[8,32,1024]{2,1,0:T(8,128)(2,1)}), bf16[8,32,1024]{2,1,0:T(8,128)(2,1)S(1)}, u32[]{:S(2)}, u32[]{:S(2)}) async-start(bf16[8,32,1024]{2,1,0:T(8,128)(2,1)} %get-tuple-element.7), calls=%async_computation.3 | async-start | bytes 1048576 | tf_op jit(solution)/shard_map/all_to_all | solution.py:54
  60.2 0.1 fusion.5
  60.3 0.2 reduce_window_sum.11
  60.4 0.2 select_reduce_fusion
  60.6 1.8 convolution_convert_fusion.2
  62.5 13.0 %all-to-all-done.3 = bf16[8,32,1024]{2,1,0:T(8,128)(2,1)S(1)} async-done(((bf16[8,32,1024]{2,1,0:T(8,128)(2,1)}), bf16[8,32,1024]{2,1,0:T(8,128)(2,1)S(1)}, u32[]{:S(2)}, u32[]{:S(2)}) %all-to-all-start.3) | async-done | bytes 524320 | tf_op jit(solution)/shard_map/all_to_all | solution.py:54
  75.5 3.6 %all-to-all-start = ((bf16[4,48,4096]{2,1,0:T(8,128)(2,1)}), bf16[4,48,4096]{2,1,0:T(8,128)(2,1)S(1)}, u32[]{:S(2)}, u32[]{:S(2)}) async-start(bf16[4,48,4096]{2,1,0:T(8,128)(2,1)} %bitcast.35), calls=%async_computation | async-start | bytes 3145728 | tf_op jit(solution)/shard_map/all_to_all | solution.py:86
  79.0 0.0 all-gather.8.cloned.1.call-start
  79.1 0.7 all-gather.8.cloned.1.call-update
  79.8 3.0 %convolution_convert_fusion = bf16[192,4096]{1,0:T(8,128)(2,1)} fusion(bf16[128,4096]{1,0:T(8,128)(2,1)} %param.10, s32[128]{0:T(128)S(1)} %multiply_add_fusion), kind=kOutput, calls=%fused_computation.5 | convolution fusion | flops 202137600 | bytes 2621952 | tf_op jit(solution)/shard_map/dot_general | solution.py:80
  82.8 33.3 %all-to-all-done = bf16[4,48,4096]{2,1,0:T(8,128)(2,1)S(1)} async-done(((bf16[4,48,4096]{2,1,0:T(8,128)(2,1)}), bf16[4,48,4096]{2,1,0:T(8,128)(2,1)S(1)}, u32[]{:S(2)}, u32[]{:S(2)}) %all-to-all-start) | async-done | bytes 1572896 | tf_op jit(solution)/shard_map/all_to_all | solution.py:86
  116.0 4.4 %all-to-all-start.5 = ((bf16[4,48,4096]{2,1,0:T(8,128)(2,1)}), bf16[4,48,4096]{2,1,0:T(8,128)(2,1)}, u32[]{:S(2)}, u32[]{:S(2)}) async-start(bf16[4,48,4096]{2,1,0:T(8,128)(2,1)} %bitcast.34), calls=%async_computation.5 | async-start | bytes 3145728 | tf_op jit(solution)/shard_map/all_to_all | solution.py:87
  120.5 0.0 all-reduce.3.cloned.1.call-start
  120.5 0.0 all-gather.4.cloned.1.call-done
  120.5 2.4 fusion.13
  123.0 0.0 all-gather.6.cloned.1.call-done
  123.0 2.4 fusion.14
  125.5 31.5 %all-to-all-done.5 = bf16[4,48,4096]{2,1,0:T(8,128)(2,1)} async-done(((bf16[4,48,4096]{2,1,0:T(8,128)(2,1)}), bf16[4,48,4096]{2,1,0:T(8,128)(2,1)}, u32[]{:S(2)}, u32[]{:S(2)}) %all-to-all-start.5) | async-done | bytes 1572896 | tf_op jit(solution)/shard_map/all_to_all | solution.py:87
  157.0 3.1 %fusion.15 = f32[192,256]{1,0:T(8,128)S(1)} fusion(bf16[192,4096]{1,0:T(8,128)(2,1)} %bitcast.12, bf16[256,4096]{1,0:T(8,128)(2,1)} %all-gather.8.cloned.1.call-done), kind=kOutput, calls=%fused_computation.44 | convolution fusion | flops 402653184 | bytes 3866624 | tf_op jit(solution)/shard_map/dot_general | solution.py:14
  160.1 1.8 convolution_convert_fusion.1
  161.9 0.6 fusion.1
  162.5 1.0 copy-done.3
  163.5 1.8 fusion
  165.2 0.0 all-reduce.3.cloned.1.call-update
  165.3 22.5 %all-reduce.3.cloned.1.call-done = (bf16[4,48,4096]{2,1,0:T(8,128)(2,1)}, bf16[4,48,4096]{2,1,0:T(8,128)(2,1)}) async-done(((bf16[4,48,4096]{2,1,0:T(8,128)(2,1)}, bf16[4,48,4096]{2,1,0:T(8,128)(2,1)}), (bf16[4,48,4096]{2,1,0:T(8,128)(2,1)}, bf16[4,48,4096]{2,1,0:T(8,128)(2,1)})) %all-reduce.3.cloned.1.call-update) | async-done | bytes 3145744 | tf_op jit(solution)/shard_map/psum | solution.py:93
  187.8 42.4 %all_to_all.37 = bf16[4,48,4096]{2,1,0:T(8,128)(2,1)} all-to-all(bf16[4,48,4096]{2,1,0:T(8,128)(2,1)} %get-tuple-element.3), channel_id=1, replica_groups=mesh['dp'=4,'expert'=4,'tensor'=2] {'expert'}, dimensions={0} | all-to-all | bytes 3145728 | tf_op jit(solution)/shard_map/all_to_all | solution.py:99
  230.2 3.6 %all-to-all-start.6 = ((bf16[4,48,4096]{2,1,0:T(8,128)(2,1)}), bf16[4,48,4096]{2,1,0:T(8,128)(2,1)S(1)}, u32[]{:S(2)}, u32[]{:S(2)}) async-start(bf16[4,48,4096]{2,1,0:T(8,128)(2,1)} %get-tuple-element.4), calls=%async_computation.6 | async-start | bytes 3145728 | tf_op jit(solution)/shard_map/all_to_all | solution.py:100
  233.7 2.9 %convolution_convert_fusion.4 = bf16[128,4096]{1,0:T(8,128)(2,1)} fusion(bf16[192,4096]{1,0:T(8,128)(2,1)} %bitcast.38, s32[128]{0:T(128)S(1)} %multiply_add_fusion), kind=kOutput, calls=%fused_computation.9 | convolution fusion | flops 201875456 | bytes 2621952 | tf_op jit(solution)/shard_map/dot_general | solution.py:26
  236.6 33.7 %all-to-all-done.6 = bf16[4,48,4096]{2,1,0:T(8,128)(2,1)S(1)} async-done(((bf16[4,48,4096]{2,1,0:T(8,128)(2,1)}), bf16[4,48,4096]{2,1,0:T(8,128)(2,1)S(1)}, u32[]{:S(2)}, u32[]{:S(2)}) %all-to-all-start.6) | async-done | bytes 1572896 | tf_op jit(solution)/shard_map/all_to_all | solution.py:100
  270.3 1.5 convolution_convert_fusion.3
  (18 shorter events, 0.1 us)
Async XLA Ops:
  7.2 53.5 %copy-start = (bf16[128,4096]{1,0:T(8,128)(2,1)S(1)}, bf16[128,4096]{1,0:T(8,128)(2,1)}, u32[]{:S(2)}) copy-start(bf16[128,4096]{1,0:T(8,128)(2,1)} %param.9) | copy-start | bytes 3145732
  7.2 113.3 %all-gather.4.cloned.1.call-start = ((), (), s32[]{:S(2)}) async-start(), calls=%async_computation.7 | async-start | bytes 2621440 | tf_op jit(solution)/shard_map/all_gather | solution.py:60
  8.3 2.7 copy-start.1
  11.0 1.2 copy-start.2
  16.4 43.8 %copy-start.7 = (s32[128,1]{0,1:T(1,128)S(1)}, s32[128,1]{0,1:T(1,128)}, u32[]{:S(2)}) copy-start(s32[128,1]{0,1:T(1,128)} %param.11) | copy-start | bytes 1540
  38.1 84.9 %all-gather.6.cloned.1.call-start = ((), (), s32[]{:S(2)}) async-start(), calls=%async_computation.8 | async-start | bytes 2621440 | tf_op jit(solution)/shard_map/all_gather | solution.py:61
  56.6 18.8 %all-to-all-start.3 = ((bf16[8,32,1024]{2,1,0:T(8,128)(2,1)}), bf16[8,32,1024]{2,1,0:T(8,128)(2,1)S(1)}, u32[]{:S(2)}, u32[]{:S(2)}) async-start(bf16[8,32,1024]{2,1,0:T(8,128)(2,1)} %get-tuple-element.7), calls=%async_computation.3 | async-start | bytes 1048576 | tf_op jit(solution)/shard_map/all_to_all | solution.py:54
  75.5 3.6 %copy-start.6 = (bf16[8,32,1024]{2,1,0:T(8,128)(2,1)}, bf16[8,32,1024]{2,1,0:T(8,128)(2,1)S(1)}, u32[]{:S(2)}) copy-start(bf16[8,32,1024]{2,1,0:T(8,128)(2,1)S(1)} %all-to-all-done.3) | copy-start | bytes 1572868
  75.5 40.6 %all-to-all-start = ((bf16[4,48,4096]{2,1,0:T(8,128)(2,1)}), bf16[4,48,4096]{2,1,0:T(8,128)(2,1)S(1)}, u32[]{:S(2)}, u32[]{:S(2)}) async-start(bf16[4,48,4096]{2,1,0:T(8,128)(2,1)} %bitcast.35), calls=%async_computation | async-start | bytes 3145728 | tf_op jit(solution)/shard_map/all_to_all | solution.py:86
  79.0 77.9 %all-gather.8.cloned.1.call-start = ((), (), s32[]{:S(2)}) async-start(), calls=%async_computation.9 | async-start | bytes 2621440 | tf_op jit(solution)/shard_map/all_gather | solution.py:62
  116.0 40.9 %all-to-all-start.5 = ((bf16[4,48,4096]{2,1,0:T(8,128)(2,1)}), bf16[4,48,4096]{2,1,0:T(8,128)(2,1)}, u32[]{:S(2)}, u32[]{:S(2)}) async-start(bf16[4,48,4096]{2,1,0:T(8,128)(2,1)} %bitcast.34), calls=%async_computation.5 | async-start | bytes 3145728 | tf_op jit(solution)/shard_map/all_to_all | solution.py:87
  120.5 67.3 %all-reduce.3.cloned.1.call-start = ((), (), s32[]{:S(2)}) async-start(), calls=%async_computation.10 | async-start | bytes 6291456 | tf_op jit(solution)/shard_map/psum | solution.py:93
  157.0 3.1 %copy-start.4 = (bf16[256,4096]{1,0:T(8,128)(2,1)S(1)}, bf16[256,4096]{1,0:T(8,128)(2,1)}, u32[]{:S(2)}) copy-start(bf16[256,4096]{1,0:T(8,128)(2,1)} %all-gather.8.cloned.1.call-done) | copy-start | bytes 6291460
  160.0 1.8 copy-start.5
  161.9 1.6 copy-start.3
  230.2 40.1 %all-to-all-start.6 = ((bf16[4,48,4096]{2,1,0:T(8,128)(2,1)}), bf16[4,48,4096]{2,1,0:T(8,128)(2,1)S(1)}, u32[]{:S(2)}, u32[]{:S(2)}) async-start(bf16[4,48,4096]{2,1,0:T(8,128)(2,1)} %get-tuple-element.4), calls=%async_computation.6 | async-start | bytes 3145728 | tf_op jit(solution)/shard_map/all_to_all | solution.py:100
Sparse Core Ops, SparseCore 0:
  38.2 34.2 all-gather.3
  74.3 35.2 all-gather.5
  112.1 35.2 all-gather.7
  165.4 22.3 all-reduce.2
where the time goes:
time: 279 us; the launch traced here: 278 us
  waiting for transfers between devices  135 us (48%)
  blocking collectives  82.5 us (30%)
  matrix products  21.3 us (8%)
  starting transfers between devices  15.2 us (5%)
  between operations  14 us (5%)
  local copies, waits for them, and re-layouts  7.77 us (3%)
    all_to_all x1, blocking collectives, per_device(): lax.all_to_all(out_back, 'expert', split_axis=0, concat_axis=0, tiled=True)  42.4 us
    all_to_all x1, waiting for transfers between devices, per_device(): lax.all_to_all(grad_back, 'expert', split_axis=0, concat_axis=0, tiled=True)  33.7 us
    all_to_all x1, waiting for transfers between devices, per_device(): lax.all_to_all(sent_tokens, 'expert', split_axis=0, concat_axis=0, tiled=...  33.3 us
    all_to_all x1, waiting for transfers between devices, per_device(): lax.all_to_all(sent_grads, 'expert', split_axis=0, concat_axis=0, tiled=T...  31.5 us
    psum x1, waiting for transfers between devices, per_device(): lax.psum(out_part.astype(jnp.bfloat16), 'tensor').astype(jnp.float32)  22.5 us
    all_to_all x1, blocking collectives, per_device(): lax.all_to_all(sent_gate, ('expert', 'tensor'), split_axis=0, concat_axis...  21.7 us
    all_to_all x1, blocking collectives, per_device(): lax.all_to_all(sent_up, ('expert', 'tensor'), split_axis=0, concat_axis=0...  18.5 us
    all_to_all x1, waiting for transfers between devices, per_device(): lax.all_to_all(sent_down, ('expert', 'tensor'), split_axis=0, concat_axis...  13 us
  transfers between devices with their start and end apart: 8, of which 5 were waited for; matrix products, arithmetic and copies ran while one was open for 5% of the time, Pallas kernels for 0%

commit v1 on v0

--- a/solution.py
+++ b/solution.py
@@ -1,7 +1,288 @@
+import functools
+
 import jax
 import jax.numpy as jnp
 from jax import lax
+from jax.experimental import pallas as pl
+from jax.experimental.pallas import tpu as pltpu
 from jax.sharding import PartitionSpec as P
+
+BF16 = jnp.bfloat16
+F32 = jnp.float32
+LAST = (((1,), (1,)), ((), ()))
+FIRST = (((0,), (0,)), ((), ()))
+VMEM_LIMIT = 48 * 1024 * 1024
+
+
+def flips(size, step):
+    return [(i, i ^ step) for i in range(size)]
+
+
+def select_kernel(n_experts, halves, shards, cluster_ref, gate_ref, up_ref, down_ref, *out_refs):
+    mine = lax.axis_index("expert")
+    source = mine * halves + lax.axis_index("tensor")
+    slots = cluster_ref.shape[1]
+    rows = gate_ref.shape[0]
+    half = slots // halves
+    run = half // shards
+    wide = n_experts * halves * run
+    lane = lax.broadcasted_iota(jnp.int32, (8, slots), 1)
+    picks = jnp.full((8, slots), -1, jnp.int32)
+    for k in range(n_experts):
+        row = cluster_ref[pl.ds(mine ^ k, 1), :]
+        row = jnp.broadcast_to(row, (8, slots))
+        for q in range(halves):
+            start = (k * halves + q) * run
+            shift = lax.rem(start + 2 * slots - q * half - source * run, slots)
+            moved = pltpu.roll(row, shift, 1)
+            picks = jnp.where((lane >= start) & (lane < start + run), moved, picks)
+    local = jnp.where(picks >= 0, picks - source * rows, -1)[0:1, :wide]
+    neuron = lax.broadcasted_iota(jnp.int32, (rows, wide), 0)
+    table = jnp.where(neuron == local, 1.0, 0.0).astype(BF16)
+    per = halves * run
+    for w, ref in enumerate((gate_ref, up_ref, down_ref)):
+        chosen = lax.dot_general(table, ref[...], FIRST, preferred_element_type=F32).astype(BF16)
+        for k in range(n_experts):
+            out_refs[k][w * per:(w + 1) * per, :] = chosen[k * per:(k + 1) * per]
+
+
+def slot_table(routes, n_experts, capacity):
+    tokens = routes.shape[1]
+    across = jnp.broadcast_to(routes, (tokens, tokens))
+    down = jnp.transpose(across)
+    i = lax.broadcasted_iota(jnp.int32, (tokens, tokens), 0)
+    j = lax.broadcasted_iota(jnp.int32, (tokens, tokens), 1)
+    before = jnp.where((across == down) & (i < j), 1, 0)
+    position = jnp.sum(before, axis=0, keepdims=True)
+    slot = (routes ^ lax.axis_index("expert")) * capacity + position
+    number = lax.broadcasted_iota(jnp.int32, (n_experts * capacity, tokens), 0)
+    return jnp.where(number == slot, 1.0, 0.0).astype(BF16)
+
+
+def dispatch_kernel(n_experts, capacity, routes_ref, tokens_ref, cotangent_ref, *refs):
+    out_refs, table_ref = refs[:-1], refs[-1]
+
+    @pl.when(pl.program_id(0) == 0)
+    def _():
+        table_ref[...] = slot_table(routes_ref[...], n_experts, capacity)
+
+    def send(source_ref):
+        sent = jnp.dot(table_ref[...], source_ref[...], preferred_element_type=F32).astype(BF16)
+        for k in range(n_experts):
+            out_refs[k][...] = sent[k * capacity:(k + 1) * capacity]
+
+    core = lax.axis_index("tensor")
+    pl.when(core == 0)(lambda: send(tokens_ref))
+    pl.when(core != 0)(lambda: send(cotangent_ref))
+
+
+def merge_kernel(n_experts, capacity, routes_ref, *refs):
+    mine_refs, other_refs = refs[:n_experts], refs[n_experts:2 * n_experts]
+    out_ref, grad_ref, table_ref = refs[2 * n_experts:]
+
+    @pl.when(pl.program_id(0) == 0)
+    def _():
+        table_ref[...] = slot_table(routes_ref[...], n_experts, capacity)
+
+    def home(parts):
+        rows = jnp.concatenate([part[...] for part in parts], axis=0)
+        return lax.dot_general(table_ref[...], rows, FIRST, preferred_element_type=F32).astype(BF16)
+
+    def both(first, second):
+        out_ref[...] = home(first)
+        grad_ref[...] = home(second)
+
+    core = lax.axis_index("tensor")
+    pl.when(core == 0)(lambda: both(mine_refs, other_refs))
+    pl.when(core != 0)(lambda: both(other_refs, mine_refs))
+
+
+def expert_kernel(n_experts, n_dp, members, capacity, *refs):
+    n_parts = n_dp + 1
+    n_rows = len(members)
+    refs = list(refs)
+    weights = [[refs.pop(0) for _ in range(n_parts)] for _ in range(n_experts)]
+    mine_refs = [refs.pop(0) for _ in range(n_rows)]
+    other_refs = [refs.pop(0) for _ in range(n_rows)]
+    keep_refs = [refs.pop(0) for _ in range(n_rows)]
+    give_refs = [refs.pop(0) for _ in range(n_rows)]
+    w_ref, x_ref, dy_ref, w_sem, row_sem = refs
+    me = lax.axis_index("dp")
+    core = lax.axis_index("tensor")
+    deep, width = w_ref.shape[2], w_ref.shape[3]
+    per = deep // 3
+
+    def weight_copies(j):
+        copies = []
+        for k in range(n_experts):
+            if j < n_dp - 1:
+                pairs = [(weights[k][j], w_ref.at[k, j], j)]
+            else:
+                cut = deep // 2
+                pairs = [
+                    (weights[k][j], w_ref.at[k, j, pl.ds(0, cut)], j),
+                    (weights[k][j + 1], w_ref.at[k, j, pl.ds(cut, cut)], j + 1),
+                ]
+            copies += [pltpu.make_async_copy(a, b, w_sem.at[k, s]) for a, b, s in pairs]
+        return copies
+
+    def row_copies(first, second):
+        copies = []
+        for i in range(n_rows):
+            at = pl.ds(i * capacity, capacity)
+            copies.append(pltpu.make_async_copy(first[i], x_ref.at[at], row_sem.at[0, i]))
+            copies.append(pltpu.make_async_copy(second[i], dy_ref.at[at], row_sem.at[1, i]))
+        return copies
+
+    def start(copies):
+        for copy in copies:
+            copy.start()
+
+    pl.when(core == 0)(lambda: start(row_copies(mine_refs, other_refs)))
+    pl.when(core != 0)(lambda: start(row_copies(other_refs, mine_refs)))
+    for j in range(n_dp):
+        start(weight_copies(j))
+    for copy in row_copies(mine_refs, other_refs):
+        copy.wait()
+
+    def columns(j):
+        return pl.ds(pl.multiple_of((me ^ j) * width, width), width)
+
+    def kind(j, w):
+        return jnp.concatenate([w_ref[k, j, w * per:(w + 1) * per, :] for k in range(n_experts)], axis=0)
+
+    pre_gate = pre_up = grad_hidden = 0.0
+    for j in range(n_dp):
+        for copy in weight_copies(j):
+            copy.wait()
+        x = x_ref[:, columns(j)]
+        dy = dy_ref[:, columns(j)]
+        pre_gate += lax.dot_general(x, kind(j, 0), LAST, preferred_element_type=F32)
+        pre_up += lax.dot_general(x, kind(j, 1), LAST, preferred_element_type=F32)
+        grad_hidden += lax.dot_general(dy, kind(j, 2), LAST, preferred_element_type=F32)
+    sig = jax.nn.sigmoid(pre_gate)
+    hidden = (pre_gate * sig * pre_up).astype(BF16)
+    grad_gate = (grad_hidden * pre_up * sig * (1.0 + pre_gate * (1.0 - sig))).astype(BF16)
+    grad_up = (grad_hidden * pre_gate * sig).astype(BF16)
+    for j in range(n_dp):
+        out = jnp.dot(hidden, kind(j, 2), preferred_element_type=F32).astype(BF16)
+        grad = jnp.dot(grad_gate, kind(j, 0), preferred_element_type=F32)
+        grad = (grad + jnp.dot(grad_up, kind(j, 1), preferred_element_type=F32)).astype(BF16)
+
+        def store(kept, given):
+            for i in range(n_rows):
+                at = slice(i * capacity, (i + 1) * capacity)
+                keep_refs[i][:, columns(j)] = kept[at]
+                give_refs[i][:, columns(j)] = given[at]
+
+        pl.when(core == 0)(lambda: store(out, grad))
+        pl.when(core != 0)(lambda: store(grad, out))
+
+
+def aligned_plan(tokens, cotangent, routes, cluster, w_gate, w_up, w_down):
+    n_dp = lax.axis_size("dp")
+    n_experts = lax.axis_size("expert")
+    halves = lax.axis_size("tensor")
+    shards = n_experts * halves
+    width_part = w_gate.shape[1]
+    tok_count, width = tokens.shape
+    run = cluster.shape[1] // (halves * shards)
+    per = halves * run
+    capacity = 3 * tok_count // (2 * n_experts)
+    params = pltpu.CompilerParams(vmem_limit_bytes=VMEM_LIMIT)
+    vmem = pl.BlockSpec(memory_space=pltpu.VMEM)
+    anywhere = pl.BlockSpec(memory_space=pl.ANY)
+    shape = jax.ShapeDtypeStruct
+
+    sent_w = pl.pallas_call(
+        functools.partial(select_kernel, n_experts, halves, shards),
+        out_shape=[shape((3 * per, width_part), BF16)] * n_experts,
+        in_specs=[vmem] * 4,
+        out_specs=[vmem] * n_experts,
+        compiler_params=params,
+        name="select_rows",
+    )(cluster, w_gate, w_up, w_down)
+
+    def over_dp(chunk):
+        cut = chunk.shape[0] // 2
+        near = lax.ppermute(chunk, "dp", flips(n_dp, 1))
+        far = lax.ppermute(chunk, "dp", flips(n_dp, 2))
+        low = lax.ppermute(near[:cut], "dp", flips(n_dp, 2))
+        high = lax.ppermute(far[cut:], "dp", flips(n_dp, 1))
+        return [chunk, near, far, low, high]
+
+    weights = [None] * n_experts
+    weights[0] = over_dp(sent_w[0])
+    for k in (2, 1, 3):
+        weights[k] = over_dp(lax.ppermute(sent_w[k], "expert", flips(n_experts, k)))
+
+    route_row = routes.reshape(1, tok_count)
+    block = width // 4
+    sent = pl.pallas_call(
+        functools.partial(dispatch_kernel, n_experts, capacity),
+        grid=(width // block,),
+        out_shape=[shape((capacity, width), BF16)] * n_experts,
+        in_specs=[
+            pl.BlockSpec((1, tok_count), lambda i: (0, 0)),
+            pl.BlockSpec((tok_count, block), lambda i: (0, i)),
+            pl.BlockSpec((tok_count, block), lambda i: (0, i)),
+        ],
+        out_specs=[pl.BlockSpec((capacity, block), lambda i: (0, i))] * n_experts,
+        scratch_shapes=[pltpu.VMEM((n_experts * capacity, tok_count), BF16)],
+        compiler_params=params,
+        name="dispatch_rows",
+    )(route_row, tokens, cotangent)
+
+    swap = flips(halves, 1)
+    rows = {0: sent[0]}
+    for k in (2, 1, 3):
+        rows[k] = lax.ppermute(sent[k], "expert", flips(n_experts, k))
+    others = {k: lax.ppermute(rows[k], "tensor", swap) for k in (0, 2, 1, 3)}
+
+    mine, other = {}, {}
+    for members in ((2, 0), (3, 1)):
+        count = len(members)
+        results = pl.pallas_call(
+            functools.partial(expert_kernel, n_experts, n_dp, members, capacity),
+            out_shape=[shape((capacity, width), BF16)] * (2 * count),
+            in_specs=[anywhere] * (n_experts * (n_dp + 1) + 2 * count),
+            out_specs=[vmem] * (2 * count),
+            scratch_shapes=[
+                pltpu.VMEM((n_experts, n_dp, 3 * per, width_part), BF16),
+                pltpu.VMEM((count * capacity, width), BF16),
+                pltpu.VMEM((count * capacity, width), BF16),
+                pltpu.SemaphoreType.DMA((n_experts, n_dp + 1)),
+                pltpu.SemaphoreType.DMA((2, count)),
+            ],
+            compiler_params=params,
+            name="expert_math",
+        )(
+            *[part for parts in weights for part in parts],
+            *[rows[k] for k in members],
+            *[others[k] for k in members],
+        )
+        for i, k in enumerate(members):
+            kept, given = results[i], results[count + i]
+            got = lax.ppermute(given, "tensor", swap)
+            total = (kept.astype(F32) + got.astype(F32)).astype(BF16)
+            if k:
+                total = lax.ppermute(total, "expert", flips(n_experts, k))
+            mine[k] = total
+            other[k] = lax.ppermute(total, "tensor", swap)
+
+    return tuple(
+        pl.pallas_call(
+            functools.partial(merge_kernel, n_experts, capacity),
+            grid=(width // block,),
+            out_shape=[shape((tok_count, width), BF16)] * 2,
+            in_specs=[pl.BlockSpec((1, tok_count), lambda i: (0, 0))]
+            + [pl.BlockSpec((capacity, block), lambda i: (0, i))] * (2 * n_experts),
+            out_specs=[pl.BlockSpec((tok_count, block), lambda i: (0, i))] * 2,
+            scratch_shapes=[pltpu.VMEM((n_experts * capacity, tok_count), BF16)],
+            compiler_params=params,
+            name="merge_rows",
+        )(route_row, *[mine[k] for k in range(n_experts)], *[other[k] for k in range(n_experts)])
+    )
 
 
 def expert_math(x_rows, dy_rows, gate_w, up_w, down_w):
@@ -27,7 +308,7 @@
     return merged.astype(jnp.bfloat16)
 
 
-def per_device(tokens, cotangent, routes, cluster, w_gate, w_up, w_down):
+def general_plan(tokens, cotangent, routes, cluster, w_gate, w_up, w_down):
     shards = lax.axis_size(("expert", "tensor"))
     source = lax.axis_index(("expert", "tensor"))
     halves = lax.axis_size("tensor")
@@ -104,6 +385,22 @@
     return (layer_out, grad_out)
 
 
+def per_device(tokens, cotangent, routes, cluster, w_gate, w_up, w_down):
+    n_experts = lax.axis_size("expert")
+    halves = lax.axis_size("tensor")
+    per = cluster.shape[1] // (halves * n_experts)
+    capacity = 3 * tokens.shape[0] // (2 * n_experts)
+    aligned = (
+        per // halves % 16 == 0
+        and capacity % 16 == 0
+        and n_experts == 4
+        and halves == 2
+        and lax.axis_size("dp") == 4
+    )
+    plan = aligned_plan if aligned else general_plan
+    return plan(tokens, cotangent, routes, cluster, w_gate, w_up, w_down)
+
+
 def solution(mesh):
     in_specs = (
         P(("dp", "expert"), None),

time: 279 us -> 177 us (0.63)
  the two profiles are of different devices: /device:TPU:0 before, /device:TPU:9 now
where the time goes in v1:
time: 177 us
  waiting for transfers between devices  95.2 us (54%)
  starting transfers between devices  50.3 us (28%)
  Pallas kernels  22.8 us (13%)
  local copies, waits for them, and re-layouts  7.22 us (4%)
    ppermute x3, waiting for transfers between devices, aligned_plan(): weights[k] = over_dp(lax.ppermute(sent_w[k], 'expert', flips(n_experts, k)))  40.2 us
    ppermute x3, waiting for transfers between devices, aligned_plan(): total = lax.ppermute(total, 'expert', flips(n_experts, k))  21.4 us
    pallas_call x2, Pallas kernels, aligned_plan(): pl.pallas_call(functools.partial(expert_kernel, n_experts, n_dp, members,...  17.5 us
    ppermute x3, waiting for transfers between devices, aligned_plan(): rows[k] = lax.ppermute(sent[k], 'expert', flips(n_experts, k))  16.4 us
    ppermute x4, starting transfers between devices, aligned_plan(): others = {k: lax.ppermute(rows[k], 'tensor', swap) for k in (0, 2, 1, 3)}  15 us
    ppermute x4, starting transfers between devices, aligned_plan(): other[k] = lax.ppermute(total, 'tensor', swap)  13.4 us
    ppermute x4, waiting for transfers between devices, over_dp(): far = lax.ppermute(chunk, 'dp', flips(n_dp, 2))  7.74 us
    unnamed x40, local copies, waits for them, and re-layouts  7.11 us
  transfers between devices with their start and end apart: 37, of which 16 were waited for; matrix products, arithmetic and copies ran while one was open for 0% of the time, Pallas kernels for 11%

profile of v1, /device:TPU:9, one launch (start us, length us, event | category | flops | bytes accessed | tf_op | source)
XLA Modules:
  0.0 176.8 jit_solution(12065506362193122009)
XLA Ops:
  0.7 1.1 copy-done.2
  1.8 1.0 copy-done.3
  2.8 1.0 copy-done.4
  3.8 0.7 copy-done.6
  4.5 0.7 select_rows.1
  5.2 1.3 collective-permute-start
  6.5 1.2 collective-permute-start.1
  7.9 2.3 %collective-permute-start.9 = (bf16[192,1024]{1,0:T(8,128)(2,1)S(1)}, bf16[192,1024]{1,0:T(8,128)(2,1)S(1)}, u32[]{:S(2)}, u32[]{:S(2)}) collective-permute-start(bf16[192,1024]{1,0:T(8,128)(2,1)S(1)} %get-tuple-element.20), channel_id=1, source_target_pairs={{0,4},{2,6},{4,0},{6,2},{1,5},{3,7},{5,1},{7,3},{8,12},{10,14},{12... | collective-permute-start | bytes 1179656 | tf_op jit(solution)/shard_map/ppermute | solution.py:217
  10.9 1.2 copy-done.1
  12.1 1.5 dispatch_rows.1
  13.6 1.6 collective-permute-done.refs_1_
  15.2 2.3 %collective-permute-start.19 = (bf16[48,4096]{1,0:T(8,128)(2,1)S(1)}, bf16[48,4096]{1,0:T(8,128)(2,1)S(1)}, u32[]{:S(2)}, u32[]{:S(2)}) collective-permute-start(bf16[48,4096]{1,0:T(8,128)(2,1)S(1)} %get-tuple-element.22), channel_id=1, source_target_pairs={{0,4},{2,6},{4,0},{6,2},{1,5},{3,7},{5,1},{7,3},{8,12},{10,14},{12... | collective-permute-start | bytes 1179656 | tf_op jit(solution)/shard_map/ppermute | solution.py:239
  17.6 4.9 %collective-permute-done.4.refs_5_ = bf16[192,1024]{1,0:T(8,128)(2,1)S(1)} collective-permute-done((bf16[192,1024]{1,0:T(8,128)(2,1)S(1)}, bf16[192,1024]{1,0:T(8,128)(2,1)S(1)}, u32[]{:S(2)}, u32[]{:S(2)}) %collective-permute-start.4) | collective-permute-done | bytes 393248 | tf_op jit(solution)/shard_map/ppermute | solution.py:217
  22.4 2.2 %collective-permute-start.24 = (bf16[48,4096]{1,0:T(8,128)(2,1)S(1)}, bf16[48,4096]{1,0:T(8,128)(2,1)S(1)}, u32[]{:S(2)}, u32[]{:S(2)}) collective-permute-start(bf16[48,4096]{1,0:T(8,128)(2,1)S(1)} %get-tuple-element.27), channel_id=1, source_target_pairs={{0,2},{2,0},{4,6},{6,4},{1,3},{3,1},{5,7},{7,5},{8,10},{10,8},{12,... | collective-permute-start | bytes 1179656 | tf_op jit(solution)/shard_map/ppermute | solution.py:239
  24.6 1.9 %collective-permute-done.9.refs_10_ = bf16[192,1024]{1,0:T(8,128)(2,1)S(1)} collective-permute-done((bf16[192,1024]{1,0:T(8,128)(2,1)S(1)}, bf16[192,1024]{1,0:T(8,128)(2,1)S(1)}, u32[]{:S(2)}, u32[]{:S(2)}) %collective-permute-start.9) | collective-permute-done | bytes 393248 | tf_op jit(solution)/shard_map/ppermute | solution.py:217
  26.8 33.4 %collective-permute-done.14.refs_15_ = bf16[192,1024]{1,0:T(8,128)(2,1)S(1)} collective-permute-done((bf16[192,1024]{1,0:T(8,128)(2,1)S(1)}, bf16[192,1024]{1,0:T(8,128)(2,1)S(1)}, u32[]{:S(2)}, u32[]{:S(2)}) %collective-permute-start.14) | collective-permute-done | bytes 393248 | tf_op jit(solution)/shard_map/ppermute | solution.py:217
  60.5 7.3 %collective-permute-done.19.refs_20_ = bf16[48,4096]{1,0:T(8,128)(2,1)S(1)} collective-permute-done((bf16[48,4096]{1,0:T(8,128)(2,1)S(1)}, bf16[48,4096]{1,0:T(8,128)(2,1)S(1)}, u32[]{:S(2)}, u32[]{:S(2)}) %collective-permute-start.19) | collective-permute-done | bytes 393248 | tf_op jit(solution)/shard_map/ppermute | solution.py:239
  68.0 9.1 %collective-permute-done.23.refs_20_ = bf16[48,4096]{1,0:T(8,128)(2,1)S(1)} collective-permute-done((bf16[48,4096]{1,0:T(8,128)(2,1)S(1)}, bf16[48,4096]{1,0:T(8,128)(2,1)S(1)}, u32[]{:S(2)}, u32[]{:S(2)}) %collective-permute-start.23) | collective-permute-done | bytes 393248 | tf_op jit(solution)/shard_map/ppermute | solution.py:239
  77.3 1.2 collective-permute-start.11
  78.6 3.0 %collective-permute-done.2.refs_3_ = bf16[96,1024]{1,0:T(8,128)(2,1)S(1)} collective-permute-done((bf16[96,1024]{1,0:T(8,128)(2,1)S(1)}, bf16[96,1024]{1,0:T(8,128)(2,1)S(1)}, u32[]{:S(2)}, u32[]{:S(2)}) %collective-permute-start.2) | collective-permute-done | bytes 196640 | tf_op jit(solution)/shard_map/ppermute | solution.py:210
  82.1 6.3 %collective-permute-start.25 = (bf16[48,4096]{1,0:T(8,128)(2,1)S(1)}, bf16[48,4096]{1,0:T(8,128)(2,1)S(1)}, u32[]{:S(2)}, u32[]{:S(2)}) collective-permute-start(bf16[48,4096]{1,0:T(8,128)(2,1)S(1)} %collective-permute-done.23.refs_20_), channel_id=1, source_target_pairs={{0,1},{1,0},{2,3},{3,2},{4,5},{5,4},{6,7},{7,6},{8,9},{9,8},{10,11... | collective-permute-start | bytes 1179656 | tf_op jit(solution)/shard_map/ppermute | solution.py:240
  88.5 1.0 collective-permute-done.11.refs_12_
  89.8 1.3 collective-permute-start.7
  91.3 6.7 %collective-permute-done.16.refs_17_ = bf16[192,1024]{1,0:T(8,128)(2,1)S(1)} collective-permute-done((bf16[192,1024]{1,0:T(8,128)(2,1)S(1)}, bf16[192,1024]{1,0:T(8,128)(2,1)S(1)}, u32[]{:S(2)}, u32[]{:S(2)}) %collective-permute-start.16) | collective-permute-done | bytes 393248 | tf_op jit(solution)/shard_map/ppermute | solution.py:209
  98.5 1.2 collective-permute-start.13
  99.8 1.2 collective-permute-start.17
  101.0 1.2 collective-permute-done.7.refs_8_
  102.4 0.7 collective-permute-done.8.refs_9_
  103.2 6.7 %collective-permute-start.21 = (bf16[48,4096]{1,0:T(8,128)(2,1)S(1)}, bf16[48,4096]{1,0:T(8,128)(2,1)S(1)}, u32[]{:S(2)}, u32[]{:S(2)}) collective-permute-start(bf16[48,4096]{1,0:T(8,128)(2,1)S(1)} %get-tuple-element.23.refs_21_), channel_id=1, source_target_pairs={{0,1},{1,0},{2,3},{3,2},{4,5},{5,4},{6,7},{7,6},{8,9},{9,8},{10,11... | collective-permute-start | bytes 1179656 | tf_op jit(solution)/shard_map/ppermute | solution.py:240
  109.9 1.9 %collective-permute-start.20 = (bf16[48,4096]{1,0:T(8,128)(2,1)S(1)}, bf16[48,4096]{1,0:T(8,128)(2,1)S(1)}, u32[]{:S(2)}, u32[]{:S(2)}) collective-permute-start(bf16[48,4096]{1,0:T(8,128)(2,1)S(1)} %collective-permute-done.19.refs_20_), channel_id=1, source_target_pairs={{0,1},{1,0},{2,3},{3,2},{4,5},{5,4},{6,7},{7,6},{8,9},{9,8},{10,11... | collective-permute-start | bytes 1179656 | tf_op jit(solution)/shard_map/ppermute | solution.py:240
  111.9 8.8 %expert_math.3 = (bf16[48,4096]{1,0:T(8,128)(2,1)S(1)}, bf16[48,4096]{1,0:T(8,128)(2,1)S(1)}, bf16[48,4096]{1,0:T(8,128)(2,1)S(1)}, bf16[48,4096]{1,0:T(8,128)(2,1)S(1)}) custom-call(bf16[192,1024]{1,0:T(8,128)(2,1)S(1)} %get-tuple-element.18.refs_0_, bf16[192,1024]{1,0:T(8,128)(2,1)S(1)} %collective-permute-done.refs_1_, ...), custom_call_target="tpu_custom_call" | custom-call | tf_op jit(solution)/shard_map/expert_math/pallas_call | solution.py:245
  120.7 2.3 %collective-permute-start.27 = (bf16[48,4096]{1,0:T(8,128)(2,1)S(1)}, bf16[48,4096]{1,0:T(8,128)(2,1)S(1)}, u32[]{:S(2)}, u32[]{:S(2)}) collective-permute-start(bf16[48,4096]{1,0:T(8,128)(2,1)S(1)} %get-tuple-element.29), channel_id=1, source_target_pairs={{0,1},{1,0},{2,3},{3,2},{4,5},{5,4},{6,7},{7,6},{8,9},{9,8},{10,11... | collective-permute-start | bytes 1179656 | tf_op jit(solution)/shard_map/ppermute | solution.py:266
  122.9 0.7 copy-done.18
  123.7 0.8 copy-done.19
  124.5 8.8 %expert_math.2 = (bf16[48,4096]{1,0:T(8,128)(2,1)S(1)}, bf16[48,4096]{1,0:T(8,128)(2,1)S(1)}, bf16[48,4096]{1,0:T(8,128)(2,1)S(1)}, bf16[48,4096]{1,0:T(8,128)(2,1)S(1)}) custom-call(bf16[192,1024]{1,0:T(8,128)(2,1)S(1)} %get-tuple-element.18.refs_0_, bf16[192,1024]{1,0:T(8,128)(2,1)S(1)} %collective-permute-done.refs_1_, ...), custom_call_target="tpu_custom_call" | custom-call | tf_op jit(solution)/shard_map/expert_math/pallas_call | solution.py:245
  133.3 0.5 collective-permute-start.29
  134.1 1.5 collective-permute-done.29
  135.7 1.0 collective-permute-start.30
  136.8 0.8 collective-permute-start.32
  137.7 0.8 collective-permute-start.33
  138.5 11.7 %collective-permute-done.28.refs_1_ = bf16[48,4096]{1,0:T(8,128)(2,1)S(1)} collective-permute-done((bf16[48,4096]{1,0:T(8,128)(2,1)S(1)}, bf16[48,4096]{1,0:T(8,128)(2,1)S(1)}, u32[]{:S(2)}, u32[]{:S(2)}) %collective-permute-start.28) | collective-permute-done | bytes 393248 | tf_op jit(solution)/shard_map/ppermute | solution.py:269
  150.1 1.0 collective-permute-start.34
  151.1 2.7 %collective-permute-done.30.refs_2_ = bf16[48,4096]{1,0:T(8,128)(2,1)S(1)} collective-permute-done((bf16[48,4096]{1,0:T(8,128)(2,1)S(1)}, bf16[48,4096]{1,0:T(8,128)(2,1)S(1)}, u32[]{:S(2)}, u32[]{:S(2)}) %collective-permute-start.30) | collective-permute-done | bytes 393248 | tf_op jit(solution)/shard_map/ppermute | solution.py:269
  153.8 10.3 %collective-permute-start.35 = (bf16[48,4096]{1,0:T(8,128)(2,1)S(1)}, bf16[48,4096]{1,0:T(8,128)(2,1)S(1)}, u32[]{:S(2)}, u32[]{:S(2)}) collective-permute-start(bf16[48,4096]{1,0:T(8,128)(2,1)S(1)} %collective-permute-done.30.refs_2_), channel_id=1, source_target_pairs={{0,1},{1,0},{2,3},{3,2},{4,5},{5,4},{6,7},{7,6},{8,9},{9,8},{10,11... | collective-permute-start | bytes 1179656 | tf_op jit(solution)/shard_map/ppermute | solution.py:271
  164.1 7.0 %collective-permute-done.32.refs_3_ = bf16[48,4096]{1,0:T(8,128)(2,1)S(1)} collective-permute-done((bf16[48,4096]{1,0:T(8,128)(2,1)S(1)}, bf16[48,4096]{1,0:T(8,128)(2,1)S(1)}, u32[]{:S(2)}, u32[]{:S(2)}) %collective-permute-start.32) | collective-permute-done | bytes 393248 | tf_op jit(solution)/shard_map/ppermute | solution.py:269
  171.1 1.4 collective-permute-start.36
  172.4 1.3 collective-permute-done.36.refs_7_
  173.8 3.0 %merge_rows.1 = (bf16[128,4096]{1,0:T(8,128)(2,1)}, bf16[128,4096]{1,0:T(8,128)(2,1)}) custom-call(s32[1,128]{1,0:T(1,128)S(1)} %bitcast.2, bf16[48,4096]{1,0:T(8,128)(2,1)S(1)} %add_convert_fusion.3.refs_0_, bf16[48,4096]{1,0:T(8,128)(2,1)S(1)} %collective-permute-done.28.refs_1_, bf16[48,4096]{1,0:T(8,128)(2,1)S(1)} %collective-permute-done.30.refs_2_, ...), custom_call_target="tpu_custom_call" | custom-call | tf_op jit(solution)/shard_map/merge_rows/pallas_call | solution.py:274
  (83 shorter events, 4.2 us)
Async XLA Ops:
  0.6 9.7 %copy-start = (bf16[128,4096]{1,0:T(8,128)(2,1)S(1)}, bf16[128,4096]{1,0:T(8,128)(2,1)}, u32[]{:S(2)}) copy-start(bf16[128,4096]{1,0:T(8,128)(2,1)} %tokens_ref.1) | copy-start | bytes 3145732
  5.2 10.0 %collective-permute-start = (bf16[192,1024]{1,0:T(8,128)(2,1)S(1)}, bf16[192,1024]{1,0:T(8,128)(2,1)S(1)}, u32[]{:S(2)}, u32[]{:S(2)}) collective-permute-start(bf16[192,1024]{1,0:T(8,128)(2,1)S(1)} %get-tuple-element.18.refs_0_), channel_id=1, source_target_pairs={{0,8},{8,0},{16,24},{24,16},{1,9},{9,1},{17,25},{25,17},{2,10},{10... | collective-permute-start | bytes 1179656 | tf_op jit(solution)/shard_map/ppermute | solution.py:208
  6.5 11.1 %collective-permute-start.1 = (bf16[192,1024]{1,0:T(8,128)(2,1)S(1)}, bf16[192,1024]{1,0:T(8,128)(2,1)S(1)}, u32[]{:S(2)}, u32[]{:S(2)}) collective-permute-start(bf16[192,1024]{1,0:T(8,128)(2,1)S(1)} %get-tuple-element.18.refs_0_), channel_id=1, source_target_pairs={{0,16},{8,24},{16,0},{24,8},{1,17},{9,25},{17,1},{25,9},{2,18},{10... | collective-permute-start | bytes 1179656 | tf_op jit(solution)/shard_map/ppermute | solution.py:209
  7.7 14.7 %collective-permute-start.4 = (bf16[192,1024]{1,0:T(8,128)(2,1)S(1)}, bf16[192,1024]{1,0:T(8,128)(2,1)S(1)}, u32[]{:S(2)}, u32[]{:S(2)}) collective-permute-start(bf16[192,1024]{1,0:T(8,128)(2,1)S(1)} %get-tuple-element.19), channel_id=1, source_target_pairs={{0,2},{2,0},{4,6},{6,4},{1,3},{3,1},{5,7},{7,5},{8,10},{10,8},{12,... | collective-permute-start | bytes 1179656 | tf_op jit(solution)/shard_map/ppermute | solution.py:217
  7.9 18.7 %collective-permute-start.9 = (bf16[192,1024]{1,0:T(8,128)(2,1)S(1)}, bf16[192,1024]{1,0:T(8,128)(2,1)S(1)}, u32[]{:S(2)}, u32[]{:S(2)}) collective-permute-start(bf16[192,1024]{1,0:T(8,128)(2,1)S(1)} %get-tuple-element.20), channel_id=1, source_target_pairs={{0,4},{2,6},{4,0},{6,2},{1,5},{3,7},{5,1},{7,3},{8,12},{10,14},{12... | collective-permute-start | bytes 1179656 | tf_op jit(solution)/shard_map/ppermute | solution.py:217
  10.2 50.1 %collective-permute-start.14 = (bf16[192,1024]{1,0:T(8,128)(2,1)S(1)}, bf16[192,1024]{1,0:T(8,128)(2,1)S(1)}, u32[]{:S(2)}, u32[]{:S(2)}) collective-permute-start(bf16[192,1024]{1,0:T(8,128)(2,1)S(1)} %get-tuple-element.21), channel_id=1, source_target_pairs={{0,6},{2,4},{4,2},{6,0},{1,7},{3,5},{5,3},{7,1},{8,14},{10,12},{12... | collective-permute-start | bytes 1179656 | tf_op jit(solution)/shard_map/ppermute | solution.py:217
  13.6 89.6 %copy-start.5 = (bf16[48,4096]{1,0:T(8,128)(2,1)}, bf16[48,4096]{1,0:T(8,128)(2,1)S(1)}, u32[]{:S(2)}) copy-start(bf16[48,4096]{1,0:T(8,128)(2,1)S(1)} %get-tuple-element.23.refs_21_) | copy-start | bytes 1179652
  15.2 52.5 %collective-permute-start.19 = (bf16[48,4096]{1,0:T(8,128)(2,1)S(1)}, bf16[48,4096]{1,0:T(8,128)(2,1)S(1)}, u32[]{:S(2)}, u32[]{:S(2)}) collective-permute-start(bf16[48,4096]{1,0:T(8,128)(2,1)S(1)} %get-tuple-element.22), channel_id=1, source_target_pairs={{0,4},{2,6},{4,0},{6,2},{1,5},{3,7},{5,1},{7,3},{8,12},{10,14},{12... | collective-permute-start | bytes 1179656 | tf_op jit(solution)/shard_map/ppermute | solution.py:239
  17.6 59.6 %collective-permute-start.23 = (bf16[48,4096]{1,0:T(8,128)(2,1)S(1)}, bf16[48,4096]{1,0:T(8,128)(2,1)S(1)}, u32[]{:S(2)}, u32[]{:S(2)}) collective-permute-start(bf16[48,4096]{1,0:T(8,128)(2,1)S(1)} %get-tuple-element.26), channel_id=1, source_target_pairs={{0,6},{2,4},{4,2},{6,0},{1,7},{3,5},{5,3},{7,1},{8,14},{10,12},{12... | collective-permute-start | bytes 1179656 | tf_op jit(solution)/shard_map/ppermute | solution.py:239
  22.4 54.9 %collective-permute-start.24 = (bf16[48,4096]{1,0:T(8,128)(2,1)S(1)}, bf16[48,4096]{1,0:T(8,128)(2,1)S(1)}, u32[]{:S(2)}, u32[]{:S(2)}) collective-permute-start(bf16[48,4096]{1,0:T(8,128)(2,1)S(1)} %get-tuple-element.27), channel_id=1, source_target_pairs={{0,2},{2,0},{4,6},{6,4},{1,3},{3,1},{5,7},{7,5},{8,10},{10,8},{12,... | collective-permute-start | bytes 1179656 | tf_op jit(solution)/shard_map/ppermute | solution.py:239
  26.6 55.3 %collective-permute-start.5 = (bf16[192,1024]{1,0:T(8,128)(2,1)S(1)}, bf16[192,1024]{1,0:T(8,128)(2,1)S(1)}, u32[]{:S(2)}, u32[]{:S(2)}) collective-permute-start(bf16[192,1024]{1,0:T(8,128)(2,1)S(1)} %collective-permute-done.4.refs_5_), channel_id=1, source_target_pairs={{0,8},{8,0},{16,24},{24,16},{1,9},{9,1},{17,25},{25,17},{2,10},{10... | collective-permute-start | bytes 1179656 | tf_op jit(solution)/shard_map/ppermute | solution.py:208
  60.3 29.6 %copy-start.12 = (bf16[192,1024]{1,0:T(8,128)(2,1)}, bf16[192,1024]{1,0:T(8,128)(2,1)S(1)}, u32[]{:S(2)}) copy-start(bf16[192,1024]{1,0:T(8,128)(2,1)S(1)} %collective-permute-done.14.refs_15_) | copy-start | bytes 1179652
  60.3 21.9 %collective-permute-start.6 = (bf16[192,1024]{1,0:T(8,128)(2,1)S(1)}, bf16[192,1024]{1,0:T(8,128)(2,1)S(1)}, u32[]{:S(2)}, u32[]{:S(2)}) collective-permute-start(bf16[192,1024]{1,0:T(8,128)(2,1)S(1)} %collective-permute-done.4.refs_5_), channel_id=1, source_target_pairs={{0,16},{8,24},{16,0},{24,8},{1,17},{9,25},{17,1},{25,9},{2,18},{10... | collective-permute-start | bytes 1179656 | tf_op jit(solution)/shard_map/ppermute | solution.py:209
  67.8 42.1 %copy-start.13 = (bf16[48,4096]{1,0:T(8,128)(2,1)}, bf16[48,4096]{1,0:T(8,128)(2,1)S(1)}, u32[]{:S(2)}) copy-start(bf16[48,4096]{1,0:T(8,128)(2,1)S(1)} %collective-permute-done.19.refs_20_) | copy-start | bytes 1179652
  67.8 20.6 %collective-permute-start.10 = (bf16[192,1024]{1,0:T(8,128)(2,1)S(1)}, bf16[192,1024]{1,0:T(8,128)(2,1)S(1)}, u32[]{:S(2)}, u32[]{:S(2)}) collective-permute-start(bf16[192,1024]{1,0:T(8,128)(2,1)S(1)} %collective-permute-done.9.refs_10_), channel_id=1, source_target_pairs={{0,8},{8,0},{16,24},{24,16},{1,9},{9,1},{17,25},{25,17},{2,10},{10... | collective-permute-start | bytes 1179656 | tf_op jit(solution)/shard_map/ppermute | solution.py:208
  77.1 14.2 %copy-start.14 = (bf16[48,4096]{1,0:T(8,128)(2,1)}, bf16[48,4096]{1,0:T(8,128)(2,1)S(1)}, u32[]{:S(2)}) copy-start(bf16[48,4096]{1,0:T(8,128)(2,1)S(1)} %collective-permute-done.23.refs_20_) | copy-start | bytes 1179652
  77.1 4.5 %collective-permute-start.2 = (bf16[96,1024]{1,0:T(8,128)(2,1)S(1)}, bf16[96,1024]{1,0:T(8,128)(2,1)S(1)}, u32[]{:S(2)}, u32[]{:S(2)}) collective-permute-start(bf16[96,1024]{1,0:T(8,128)(2,1)S(1)} %slice.32), channel_id=1, source_target_pairs={{0,16},{8,24},{16,0},{24,8},{1,17},{9,25},{17,1},{25,9},{2,18},{10... | collective-permute-start | bytes 589832 | tf_op jit(solution)/shard_map/ppermute | solution.py:210
  77.3 13.9 %copy-start.15 = (bf16[48,4096]{1,0:T(8,128)(2,1)}, bf16[48,4096]{1,0:T(8,128)(2,1)S(1)}, u32[]{:S(2)}) copy-start(bf16[48,4096]{1,0:T(8,128)(2,1)S(1)} %collective-permute-done.24.refs_21_) | copy-start | bytes 1179652
  77.3 12.2 %collective-permute-start.11 = (bf16[192,1024]{1,0:T(8,128)(2,1)S(1)}, bf16[192,1024]{1,0:T(8,128)(2,1)S(1)}, u32[]{:S(2)}, u32[]{:S(2)}) collective-permute-start(bf16[192,1024]{1,0:T(8,128)(2,1)S(1)} %collective-permute-done.9.refs_10_), channel_id=1, source_target_pairs={{0,16},{8,24},{16,0},{24,8},{1,17},{9,25},{17,1},{25,9},{2,18},{10... | collective-permute-start | bytes 1179656 | tf_op jit(solution)/shard_map/ppermute | solution.py:209
  81.6 8.2 %collective-permute-start.15 = (bf16[192,1024]{1,0:T(8,128)(2,1)S(1)}, bf16[192,1024]{1,0:T(8,128)(2,1)S(1)}, u32[]{:S(2)}, u32[]{:S(2)}) collective-permute-start(bf16[192,1024]{1,0:T(8,128)(2,1)S(1)} %collective-permute-done.14.refs_15_), channel_id=1, source_target_pairs={{0,8},{8,0},{16,24},{24,16},{1,9},{9,1},{17,25},{25,17},{2,10},{10... | collective-permute-start | bytes 1179656 | tf_op jit(solution)/shard_map/ppermute | solution.py:208
  81.9 16.1 %collective-permute-start.16 = (bf16[192,1024]{1,0:T(8,128)(2,1)S(1)}, bf16[192,1024]{1,0:T(8,128)(2,1)S(1)}, u32[]{:S(2)}, u32[]{:S(2)}) collective-permute-start(bf16[192,1024]{1,0:T(8,128)(2,1)S(1)} %collective-permute-done.14.refs_15_), channel_id=1, source_target_pairs={{0,16},{8,24},{16,0},{24,8},{1,17},{9,25},{17,1},{25,9},{2,18},{10... | collective-permute-start | bytes 1179656 | tf_op jit(solution)/shard_map/ppermute | solution.py:209
  82.1 16.4 %collective-permute-start.25 = (bf16[48,4096]{1,0:T(8,128)(2,1)S(1)}, bf16[48,4096]{1,0:T(8,128)(2,1)S(1)}, u32[]{:S(2)}, u32[]{:S(2)}) collective-permute-start(bf16[48,4096]{1,0:T(8,128)(2,1)S(1)} %collective-permute-done.23.refs_20_), channel_id=1, source_target_pairs={{0,1},{1,0},{2,3},{3,2},{4,5},{5,4},{6,7},{7,6},{8,9},{9,8},{10,11... | collective-permute-start | bytes 1179656 | tf_op jit(solution)/shard_map/ppermute | solution.py:240
  88.4 2.8 %copy-start.8 = (bf16[192,1024]{1,0:T(8,128)(2,1)}, bf16[192,1024]{1,0:T(8,128)(2,1)S(1)}, u32[]{:S(2)}) copy-start(bf16[192,1024]{1,0:T(8,128)(2,1)S(1)} %collective-permute-done.10.refs_11_) | copy-start | bytes 1179652
  88.4 11.4 %collective-permute-start.26 = (bf16[48,4096]{1,0:T(8,128)(2,1)S(1)}, bf16[48,4096]{1,0:T(8,128)(2,1)S(1)}, u32[]{:S(2)}, u32[]{:S(2)}) collective-permute-start(bf16[48,4096]{1,0:T(8,128)(2,1)S(1)} %collective-permute-done.24.refs_21_), channel_id=1, source_target_pairs={{0,1},{1,0},{2,3},{3,2},{4,5},{5,4},{6,7},{7,6},{8,9},{9,8},{10,11... | collective-permute-start | bytes 1179656 | tf_op jit(solution)/shard_map/ppermute | solution.py:240
  89.5 1.7 copy-start.9
  89.5 8.7 %collective-permute-start.3 = (bf16[96,1024]{1,0:T(8,128)(2,1)S(1)}, bf16[96,1024]{1,0:T(8,128)(2,1)S(1)}, u32[]{:S(2)}, u32[]{:S(2)}) collective-permute-start(bf16[96,1024]{1,0:T(8,128)(2,1)S(1)} %slice.33), channel_id=1, source_target_pairs={{0,8},{8,0},{16,24},{24,16},{1,9},{9,1},{17,25},{25,17},{2,10},{10... | collective-permute-start | bytes 589832 | tf_op jit(solution)/shard_map/ppermute | solution.py:211
  89.8 12.3 %collective-permute-start.7 = (bf16[96,1024]{1,0:T(8,128)(2,1)S(1)}, bf16[96,1024]{1,0:T(8,128)(2,1)S(1)}, u32[]{:S(2)}, u32[]{:S(2)}) collective-permute-start(bf16[96,1024]{1,0:T(8,128)(2,1)S(1)} %slice.34), channel_id=1, source_target_pairs={{0,16},{8,24},{16,0},{24,8},{1,17},{9,25},{17,1},{25,9},{2,18},{10... | collective-permute-start | bytes 589832 | tf_op jit(solution)/shard_map/ppermute | solution.py:210
  98.0 13.9 %copy-start.11 = (bf16[192,1024]{1,0:T(8,128)(2,1)}, bf16[192,1024]{1,0:T(8,128)(2,1)S(1)}, u32[]{:S(2)}) copy-start(bf16[192,1024]{1,0:T(8,128)(2,1)S(1)} %collective-permute-done.16.refs_17_) | copy-start | bytes 1179652
  98.0 5.2 %collective-permute-start.8 = (bf16[96,1024]{1,0:T(8,128)(2,1)S(1)}, bf16[96,1024]{1,0:T(8,128)(2,1)S(1)}, u32[]{:S(2)}, u32[]{:S(2)}) collective-permute-start(bf16[96,1024]{1,0:T(8,128)(2,1)S(1)} %slice.35), channel_id=1, source_target_pairs={{0,8},{8,0},{16,24},{24,16},{1,9},{9,1},{17,25},{25,17},{2,10},{10... | collective-permute-start | bytes 589832 | tf_op jit(solution)/shard_map/ppermute | solution.py:211
  98.3 11.6 %collective-permute-start.12 = (bf16[96,1024]{1,0:T(8,128)(2,1)S(1)}, bf16[96,1024]{1,0:T(8,128)(2,1)S(1)}, u32[]{:S(2)}, u32[]{:S(2)}) collective-permute-start(bf16[96,1024]{1,0:T(8,128)(2,1)S(1)} %slice.36), channel_id=1, source_target_pairs={{0,16},{8,24},{16,0},{24,8},{1,17},{9,25},{17,1},{25,9},{2,18},{10... | collective-permute-start | bytes 589832 | tf_op jit(solution)/shard_map/ppermute | solution.py:210
  98.5 13.3 %copy-start.16 = (bf16[48,4096]{1,0:T(8,128)(2,1)}, bf16[48,4096]{1,0:T(8,128)(2,1)S(1)}, u32[]{:S(2)}) copy-start(bf16[48,4096]{1,0:T(8,128)(2,1)S(1)} %collective-permute-done.25.refs_22_) | copy-start | bytes 1179652
  98.5 13.3 %collective-permute-start.13 = (bf16[96,1024]{1,0:T(8,128)(2,1)S(1)}, bf16[96,1024]{1,0:T(8,128)(2,1)S(1)}, u32[]{:S(2)}, u32[]{:S(2)}) collective-permute-start(bf16[96,1024]{1,0:T(8,128)(2,1)S(1)} %slice.37), channel_id=1, source_target_pairs={{0,8},{8,0},{16,24},{24,16},{1,9},{9,1},{17,25},{25,17},{2,10},{10... | collective-permute-start | bytes 589832 | tf_op jit(solution)/shard_map/ppermute | solution.py:211
  99.8 12.1 %copy-start.17 = (bf16[48,4096]{1,0:T(8,128)(2,1)}, bf16[48,4096]{1,0:T(8,128)(2,1)S(1)}, u32[]{:S(2)}) copy-start(bf16[48,4096]{1,0:T(8,128)(2,1)S(1)} %collective-permute-done.26.refs_23_) | copy-start | bytes 1179652
  99.8 12.1 %collective-permute-start.17 = (bf16[96,1024]{1,0:T(8,128)(2,1)S(1)}, bf16[96,1024]{1,0:T(8,128)(2,1)S(1)}, u32[]{:S(2)}, u32[]{:S(2)}) collective-permute-start(bf16[96,1024]{1,0:T(8,128)(2,1)S(1)} %slice.38), channel_id=1, source_target_pairs={{0,16},{8,24},{16,0},{24,8},{1,17},{9,25},{17,1},{25,9},{2,18},{10... | collective-permute-start | bytes 589832 | tf_op jit(solution)/shard_map/ppermute | solution.py:210
  102.2 9.6 %collective-permute-start.18 = (bf16[96,1024]{1,0:T(8,128)(2,1)S(1)}, bf16[96,1024]{1,0:T(8,128)(2,1)S(1)}, u32[]{:S(2)}, u32[]{:S(2)}) collective-permute-start(bf16[96,1024]{1,0:T(8,128)(2,1)S(1)} %slice.39), channel_id=1, source_target_pairs={{0,8},{8,0},{16,24},{24,16},{1,9},{9,1},{17,25},{25,17},{2,10},{10... | collective-permute-start | bytes 589832 | tf_op jit(solution)/shard_map/ppermute | solution.py:211
  103.2 19.8 %collective-permute-start.21 = (bf16[48,4096]{1,0:T(8,128)(2,1)S(1)}, bf16[48,4096]{1,0:T(8,128)(2,1)S(1)}, u32[]{:S(2)}, u32[]{:S(2)}) collective-permute-start(bf16[48,4096]{1,0:T(8,128)(2,1)S(1)} %get-tuple-element.23.refs_21_), channel_id=1, source_target_pairs={{0,1},{1,0},{2,3},{3,2},{4,5},{5,4},{6,7},{7,6},{8,9},{9,8},{10,11... | collective-permute-start | bytes 1179656 | tf_op jit(solution)/shard_map/ppermute | solution.py:240
  109.9 13.1 %collective-permute-start.20 = (bf16[48,4096]{1,0:T(8,128)(2,1)S(1)}, bf16[48,4096]{1,0:T(8,128)(2,1)S(1)}, u32[]{:S(2)}, u32[]{:S(2)}) collective-permute-start(bf16[48,4096]{1,0:T(8,128)(2,1)S(1)} %collective-permute-done.19.refs_20_), channel_id=1, source_target_pairs={{0,1},{1,0},{2,3},{3,2},{4,5},{5,4},{6,7},{7,6},{8,9},{9,8},{10,11... | collective-permute-start | bytes 1179656 | tf_op jit(solution)/shard_map/ppermute | solution.py:240
  120.7 13.2 %collective-permute-start.27 = (bf16[48,4096]{1,0:T(8,128)(2,1)S(1)}, bf16[48,4096]{1,0:T(8,128)(2,1)S(1)}, u32[]{:S(2)}, u32[]{:S(2)}) collective-permute-start(bf16[48,4096]{1,0:T(8,128)(2,1)S(1)} %get-tuple-element.29), channel_id=1, source_target_pairs={{0,1},{1,0},{2,3},{3,2},{4,5},{5,4},{6,7},{7,6},{8,9},{9,8},{10,11... | collective-permute-start | bytes 1179656 | tf_op jit(solution)/shard_map/ppermute | solution.py:266
  133.2 4.4 %collective-permute-start.22 = (bf16[48,4096]{1,0:T(8,128)(2,1)S(1)}, bf16[48,4096]{1,0:T(8,128)(2,1)S(1)}, u32[]{:S(2)}, u32[]{:S(2)}) collective-permute-start(bf16[48,4096]{1,0:T(8,128)(2,1)S(1)} %get-tuple-element.25), channel_id=1, source_target_pairs={{0,1},{1,0},{2,3},{3,2},{4,5},{5,4},{6,7},{7,6},{8,9},{9,8},{10,11... | collective-permute-start | bytes 1179656 | tf_op jit(solution)/shard_map/ppermute | solution.py:266
  133.3 2.3 %collective-permute-start.29 = (bf16[48,4096]{1,0:T(8,128)(2,1)S(1)}, bf16[48,4096]{1,0:T(8,128)(2,1)S(1)}, u32[]{:S(2)}, u32[]{:S(2)}) collective-permute-start(bf16[48,4096]{1,0:T(8,128)(2,1)S(1)} %get-tuple-element.31), channel_id=1, source_target_pairs={{0,1},{1,0},{2,3},{3,2},{4,5},{5,4},{6,7},{7,6},{8,9},{9,8},{10,11... | collective-permute-start | bytes 1179656 | tf_op jit(solution)/shard_map/ppermute | solution.py:266
  133.8 2.9 %collective-permute-start.31 = (bf16[48,4096]{1,0:T(8,128)(2,1)S(1)}, bf16[48,4096]{1,0:T(8,128)(2,1)S(1)}, u32[]{:S(2)}, u32[]{:S(2)}) collective-permute-start(bf16[48,4096]{1,0:T(8,128)(2,1)S(1)} %get-tuple-element.33), channel_id=1, source_target_pairs={{0,1},{1,0},{2,3},{3,2},{4,5},{5,4},{6,7},{7,6},{8,9},{9,8},{10,11... | collective-permute-start | bytes 1179656 | tf_op jit(solution)/shard_map/ppermute | solution.py:266
  134.0 16.2 %collective-permute-start.28 = (bf16[48,4096]{1,0:T(8,128)(2,1)S(1)}, bf16[48,4096]{1,0:T(8,128)(2,1)S(1)}, u32[]{:S(2)}, u32[]{:S(2)}) collective-permute-start(bf16[48,4096]{1,0:T(8,128)(2,1)S(1)} %add_convert_fusion.2), channel_id=1, source_target_pairs={{0,2},{2,0},{4,6},{6,4},{1,3},{3,1},{5,7},{7,5},{8,10},{10,8},{12,... | collective-permute-start | bytes 1179656 | tf_op jit(solution)/shard_map/ppermute | solution.py:269
  135.7 18.1 %collective-permute-start.30 = (bf16[48,4096]{1,0:T(8,128)(2,1)S(1)}, bf16[48,4096]{1,0:T(8,128)(2,1)S(1)}, u32[]{:S(2)}, u32[]{:S(2)}) collective-permute-start(bf16[48,4096]{1,0:T(8,128)(2,1)S(1)} %add_convert_fusion.1), channel_id=1, source_target_pairs={{0,4},{2,6},{4,0},{6,2},{1,5},{3,7},{5,1},{7,3},{8,12},{10,14},{12... | collective-permute-start | bytes 1179656 | tf_op jit(solution)/shard_map/ppermute | solution.py:269
  136.8 34.3 %collective-permute-start.32 = (bf16[48,4096]{1,0:T(8,128)(2,1)S(1)}, bf16[48,4096]{1,0:T(8,128)(2,1)S(1)}, u32[]{:S(2)}, u32[]{:S(2)}) collective-permute-start(bf16[48,4096]{1,0:T(8,128)(2,1)S(1)} %add_convert_fusion), channel_id=1, source_target_pairs={{0,6},{2,4},{4,2},{6,0},{1,7},{3,5},{5,3},{7,1},{8,14},{10,12},{12... | collective-permute-start | bytes 1179656 | tf_op jit(solution)/shard_map/ppermute | solution.py:269
  137.7 34.7 %collective-permute-start.33 = (bf16[48,4096]{1,0:T(8,128)(2,1)S(1)}, bf16[48,4096]{1,0:T(8,128)(2,1)S(1)}, u32[]{:S(2)}, u32[]{:S(2)}) collective-permute-start(bf16[48,4096]{1,0:T(8,128)(2,1)S(1)} %add_convert_fusion.3.refs_0_), channel_id=1, source_target_pairs={{0,1},{1,0},{2,3},{3,2},{4,5},{5,4},{6,7},{7,6},{8,9},{9,8},{10,11... | collective-permute-start | bytes 1179656 | tf_op jit(solution)/shard_map/ppermute | solution.py:271
  150.1 22.3 %collective-permute-start.34 = (bf16[48,4096]{1,0:T(8,128)(2,1)S(1)}, bf16[48,4096]{1,0:T(8,128)(2,1)S(1)}, u32[]{:S(2)}, u32[]{:S(2)}) collective-permute-start(bf16[48,4096]{1,0:T(8,128)(2,1)S(1)} %collective-permute-done.28.refs_1_), channel_id=1, source_target_pairs={{0,1},{1,0},{2,3},{3,2},{4,5},{5,4},{6,7},{7,6},{8,9},{9,8},{10,11... | collective-permute-start | bytes 1179656 | tf_op jit(solution)/shard_map/ppermute | solution.py:271
  153.8 18.7 %collective-permute-start.35 = (bf16[48,4096]{1,0:T(8,128)(2,1)S(1)}, bf16[48,4096]{1,0:T(8,128)(2,1)S(1)}, u32[]{:S(2)}, u32[]{:S(2)}) collective-permute-start(bf16[48,4096]{1,0:T(8,128)(2,1)S(1)} %collective-permute-done.30.refs_2_), channel_id=1, source_target_pairs={{0,1},{1,0},{2,3},{3,2},{4,5},{5,4},{6,7},{7,6},{8,9},{9,8},{10,11... | collective-permute-start | bytes 1179656 | tf_op jit(solution)/shard_map/ppermute | solution.py:271
  171.1 2.7 %collective-permute-start.36 = (bf16[48,4096]{1,0:T(8,128)(2,1)S(1)}, bf16[48,4096]{1,0:T(8,128)(2,1)S(1)}, u32[]{:S(2)}, u32[]{:S(2)}) collective-permute-start(bf16[48,4096]{1,0:T(8,128)(2,1)S(1)} %collective-permute-done.32.refs_3_), channel_id=1, source_target_pairs={{0,1},{1,0},{2,3},{3,2},{4,5},{5,4},{6,7},{7,6},{8,9},{9,8},{10,11... | collective-permute-start | bytes 1179656 | tf_op jit(solution)/shard_map/ppermute | solution.py:271
  (9 other events, 8.7 us)

commit v2 on v1

--- a/solution.py
+++ b/solution.py
@@ -11,18 +11,26 @@
 F32 = jnp.float32
 LAST = (((1,), (1,)), ((), ()))
 FIRST = (((0,), (0,)), ((), ()))
-VMEM_LIMIT = 48 * 1024 * 1024
+VMEM_LIMIT = 16 * 1024 * 1024
+MOST_VMEM = 60 * 1024 * 1024
 
 
 def flips(size, step):
     return [(i, i ^ step) for i in range(size)]
 
 
-def select_kernel(n_experts, halves, shards, cluster_ref, gate_ref, up_ref, down_ref, *out_refs):
+def select_kernel(n_experts, halves, shards, cluster_hbm, gate_hbm, up_hbm, down_hbm, *refs):
+    out_refs, scratch, sems = refs[:n_experts], refs[n_experts:-1], refs[-1]
+    sources = (cluster_hbm, gate_hbm, up_hbm, down_hbm)
+    copies = [pltpu.make_async_copy(a, b, sems.at[i]) for i, (a, b) in enumerate(zip(sources, scratch))]
+    for copy in copies:
+        copy.start()
+    cluster_ref, *weight_refs = scratch
+    copies[0].wait()
     mine = lax.axis_index("expert")
     source = mine * halves + lax.axis_index("tensor")
     slots = cluster_ref.shape[1]
-    rows = gate_ref.shape[0]
+    rows = gate_hbm.shape[0]
     half = slots // halves
     run = half // shards
     wide = n_experts * halves * run
@@ -40,7 +48,8 @@
     neuron = lax.broadcasted_iota(jnp.int32, (rows, wide), 0)
     table = jnp.where(neuron == local, 1.0, 0.0).astype(BF16)
     per = halves * run
-    for w, ref in enumerate((gate_ref, up_ref, down_ref)):
+    for w, ref in enumerate(weight_refs):
+        copies[w + 1].wait()
         chosen = lax.dot_general(table, ref[...], FIRST, preferred_element_type=F32).astype(BF16)
         for k in range(n_experts):
             out_refs[k][w * per:(w + 1) * per, :] = chosen[k * per:(k + 1) * per]
@@ -97,66 +106,41 @@
     pl.when(core != 0)(lambda: both(other_refs, mine_refs))
 
 
-def expert_kernel(n_experts, n_dp, members, capacity, *refs):
-    n_parts = n_dp + 1
-    n_rows = len(members)
+def expert_kernel(n_experts, n_dp, n_rows, *refs):
     refs = list(refs)
-    weights = [[refs.pop(0) for _ in range(n_parts)] for _ in range(n_experts)]
+    weights = [[refs.pop(0) for _ in range(n_dp + 1)] for _ in range(n_experts)]
     mine_refs = [refs.pop(0) for _ in range(n_rows)]
     other_refs = [refs.pop(0) for _ in range(n_rows)]
     keep_refs = [refs.pop(0) for _ in range(n_rows)]
     give_refs = [refs.pop(0) for _ in range(n_rows)]
-    w_ref, x_ref, dy_ref, w_sem, row_sem = refs
     me = lax.axis_index("dp")
-    core = lax.axis_index("tensor")
-    deep, width = w_ref.shape[2], w_ref.shape[3]
-    per = deep // 3
-
-    def weight_copies(j):
-        copies = []
+    first = lax.axis_index("tensor") == 0
+    deep, width = weights[0][0].shape
+    capacity = mine_refs[0].shape[0]
+    per, cut = deep // 3, deep // 2
+
+    def columns(j):
+        return pl.ds(pl.multiple_of((me ^ j) * width, width), width)
+
+    def kind(j, w):
+        parts = []
+        lower, upper = w * per, (w + 1) * per
         for k in range(n_experts):
             if j < n_dp - 1:
-                pairs = [(weights[k][j], w_ref.at[k, j], j)]
-            else:
-                cut = deep // 2
-                pairs = [
-                    (weights[k][j], w_ref.at[k, j, pl.ds(0, cut)], j),
-                    (weights[k][j + 1], w_ref.at[k, j, pl.ds(cut, cut)], j + 1),
-                ]
-            copies += [pltpu.make_async_copy(a, b, w_sem.at[k, s]) for a, b, s in pairs]
-        return copies
-
-    def row_copies(first, second):
-        copies = []
-        for i in range(n_rows):
-            at = pl.ds(i * capacity, capacity)
-            copies.append(pltpu.make_async_copy(first[i], x_ref.at[at], row_sem.at[0, i]))
-            copies.append(pltpu.make_async_copy(second[i], dy_ref.at[at], row_sem.at[1, i]))
-        return copies
-
-    def start(copies):
-        for copy in copies:
-            copy.start()
-
-    pl.when(core == 0)(lambda: start(row_copies(mine_refs, other_refs)))
-    pl.when(core != 0)(lambda: start(row_copies(other_refs, mine_refs)))
-    for j in range(n_dp):
-        start(weight_copies(j))
-    for copy in row_copies(mine_refs, other_refs):
-        copy.wait()
-
-    def columns(j):
-        return pl.ds(pl.multiple_of((me ^ j) * width, width), width)
-
-    def kind(j, w):
-        return jnp.concatenate([w_ref[k, j, w * per:(w + 1) * per, :] for k in range(n_experts)], axis=0)
+                parts.append(weights[k][j][lower:upper, :])
+                continue
+            if lower < cut:
+                parts.append(weights[k][j][lower:min(upper, cut), :])
+            if upper > cut:
+                parts.append(weights[k][j + 1][max(lower, cut) - cut:upper - cut, :])
+        return jnp.concatenate(parts, axis=0)
 
     pre_gate = pre_up = grad_hidden = 0.0
     for j in range(n_dp):
-        for copy in weight_copies(j):
-            copy.wait()
-        x = x_ref[:, columns(j)]
-        dy = dy_ref[:, columns(j)]
+        mine = jnp.concatenate([ref[:, columns(j)] for ref in mine_refs], axis=0)
+        other = jnp.concatenate([ref[:, columns(j)] for ref in other_refs], axis=0)
+        x = jnp.where(first, mine, other)
+        dy = jnp.where(first, other, mine)
         pre_gate += lax.dot_general(x, kind(j, 0), LAST, preferred_element_type=F32)
         pre_up += lax.dot_general(x, kind(j, 1), LAST, preferred_element_type=F32)
         grad_hidden += lax.dot_general(dy, kind(j, 2), LAST, preferred_element_type=F32)
@@ -165,18 +149,19 @@
     grad_gate = (grad_hidden * pre_up * sig * (1.0 + pre_gate * (1.0 - sig))).astype(BF16)
     grad_up = (grad_hidden * pre_gate * sig).astype(BF16)
     for j in range(n_dp):
-        out = jnp.dot(hidden, kind(j, 2), preferred_element_type=F32).astype(BF16)
+        out = jnp.dot(hidden, kind(j, 2), preferred_element_type=F32)
         grad = jnp.dot(grad_gate, kind(j, 0), preferred_element_type=F32)
-        grad = (grad + jnp.dot(grad_up, kind(j, 1), preferred_element_type=F32)).astype(BF16)
-
-        def store(kept, given):
-            for i in range(n_rows):
-                at = slice(i * capacity, (i + 1) * capacity)
-                keep_refs[i][:, columns(j)] = kept[at]
-                give_refs[i][:, columns(j)] = given[at]
-
-        pl.when(core == 0)(lambda: store(out, grad))
-        pl.when(core != 0)(lambda: store(grad, out))
+        grad = grad + jnp.dot(grad_up, kind(j, 1), preferred_element_type=F32)
+        kept = jnp.where(first, out, grad).astype(BF16)
+        given = jnp.where(first, grad, out).astype(BF16)
+        for i in range(n_rows):
+            at = slice(i * capacity, (i + 1) * capacity)
+            keep_refs[i][:, columns(j)] = kept[at]
+            give_refs[i][:, columns(j)] = given[at]
+
+
+def after(values, awaited):
+    return lax.optimization_barrier((tuple(values), tuple(awaited)))[0]
 
 
 def aligned_plan(tokens, cotangent, routes, cluster, w_gate, w_up, w_down):
@@ -191,30 +176,53 @@
     capacity = 3 * tok_count // (2 * n_experts)
     params = pltpu.CompilerParams(vmem_limit_bytes=VMEM_LIMIT)
     vmem = pl.BlockSpec(memory_space=pltpu.VMEM)
-    anywhere = pl.BlockSpec(memory_space=pl.ANY)
     shape = jax.ShapeDtypeStruct
 
     sent_w = pl.pallas_call(
         functools.partial(select_kernel, n_experts, halves, shards),
         out_shape=[shape((3 * per, width_part), BF16)] * n_experts,
-        in_specs=[vmem] * 4,
+        in_specs=[pl.BlockSpec(memory_space=pltpu.HBM)] * 4,
         out_specs=[vmem] * n_experts,
-        compiler_params=params,
+        scratch_shapes=[pltpu.VMEM(cluster.shape, jnp.int32)]
+        + [pltpu.VMEM(w_gate.shape, BF16)] * 3
+        + [pltpu.SemaphoreType.DMA((4,))],
+        compiler_params=pltpu.CompilerParams(vmem_limit_bytes=MOST_VMEM),
         name="select_rows",
     )(cluster, w_gate, w_up, w_down)
 
-    def over_dp(chunk):
-        cut = chunk.shape[0] // 2
-        near = lax.ppermute(chunk, "dp", flips(n_dp, 1))
-        far = lax.ppermute(chunk, "dp", flips(n_dp, 2))
+    def planes(chunk, k):
+        return lax.ppermute(chunk, "expert", flips(n_experts, k))
+
+    weights = [None] * n_experts
+    arrived = {}
+    near_far = {}
+
+    def over_dp(k, awaited):
+        (chunk,) = after([arrived[k]], [awaited])
+        near_far[k] = (
+            lax.ppermute(chunk, "dp", flips(n_dp, 1)),
+            lax.ppermute(chunk, "dp", flips(n_dp, 2)),
+        )
+
+    def over_dp_far(k):
+        near, far = near_far[k]
+        cut = near.shape[0] // 2
         low = lax.ppermute(near[:cut], "dp", flips(n_dp, 2))
         high = lax.ppermute(far[cut:], "dp", flips(n_dp, 1))
-        return [chunk, near, far, low, high]
-
-    weights = [None] * n_experts
-    weights[0] = over_dp(sent_w[0])
-    for k in (2, 1, 3):
-        weights[k] = over_dp(lax.ppermute(sent_w[k], "expert", flips(n_experts, k)))
+        weights[k] = [arrived[k], near, far, low, high]
+
+    arrived[0] = sent_w[0]
+    arrived[3] = planes(sent_w[3], 3)
+    arrived[1] = planes(sent_w[1], 1)
+    over_dp(0, [])
+    over_dp_far(0)
+    arrived[2] = planes(after([sent_w[2]], [arrived[1]])[0], 2)
+    over_dp(1, near_far[0])
+    over_dp_far(1)
+    over_dp(3, (near_far[1], weights[0][3:]))
+    over_dp_far(3)
+    over_dp(2, (near_far[3], weights[1][3:]))
+    over_dp_far(2)
 
     route_row = routes.reshape(1, tok_count)
     block = width // 4
@@ -235,38 +243,42 @@
 
     swap = flips(halves, 1)
     rows = {0: sent[0]}
-    for k in (2, 1, 3):
-        rows[k] = lax.ppermute(sent[k], "expert", flips(n_experts, k))
+    early = after([sent[2], sent[1]], [arrived[3], arrived[1]])
+    rows[2] = planes(early[0], 2)
+    rows[1] = planes(early[1], 1)
+    (late,) = after([sent[3]], [arrived[2]])
+    rows[3] = planes(late, 3)
     others = {k: lax.ppermute(rows[k], "tensor", swap) for k in (0, 2, 1, 3)}
 
     mine, other = {}, {}
-    for members in ((2, 0), (3, 1)):
+    returned = []
+    for members in ((2, 1), (3, 0)):
         count = len(members)
+        here = {k: rows[k] for k in members}
+        if returned:
+            here[members[0]] = after([rows[members[0]]], returned)[0]
         results = pl.pallas_call(
-            functools.partial(expert_kernel, n_experts, n_dp, members, capacity),
+            functools.partial(expert_kernel, n_experts, n_dp, count),
             out_shape=[shape((capacity, width), BF16)] * (2 * count),
-            in_specs=[anywhere] * (n_experts * (n_dp + 1) + 2 * count),
+            in_specs=[vmem] * (n_experts * (n_dp + 1) + 2 * count),
             out_specs=[vmem] * (2 * count),
-            scratch_shapes=[
-                pltpu.VMEM((n_experts, n_dp, 3 * per, width_part), BF16),
-                pltpu.VMEM((count * capacity, width), BF16),
-                pltpu.VMEM((count * capacity, width), BF16),
-                pltpu.SemaphoreType.DMA((n_experts, n_dp + 1)),
-                pltpu.SemaphoreType.DMA((2, count)),
-            ],
             compiler_params=params,
+            cost_estimate=pl.CostEstimate(flops=1000, bytes_accessed=1000, transcendentals=0),
             name="expert_math",
         )(
             *[part for parts in weights for part in parts],
-            *[rows[k] for k in members],
+            *[here[k] for k in members],
             *[others[k] for k in members],
         )
         for i, k in enumerate(members):
             kept, given = results[i], results[count + i]
             got = lax.ppermute(given, "tensor", swap)
             total = (kept.astype(F32) + got.astype(F32)).astype(BF16)
+            returned.append(total)
+            if k == 3:
+                (total,) = after([total], [mine[2]])
             if k:
-                total = lax.ppermute(total, "expert", flips(n_experts, k))
+                total = planes(total, k)
             mine[k] = total
             other[k] = lax.ppermute(total, "tensor", swap)
 

time: 177 us -> 141 us (0.80)
  starting transfers between devices: 50.3 us -> 38.9 us
  waiting for transfers between devices: 95.2 us -> 84.7 us
  Pallas kernels: 22.8 us -> 15.6 us
  local copies, waits for them, and re-layouts: 7.22 us -> 0.13 us
    ppermute x4, starting transfers between devices: 15 us -> 3.6 us  [aligned_plan(): others = {k: lax.ppermute(rows[k], 'tensor', swap) for k in (0, 2, 1, 3)}]
    ppermute x25, waiting for transfers between devices: 92.3 us -> 81.5 us  [the longest x9 64 us: planes(): return lax.ppermute(chunk, 'expert', flips(n_experts, k))]
    ppermute x25, starting transfers between devices: 19 us -> 29.3 us  [the longest x9 17 us: planes(): return lax.ppermute(chunk, 'expert', flips(n_experts, k))]
    pallas_call x2, Pallas kernels: 17.5 us -> 7.79 us  [aligned_plan(): pl.pallas_call(functools.partial(expert_kernel, n_experts, n_dp, count),...]
    ppermute x4, starting transfers between devices: 13.4 us -> 3.63 us  [aligned_plan(): other[k] = lax.ppermute(total, 'tensor', swap)]
    unnamed x40 -> x8, local copies, waits for them, and re-layouts: 7.11 us -> 0.02 us
    pallas_call x1, Pallas kernels: 0.69 us -> 3.25 us  [aligned_plan(): pl.pallas_call(functools.partial(select_kernel, n_experts, halves, shards...]
  transfers between devices with their start and end apart: 37 -> 37, of which waited for: 16 -> 16; matrix products, arithmetic and copies ran while one was open for 0% -> 0% of each run, Pallas kernels for 11% -> 4%
where the time goes in v2:
time: 141 us; the launch traced here: 140 us
  waiting for transfers between devices  84.7 us (60%)
  starting transfers between devices  38.9 us (28%)
  Pallas kernels  15.6 us (11%)
    ppermute x9, waiting for transfers between devices, planes(): return lax.ppermute(chunk, 'expert', flips(n_experts, k))  64 us
    ppermute x9, starting transfers between devices, planes(): return lax.ppermute(chunk, 'expert', flips(n_experts, k))  17 us
    pallas_call x2, Pallas kernels, aligned_plan(): pl.pallas_call(functools.partial(expert_kernel, n_experts, n_dp, count),...  7.79 us
    ppermute x4, waiting for transfers between devices, over_dp_far(): low = lax.ppermute(near[:cut], 'dp', flips(n_dp, 2))  5.78 us
    ppermute x4, waiting for transfers between devices, over_dp_far(): high = lax.ppermute(far[cut:], 'dp', flips(n_dp, 1))  5.63 us
    ppermute x4, waiting for transfers between devices, over_dp(): lax.ppermute(chunk, 'dp', flips(n_dp, 1))  5.16 us
    ppermute x4, starting transfers between devices, over_dp_far(): low = lax.ppermute(near[:cut], 'dp', flips(n_dp, 2))  3.96 us
    ppermute x4, starting transfers between devices, aligned_plan(): other[k] = lax.ppermute(total, 'tensor', swap)  3.63 us
  transfers between devices with their start and end apart: 37, of which 16 were waited for; matrix products, arithmetic and copies ran while one was open for 0% of the time, Pallas kernels for 4%

profile of v2, /device:TPU:9, one launch (start us, length us, event | category | flops | bytes accessed | tf_op | source)
XLA Modules:
  0.0 140.4 jit_solution(17877365877294974463)
XLA Ops:
  0.7 3.2 %select_rows.1 = (bf16[192,1024]{1,0:T(8,128)(2,1)}, bf16[192,1024]{1,0:T(8,128)(2,1)}, bf16[192,1024]{1,0:T(8,128)(2,1)}, bf16[192,1024]{1,0:T(8,128)(2,1)}) custom-call(s32[4,512]{1,0:T(4,128)} %cluster_hbm.1, bf16[231,1024]{1,0:T(8,128)(2,1)} %gate_hbm.1, bf16[231,1024]{1,0:T(8,128)(2,1)} %up_hbm.1, bf16[231,1024]{1,0:T(8,128)(2,1)} %down_hbm.1), custom_call_target="tpu_custom_call" | custom-call | tf_op jit(solution)/shard_map/select_rows/pallas_call | solution.py:181
  3.9 1.3 collective-permute-start
  5.2 1.2 collective-permute-start.1
  6.6 2.4 %collective-permute-start.10 = (bf16[192,1024]{1,0:T(8,128)(2,1)}, bf16[192,1024]{1,0:T(8,128)(2,1)S(1)}, u32[]{:S(2)}, u32[]{:S(2)}) collective-permute-start(bf16[192,1024]{1,0:T(8,128)(2,1)} %get-tuple-element.32), channel_id=1, source_target_pairs={{0,6},{2,4},{4,2},{6,0},{1,7},{3,5},{5,3},{7,1},{8,14},{10,12},{12... | collective-permute-start | bytes 1179656 | tf_op jit(solution)/shard_map/ppermute | solution.py:194
  9.0 5.1 %collective-permute-done.refs_1_ = bf16[192,1024]{1,0:T(8,128)(2,1)S(1)} collective-permute-done((bf16[192,1024]{1,0:T(8,128)(2,1)}, bf16[192,1024]{1,0:T(8,128)(2,1)S(1)}, u32[]{:S(2)}, u32[]{:S(2)}) %collective-permute-start) | collective-permute-done | bytes 393248 | tf_op jit(solution)/shard_map/ppermute | solution.py:203
  14.2 0.9 collective-permute-done.1.refs_2_
  15.1 0.9 collective-permute-done.4.refs_5_
  16.3 0.4 collective-permute-start.6
  16.6 1.2 collective-permute-start.2
  17.8 1.3 collective-permute-start.3
  19.1 7.5 %collective-permute-start.9 = (bf16[192,1024]{1,0:T(8,128)(2,1)}, bf16[192,1024]{1,0:T(8,128)(2,1)S(1)}, u32[]{:S(2)}, u32[]{:S(2)}) collective-permute-start(bf16[192,1024]{1,0:T(8,128)(2,1)} %get-tuple-element.31), channel_id=1, source_target_pairs={{0,4},{2,6},{4,0},{6,2},{1,5},{3,7},{5,1},{7,3},{8,12},{10,14},{12... | collective-permute-start | bytes 1179656 | tf_op jit(solution)/shard_map/ppermute | solution.py:194
  26.6 0.3 collective-permute-done.2.refs_3_
  26.9 1.3 collective-permute-start.11
  28.2 0.4 collective-permute-start.12
  28.6 1.2 collective-permute-start.7
  29.7 1.5 %dispatch_rows.1 = (bf16[48,4096]{1,0:T(8,128)(2,1)S(1)}, bf16[48,4096]{1,0:T(8,128)(2,1)S(1)}, bf16[48,4096]{1,0:T(8,128)(2,1)S(1)}, bf16[48,4096]{1,0:T(8,128)(2,1)S(1)}) custom-call(s32[1,128]{1,0:T(1,128)S(1)} %bitcast.1, bf16[128,4096]{1,0:T(8,128)(2,1)S(1)} %copy-done.1, bf16[128,4096]{1,0:T(8,128)(2,1)S(1)} %copy-done.2), custom_call_target="tpu_custom_call" | custom-call | tf_op jit(solution)/shard_map/dispatch_rows/pallas_call | solution.py:229
  31.3 0.7 collective-permute-start.20
  32.0 20.4 %collective-permute-done.9.refs_10_ = bf16[192,1024]{1,0:T(8,128)(2,1)S(1)} collective-permute-done((bf16[192,1024]{1,0:T(8,128)(2,1)}, bf16[192,1024]{1,0:T(8,128)(2,1)S(1)}, u32[]{:S(2)}, u32[]{:S(2)}) %collective-permute-start.9) | collective-permute-done | bytes 393248 | tf_op jit(solution)/shard_map/ppermute | solution.py:194
  52.7 5.6 %collective-permute-done.8.refs_9_ = bf16[96,1024]{1,0:T(8,128)(2,1)S(1)} collective-permute-done((bf16[96,1024]{1,0:T(8,128)(2,1)S(1)}, bf16[96,1024]{1,0:T(8,128)(2,1)S(1)}, u32[]{:S(2)}, u32[]{:S(2)}) %collective-permute-start.8) | collective-permute-done | bytes 196640 | tf_op jit(solution)/shard_map/ppermute | solution.py:211
  58.3 0.3 collective-permute-start.13
  58.8 2.0 %collective-permute-done.20.refs_20_ = bf16[48,4096]{1,0:T(8,128)(2,1)S(1)} collective-permute-done((bf16[48,4096]{1,0:T(8,128)(2,1)S(1)}, bf16[48,4096]{1,0:T(8,128)(2,1)S(1)}, u32[]{:S(2)}, u32[]{:S(2)}) %collective-permute-start.20) | collective-permute-done | bytes 393248 | tf_op jit(solution)/shard_map/ppermute | solution.py:194
  60.8 0.5 collective-permute-start.22
  61.3 6.2 %collective-permute-done.21.refs_21_ = bf16[48,4096]{1,0:T(8,128)(2,1)S(1)} collective-permute-done((bf16[48,4096]{1,0:T(8,128)(2,1)S(1)}, bf16[48,4096]{1,0:T(8,128)(2,1)S(1)}, u32[]{:S(2)}, u32[]{:S(2)}) %collective-permute-start.21) | collective-permute-done | bytes 393248 | tf_op jit(solution)/shard_map/ppermute | solution.py:194
  67.5 1.3 collective-permute-start.23
  69.1 0.6 collective-permute-start.18
  69.7 1.4 collective-permute-start.15
  71.1 1.0 collective-permute-start.16
  72.1 2.1 %collective-permute-start.19 = (bf16[48,4096]{1,0:T(8,128)(2,1)S(1)}, bf16[48,4096]{1,0:T(8,128)(2,1)S(1)}, u32[]{:S(2)}, u32[]{:S(2)}) collective-permute-start(bf16[48,4096]{1,0:T(8,128)(2,1)S(1)} %get-tuple-element.36), channel_id=1, source_target_pairs={{0,6},{2,4},{4,2},{6,0},{1,7},{3,5},{5,3},{7,1},{8,14},{10,12},{12... | collective-permute-start | bytes 1179656 | tf_op jit(solution)/shard_map/ppermute | solution.py:194
  74.1 1.2 collective-permute-done.17.refs_18_
  75.4 4.2 %collective-permute-done.15.refs_13_ = bf16[96,1024]{1,0:T(8,128)(2,1)S(1)} collective-permute-done((bf16[96,1024]{1,0:T(8,128)(2,1)S(1)}, bf16[96,1024]{1,0:T(8,128)(2,1)S(1)}, u32[]{:S(2)}, u32[]{:S(2)}) %collective-permute-start.15) | collective-permute-done | bytes 196640 | tf_op jit(solution)/shard_map/ppermute | solution.py:210
  79.6 3.9 %expert_math.2 = (bf16[48,4096]{1,0:T(8,128)(2,1)S(1)}, bf16[48,4096]{1,0:T(8,128)(2,1)S(1)}, bf16[48,4096]{1,0:T(8,128)(2,1)S(1)}, bf16[48,4096]{1,0:T(8,128)(2,1)S(1)}) custom-call(bf16[192,1024]{1,0:T(8,128)(2,1)S(1)} %copy-done, bf16[192,1024]{1,0:T(8,128)(2,1)S(1)} %collective-permute-done.refs_1_, ...), custom_call_target="tpu_custom_call" | custom-call | flops 1000 | bytes 1000 | tf_op jit(solution)/shard_map/expert_math/pallas_call | solution.py:260
  83.5 1.1 collective-permute-start.25
  84.7 6.2 %collective-permute-done.19.refs_20_ = bf16[48,4096]{1,0:T(8,128)(2,1)S(1)} collective-permute-done((bf16[48,4096]{1,0:T(8,128)(2,1)S(1)}, bf16[48,4096]{1,0:T(8,128)(2,1)S(1)}, u32[]{:S(2)}, u32[]{:S(2)}) %collective-permute-start.19) | collective-permute-done | bytes 393248 | tf_op jit(solution)/shard_map/ppermute | solution.py:194
  90.9 1.8 %collective-permute-start.26 = (bf16[48,4096]{1,0:T(8,128)(2,1)S(1)}, bf16[48,4096]{1,0:T(8,128)(2,1)S(1)}, u32[]{:S(2)}, u32[]{:S(2)}) collective-permute-start(bf16[48,4096]{1,0:T(8,128)(2,1)S(1)} %collective-permute-done.19.refs_20_), channel_id=1, source_target_pairs={{0,1},{1,0},{2,3},{3,2},{4,5},{5,4},{6,7},{7,6},{8,9},{9,8},{10,11... | collective-permute-start | bytes 1179656 | tf_op jit(solution)/shard_map/ppermute | solution.py:251
  92.7 1.8 %collective-permute-done.24 = bf16[48,4096]{1,0:T(8,128)(2,1)S(1)} collective-permute-done((bf16[48,4096]{1,0:T(8,128)(2,1)S(1)}, bf16[48,4096]{1,0:T(8,128)(2,1)S(1)}, u32[]{:S(2)}, u32[]{:S(2)}) %collective-permute-start.24) | collective-permute-done | bytes 393248 | tf_op jit(solution)/shard_map/ppermute | solution.py:275
  94.7 3.9 %expert_math.3 = (bf16[48,4096]{1,0:T(8,128)(2,1)S(1)}, bf16[48,4096]{1,0:T(8,128)(2,1)S(1)}, bf16[48,4096]{1,0:T(8,128)(2,1)S(1)}, bf16[48,4096]{1,0:T(8,128)(2,1)S(1)}) custom-call(bf16[192,1024]{1,0:T(8,128)(2,1)S(1)} %copy-done, bf16[192,1024]{1,0:T(8,128)(2,1)S(1)} %collective-permute-done.refs_1_, ...), custom_call_target="tpu_custom_call" | custom-call | flops 1000 | bytes 1000 | tf_op jit(solution)/shard_map/expert_math/pallas_call | solution.py:260
  98.6 0.4 collective-permute-start.31
  99.0 2.6 %collective-permute-start.29 = (bf16[48,4096]{1,0:T(8,128)(2,1)S(1)}, bf16[48,4096]{1,0:T(8,128)(2,1)S(1)}, u32[]{:S(2)}, u32[]{:S(2)}) collective-permute-start(bf16[48,4096]{1,0:T(8,128)(2,1)S(1)} %add_convert_fusion.2), channel_id=1, source_target_pairs={{0,2},{2,0},{4,6},{6,4},{1,3},{3,1},{5,7},{7,5},{8,10},{10,8},{12,... | collective-permute-start | bytes 1179656 | tf_op jit(solution)/shard_map/ppermute | solution.py:194
  101.7 0.7 collective-permute-start.28
  102.5 13.6 %collective-permute-done.30.refs_2_ = bf16[48,4096]{1,0:T(8,128)(2,1)S(1)} collective-permute-done((bf16[48,4096]{1,0:T(8,128)(2,1)S(1)}, bf16[48,4096]{1,0:T(8,128)(2,1)S(1)}, u32[]{:S(2)}, u32[]{:S(2)}) %collective-permute-start.30) | collective-permute-done | bytes 393248 | tf_op jit(solution)/shard_map/ppermute | solution.py:194
  116.0 1.5 %collective-permute-start.32 = (bf16[48,4096]{1,0:T(8,128)(2,1)S(1)}, bf16[48,4096]{1,0:T(8,128)(2,1)S(1)}, u32[]{:S(2)}, u32[]{:S(2)}) collective-permute-start(bf16[48,4096]{1,0:T(8,128)(2,1)S(1)} %add_convert_fusion), channel_id=1, source_target_pairs={{0,6},{2,4},{4,2},{6,0},{1,7},{3,5},{5,3},{7,1},{8,14},{10,12},{12... | collective-permute-start | bytes 1179656 | tf_op jit(solution)/shard_map/ppermute | solution.py:194
  117.7 1.1 collective-permute-start.33
  118.8 0.4 collective-permute-done.29.refs_1_
  119.2 1.0 collective-permute-start.34
  120.2 14.3 %collective-permute-done.32.refs_3_ = bf16[48,4096]{1,0:T(8,128)(2,1)S(1)} collective-permute-done((bf16[48,4096]{1,0:T(8,128)(2,1)S(1)}, bf16[48,4096]{1,0:T(8,128)(2,1)S(1)}, u32[]{:S(2)}, u32[]{:S(2)}) %collective-permute-start.32) | collective-permute-done | bytes 393248 | tf_op jit(solution)/shard_map/ppermute | solution.py:194
  134.5 1.5 %collective-permute-start.36 = (bf16[48,4096]{1,0:T(8,128)(2,1)S(1)}, bf16[48,4096]{1,0:T(8,128)(2,1)S(1)}, u32[]{:S(2)}, u32[]{:S(2)}) collective-permute-start(bf16[48,4096]{1,0:T(8,128)(2,1)S(1)} %collective-permute-done.32.refs_3_), channel_id=1, source_target_pairs={{0,1},{1,0},{2,3},{3,2},{4,5},{5,4},{6,7},{7,6},{8,9},{9,8},{10,11... | collective-permute-start | bytes 1179656 | tf_op jit(solution)/shard_map/ppermute | solution.py:283
  136.1 1.3 collective-permute-done.36.refs_7_
  137.4 3.0 %merge_rows.1 = (bf16[128,4096]{1,0:T(8,128)(2,1)}, bf16[128,4096]{1,0:T(8,128)(2,1)}) custom-call(s32[1,128]{1,0:T(1,128)S(1)} %bitcast.2, bf16[48,4096]{1,0:T(8,128)(2,1)S(1)} %add_convert_fusion.1.refs_0_, bf16[48,4096]{1,0:T(8,128)(2,1)S(1)} %collective-permute-done.29.refs_1_, bf16[48,4096]{1,0:T(8,128)(2,1)S(1)} %collective-permute-done.30.refs_2_, ...), custom_call_target="tpu_custom_call" | custom-call | tf_op jit(solution)/shard_map/merge_rows/pallas_call | solution.py:286
  (51 shorter events, 1.9 us)
Async XLA Ops:
  0.6 29.1 %copy-start.1 = (bf16[128,4096]{1,0:T(8,128)(2,1)S(1)}, bf16[128,4096]{1,0:T(8,128)(2,1)}, u32[]{:S(2)}) copy-start(bf16[128,4096]{1,0:T(8,128)(2,1)} %tokens_ref.1) | copy-start | bytes 3145732
  0.6 29.1 %copy-start.2 = (bf16[128,4096]{1,0:T(8,128)(2,1)S(1)}, bf16[128,4096]{1,0:T(8,128)(2,1)}, u32[]{:S(2)}) copy-start(bf16[128,4096]{1,0:T(8,128)(2,1)} %cotangent_ref.1) | copy-start | bytes 3145732
  3.9 10.3 %collective-permute-start = (bf16[192,1024]{1,0:T(8,128)(2,1)}, bf16[192,1024]{1,0:T(8,128)(2,1)S(1)}, u32[]{:S(2)}, u32[]{:S(2)}) collective-permute-start(bf16[192,1024]{1,0:T(8,128)(2,1)} %get-tuple-element.27.refs_0_), channel_id=1, source_target_pairs={{0,8},{8,0},{16,24},{24,16},{1,9},{9,1},{17,25},{25,17},{2,10},{10... | collective-permute-start | bytes 1179656 | tf_op jit(solution)/shard_map/ppermute | solution.py:203
  5.2 9.9 %collective-permute-start.1 = (bf16[192,1024]{1,0:T(8,128)(2,1)}, bf16[192,1024]{1,0:T(8,128)(2,1)S(1)}, u32[]{:S(2)}, u32[]{:S(2)}) collective-permute-start(bf16[192,1024]{1,0:T(8,128)(2,1)} %get-tuple-element.27.refs_0_), channel_id=1, source_target_pairs={{0,16},{8,24},{16,0},{24,8},{1,17},{9,25},{17,1},{25,9},{2,18},{10... | collective-permute-start | bytes 1179656 | tf_op jit(solution)/shard_map/ppermute | solution.py:204
  6.4 9.6 %collective-permute-start.4 = (bf16[192,1024]{1,0:T(8,128)(2,1)}, bf16[192,1024]{1,0:T(8,128)(2,1)S(1)}, u32[]{:S(2)}, u32[]{:S(2)}) collective-permute-start(bf16[192,1024]{1,0:T(8,128)(2,1)} %get-tuple-element.28), channel_id=1, source_target_pairs={{0,2},{2,0},{4,6},{6,4},{1,3},{3,1},{5,7},{7,5},{8,10},{10,8},{12,... | collective-permute-start | bytes 1179656 | tf_op jit(solution)/shard_map/ppermute | solution.py:194
  6.6 12.5 %collective-permute-start.10 = (bf16[192,1024]{1,0:T(8,128)(2,1)}, bf16[192,1024]{1,0:T(8,128)(2,1)S(1)}, u32[]{:S(2)}, u32[]{:S(2)}) collective-permute-start(bf16[192,1024]{1,0:T(8,128)(2,1)} %get-tuple-element.32), channel_id=1, source_target_pairs={{0,6},{2,4},{4,2},{6,0},{1,7},{3,5},{5,3},{7,1},{8,14},{10,12},{12... | collective-permute-start | bytes 1179656 | tf_op jit(solution)/shard_map/ppermute | solution.py:194
  16.0 10.9 %collective-permute-start.5 = (bf16[192,1024]{1,0:T(8,128)(2,1)S(1)}, bf16[192,1024]{1,0:T(8,128)(2,1)S(1)}, u32[]{:S(2)}, u32[]{:S(2)}) collective-permute-start(bf16[192,1024]{1,0:T(8,128)(2,1)S(1)} %collective-permute-done.4.refs_5_), channel_id=1, source_target_pairs={{0,8},{8,0},{16,24},{24,16},{1,9},{9,1},{17,25},{25,17},{2,10},{10... | collective-permute-start | bytes 1179656 | tf_op jit(solution)/shard_map/ppermute | solution.py:203
  16.3 10.7 %collective-permute-start.6 = (bf16[192,1024]{1,0:T(8,128)(2,1)S(1)}, bf16[192,1024]{1,0:T(8,128)(2,1)S(1)}, u32[]{:S(2)}, u32[]{:S(2)}) collective-permute-start(bf16[192,1024]{1,0:T(8,128)(2,1)S(1)} %collective-permute-done.4.refs_5_), channel_id=1, source_target_pairs={{0,16},{8,24},{16,0},{24,8},{1,17},{9,25},{17,1},{25,9},{2,18},{10... | collective-permute-start | bytes 1179656 | tf_op jit(solution)/shard_map/ppermute | solution.py:204
  16.6 10.3 %collective-permute-start.2 = (bf16[96,1024]{1,0:T(8,128)(2,1)S(1)}, bf16[96,1024]{1,0:T(8,128)(2,1)S(1)}, u32[]{:S(2)}, u32[]{:S(2)}) collective-permute-start(bf16[96,1024]{1,0:T(8,128)(2,1)S(1)} %slice.32), channel_id=1, source_target_pairs={{0,16},{8,24},{16,0},{24,8},{1,17},{9,25},{17,1},{25,9},{2,18},{10... | collective-permute-start | bytes 589832 | tf_op jit(solution)/shard_map/ppermute | solution.py:210
  17.8 9.1 %collective-permute-start.3 = (bf16[96,1024]{1,0:T(8,128)(2,1)S(1)}, bf16[96,1024]{1,0:T(8,128)(2,1)S(1)}, u32[]{:S(2)}, u32[]{:S(2)}) collective-permute-start(bf16[96,1024]{1,0:T(8,128)(2,1)S(1)} %slice.33), channel_id=1, source_target_pairs={{0,8},{8,0},{16,24},{24,16},{1,9},{9,1},{17,25},{25,17},{2,10},{10... | collective-permute-start | bytes 589832 | tf_op jit(solution)/shard_map/ppermute | solution.py:211
  19.1 33.3 %collective-permute-start.9 = (bf16[192,1024]{1,0:T(8,128)(2,1)}, bf16[192,1024]{1,0:T(8,128)(2,1)S(1)}, u32[]{:S(2)}, u32[]{:S(2)}) collective-permute-start(bf16[192,1024]{1,0:T(8,128)(2,1)} %get-tuple-element.31), channel_id=1, source_target_pairs={{0,4},{2,6},{4,0},{6,2},{1,5},{3,7},{5,1},{7,3},{8,12},{10,14},{12... | collective-permute-start | bytes 1179656 | tf_op jit(solution)/shard_map/ppermute | solution.py:194
  26.9 31.3 %collective-permute-start.11 = (bf16[192,1024]{1,0:T(8,128)(2,1)S(1)}, bf16[192,1024]{1,0:T(8,128)(2,1)S(1)}, u32[]{:S(2)}, u32[]{:S(2)}) collective-permute-start(bf16[192,1024]{1,0:T(8,128)(2,1)S(1)} %collective-permute-done.10.refs_15_), channel_id=1, source_target_pairs={{0,8},{8,0},{16,24},{24,16},{1,9},{9,1},{17,25},{25,17},{2,10},{10... | collective-permute-start | bytes 1179656 | tf_op jit(solution)/shard_map/ppermute | solution.py:203
  28.2 30.1 %collective-permute-start.12 = (bf16[192,1024]{1,0:T(8,128)(2,1)S(1)}, bf16[192,1024]{1,0:T(8,128)(2,1)S(1)}, u32[]{:S(2)}, u32[]{:S(2)}) collective-permute-start(bf16[192,1024]{1,0:T(8,128)(2,1)S(1)} %collective-permute-done.10.refs_15_), channel_id=1, source_target_pairs={{0,16},{8,24},{16,0},{24,8},{1,17},{9,25},{17,1},{25,9},{2,18},{10... | collective-permute-start | bytes 1179656 | tf_op jit(solution)/shard_map/ppermute | solution.py:204
  28.6 1.2 copy-start.3
  28.6 24.1 %collective-permute-start.7 = (bf16[96,1024]{1,0:T(8,128)(2,1)S(1)}, bf16[96,1024]{1,0:T(8,128)(2,1)S(1)}, u32[]{:S(2)}, u32[]{:S(2)}) collective-permute-start(bf16[96,1024]{1,0:T(8,128)(2,1)S(1)} %slice.34), channel_id=1, source_target_pairs={{0,16},{8,24},{16,0},{24,8},{1,17},{9,25},{17,1},{25,9},{2,18},{10... | collective-permute-start | bytes 589832 | tf_op jit(solution)/shard_map/ppermute | solution.py:210
  31.3 29.5 %collective-permute-start.20 = (bf16[48,4096]{1,0:T(8,128)(2,1)S(1)}, bf16[48,4096]{1,0:T(8,128)(2,1)S(1)}, u32[]{:S(2)}, u32[]{:S(2)}) collective-permute-start(bf16[48,4096]{1,0:T(8,128)(2,1)S(1)} %get-tuple-element.39), channel_id=1, source_target_pairs={{0,4},{2,6},{4,0},{6,2},{1,5},{3,7},{5,1},{7,3},{8,12},{10,14},{12... | collective-permute-start | bytes 1179656 | tf_op jit(solution)/shard_map/ppermute | solution.py:194
  52.4 5.9 %collective-permute-start.8 = (bf16[96,1024]{1,0:T(8,128)(2,1)S(1)}, bf16[96,1024]{1,0:T(8,128)(2,1)S(1)}, u32[]{:S(2)}, u32[]{:S(2)}) collective-permute-start(bf16[96,1024]{1,0:T(8,128)(2,1)S(1)} %slice.35), channel_id=1, source_target_pairs={{0,8},{8,0},{16,24},{24,16},{1,9},{9,1},{17,25},{25,17},{2,10},{10... | collective-permute-start | bytes 589832 | tf_op jit(solution)/shard_map/ppermute | solution.py:211
  52.7 14.8 %collective-permute-start.21 = (bf16[48,4096]{1,0:T(8,128)(2,1)S(1)}, bf16[48,4096]{1,0:T(8,128)(2,1)S(1)}, u32[]{:S(2)}, u32[]{:S(2)}) collective-permute-start(bf16[48,4096]{1,0:T(8,128)(2,1)S(1)} %get-tuple-element.40), channel_id=1, source_target_pairs={{0,2},{2,0},{4,6},{6,4},{1,3},{3,1},{5,7},{7,5},{8,10},{10,8},{12,... | collective-permute-start | bytes 1179656 | tf_op jit(solution)/shard_map/ppermute | solution.py:194
  58.3 10.8 %collective-permute-start.13 = (bf16[192,1024]{1,0:T(8,128)(2,1)S(1)}, bf16[192,1024]{1,0:T(8,128)(2,1)S(1)}, u32[]{:S(2)}, u32[]{:S(2)}) collective-permute-start(bf16[192,1024]{1,0:T(8,128)(2,1)S(1)} %collective-permute-done.9.refs_10_), channel_id=1, source_target_pairs={{0,8},{8,0},{16,24},{24,16},{1,9},{9,1},{17,25},{25,17},{2,10},{10... | collective-permute-start | bytes 1179656 | tf_op jit(solution)/shard_map/ppermute | solution.py:203
  58.5 11.2 %collective-permute-start.14 = (bf16[192,1024]{1,0:T(8,128)(2,1)S(1)}, bf16[192,1024]{1,0:T(8,128)(2,1)S(1)}, u32[]{:S(2)}, u32[]{:S(2)}) collective-permute-start(bf16[192,1024]{1,0:T(8,128)(2,1)S(1)} %collective-permute-done.9.refs_10_), channel_id=1, source_target_pairs={{0,16},{8,24},{16,0},{24,8},{1,17},{9,25},{17,1},{25,9},{2,18},{10... | collective-permute-start | bytes 1179656 | tf_op jit(solution)/shard_map/ppermute | solution.py:204
  60.8 10.3 %collective-permute-start.22 = (bf16[48,4096]{1,0:T(8,128)(2,1)S(1)}, bf16[48,4096]{1,0:T(8,128)(2,1)S(1)}, u32[]{:S(2)}, u32[]{:S(2)}) collective-permute-start(bf16[48,4096]{1,0:T(8,128)(2,1)S(1)} %collective-permute-done.20.refs_20_), channel_id=1, source_target_pairs={{0,1},{1,0},{2,3},{3,2},{4,5},{5,4},{6,7},{7,6},{8,9},{9,8},{10,11... | collective-permute-start | bytes 1179656 | tf_op jit(solution)/shard_map/ppermute | solution.py:251
  67.5 4.6 %collective-permute-start.23 = (bf16[48,4096]{1,0:T(8,128)(2,1)S(1)}, bf16[48,4096]{1,0:T(8,128)(2,1)S(1)}, u32[]{:S(2)}, u32[]{:S(2)}) collective-permute-start(bf16[48,4096]{1,0:T(8,128)(2,1)S(1)} %collective-permute-done.21.refs_21_), channel_id=1, source_target_pairs={{0,1},{1,0},{2,3},{3,2},{4,5},{5,4},{6,7},{7,6},{8,9},{9,8},{10,11... | collective-permute-start | bytes 1179656 | tf_op jit(solution)/shard_map/ppermute | solution.py:251
  68.8 6.6 %collective-permute-start.17 = (bf16[96,1024]{1,0:T(8,128)(2,1)S(1)}, bf16[96,1024]{1,0:T(8,128)(2,1)S(1)}, u32[]{:S(2)}, u32[]{:S(2)}) collective-permute-start(bf16[96,1024]{1,0:T(8,128)(2,1)S(1)} %slice.38), channel_id=1, source_target_pairs={{0,16},{8,24},{16,0},{24,8},{1,17},{9,25},{17,1},{25,9},{2,18},{10... | collective-permute-start | bytes 589832 | tf_op jit(solution)/shard_map/ppermute | solution.py:210
  69.0 10.5 %copy-start = (bf16[192,1024]{1,0:T(8,128)(2,1)S(1)}, bf16[192,1024]{1,0:T(8,128)(2,1)}, u32[]{:S(2)}) copy-start(bf16[192,1024]{1,0:T(8,128)(2,1)} %get-tuple-element.27.refs_0_) | copy-start | bytes 1179652
  69.1 6.3 %collective-permute-start.18 = (bf16[96,1024]{1,0:T(8,128)(2,1)S(1)}, bf16[96,1024]{1,0:T(8,128)(2,1)S(1)}, u32[]{:S(2)}, u32[]{:S(2)}) collective-permute-start(bf16[96,1024]{1,0:T(8,128)(2,1)S(1)} %slice.39), channel_id=1, source_target_pairs={{0,8},{8,0},{16,24},{24,16},{1,9},{9,1},{17,25},{25,17},{2,10},{10... | collective-permute-start | bytes 589832 | tf_op jit(solution)/shard_map/ppermute | solution.py:211
  69.7 9.9 %collective-permute-start.15 = (bf16[96,1024]{1,0:T(8,128)(2,1)S(1)}, bf16[96,1024]{1,0:T(8,128)(2,1)S(1)}, u32[]{:S(2)}, u32[]{:S(2)}) collective-permute-start(bf16[96,1024]{1,0:T(8,128)(2,1)S(1)} %slice.36), channel_id=1, source_target_pairs={{0,16},{8,24},{16,0},{24,8},{1,17},{9,25},{17,1},{25,9},{2,18},{10... | collective-permute-start | bytes 589832 | tf_op jit(solution)/shard_map/ppermute | solution.py:210
  71.1 8.5 %collective-permute-start.16 = (bf16[96,1024]{1,0:T(8,128)(2,1)S(1)}, bf16[96,1024]{1,0:T(8,128)(2,1)S(1)}, u32[]{:S(2)}, u32[]{:S(2)}) collective-permute-start(bf16[96,1024]{1,0:T(8,128)(2,1)S(1)} %slice.37), channel_id=1, source_target_pairs={{0,8},{8,0},{16,24},{24,16},{1,9},{9,1},{17,25},{25,17},{2,10},{10... | collective-permute-start | bytes 589832 | tf_op jit(solution)/shard_map/ppermute | solution.py:211
  72.1 18.8 %collective-permute-start.19 = (bf16[48,4096]{1,0:T(8,128)(2,1)S(1)}, bf16[48,4096]{1,0:T(8,128)(2,1)S(1)}, u32[]{:S(2)}, u32[]{:S(2)}) collective-permute-start(bf16[48,4096]{1,0:T(8,128)(2,1)S(1)} %get-tuple-element.36), channel_id=1, source_target_pairs={{0,6},{2,4},{4,2},{6,0},{1,7},{3,5},{5,3},{7,1},{8,14},{10,12},{12... | collective-permute-start | bytes 1179656 | tf_op jit(solution)/shard_map/ppermute | solution.py:194
  83.5 9.2 %collective-permute-start.25 = (bf16[48,4096]{1,0:T(8,128)(2,1)S(1)}, bf16[48,4096]{1,0:T(8,128)(2,1)S(1)}, u32[]{:S(2)}, u32[]{:S(2)}) collective-permute-start(bf16[48,4096]{1,0:T(8,128)(2,1)S(1)} %get-tuple-element.44), channel_id=1, source_target_pairs={{0,1},{1,0},{2,3},{3,2},{4,5},{5,4},{6,7},{7,6},{8,9},{9,8},{10,11... | collective-permute-start | bytes 1179656 | tf_op jit(solution)/shard_map/ppermute | solution.py:275
  84.6 10.0 %collective-permute-start.27 = (bf16[48,4096]{1,0:T(8,128)(2,1)S(1)}, bf16[48,4096]{1,0:T(8,128)(2,1)S(1)}, u32[]{:S(2)}, u32[]{:S(2)}) collective-permute-start(bf16[48,4096]{1,0:T(8,128)(2,1)S(1)} %get-tuple-element.46.refs_21_), channel_id=1, source_target_pairs={{0,1},{1,0},{2,3},{3,2},{4,5},{5,4},{6,7},{7,6},{8,9},{9,8},{10,11... | collective-permute-start | bytes 1179656 | tf_op jit(solution)/shard_map/ppermute | solution.py:251
  90.9 3.8 %collective-permute-start.26 = (bf16[48,4096]{1,0:T(8,128)(2,1)S(1)}, bf16[48,4096]{1,0:T(8,128)(2,1)S(1)}, u32[]{:S(2)}, u32[]{:S(2)}) collective-permute-start(bf16[48,4096]{1,0:T(8,128)(2,1)S(1)} %collective-permute-done.19.refs_20_), channel_id=1, source_target_pairs={{0,1},{1,0},{2,3},{3,2},{4,5},{5,4},{6,7},{7,6},{8,9},{9,8},{10,11... | collective-permute-start | bytes 1179656 | tf_op jit(solution)/shard_map/ppermute | solution.py:251
  92.6 1.9 %collective-permute-start.24 = (bf16[48,4096]{1,0:T(8,128)(2,1)S(1)}, bf16[48,4096]{1,0:T(8,128)(2,1)S(1)}, u32[]{:S(2)}, u32[]{:S(2)}) collective-permute-start(bf16[48,4096]{1,0:T(8,128)(2,1)S(1)} %get-tuple-element.42), channel_id=1, source_target_pairs={{0,1},{1,0},{2,3},{3,2},{4,5},{5,4},{6,7},{7,6},{8,9},{9,8},{10,11... | collective-permute-start | bytes 1179656 | tf_op jit(solution)/shard_map/ppermute | solution.py:275
  98.6 3.8 %collective-permute-start.31 = (bf16[48,4096]{1,0:T(8,128)(2,1)S(1)}, bf16[48,4096]{1,0:T(8,128)(2,1)S(1)}, u32[]{:S(2)}, u32[]{:S(2)}) collective-permute-start(bf16[48,4096]{1,0:T(8,128)(2,1)S(1)} %get-tuple-element.50), channel_id=1, source_target_pairs={{0,1},{1,0},{2,3},{3,2},{4,5},{5,4},{6,7},{7,6},{8,9},{9,8},{10,11... | collective-permute-start | bytes 1179656 | tf_op jit(solution)/shard_map/ppermute | solution.py:275
  99.0 17.0 %collective-permute-start.30 = (bf16[48,4096]{1,0:T(8,128)(2,1)S(1)}, bf16[48,4096]{1,0:T(8,128)(2,1)S(1)}, u32[]{:S(2)}, u32[]{:S(2)}) collective-permute-start(bf16[48,4096]{1,0:T(8,128)(2,1)S(1)} %add_convert_fusion.3), channel_id=1, source_target_pairs={{0,4},{2,6},{4,0},{6,2},{1,5},{3,7},{5,1},{7,3},{8,12},{10,14},{12... | collective-permute-start | bytes 1179656 | tf_op jit(solution)/shard_map/ppermute | solution.py:194
  99.0 20.2 %collective-permute-start.29 = (bf16[48,4096]{1,0:T(8,128)(2,1)S(1)}, bf16[48,4096]{1,0:T(8,128)(2,1)S(1)}, u32[]{:S(2)}, u32[]{:S(2)}) collective-permute-start(bf16[48,4096]{1,0:T(8,128)(2,1)S(1)} %add_convert_fusion.2), channel_id=1, source_target_pairs={{0,2},{2,0},{4,6},{6,4},{1,3},{3,1},{5,7},{7,5},{8,10},{10,8},{12,... | collective-permute-start | bytes 1179656 | tf_op jit(solution)/shard_map/ppermute | solution.py:194
  101.7 15.9 %collective-permute-start.28 = (bf16[48,4096]{1,0:T(8,128)(2,1)S(1)}, bf16[48,4096]{1,0:T(8,128)(2,1)S(1)}, u32[]{:S(2)}, u32[]{:S(2)}) collective-permute-start(bf16[48,4096]{1,0:T(8,128)(2,1)S(1)} %get-tuple-element.48), channel_id=1, source_target_pairs={{0,1},{1,0},{2,3},{3,2},{4,5},{5,4},{6,7},{7,6},{8,9},{9,8},{10,11... | collective-permute-start | bytes 1179656 | tf_op jit(solution)/shard_map/ppermute | solution.py:275
  116.0 18.5 %collective-permute-start.32 = (bf16[48,4096]{1,0:T(8,128)(2,1)S(1)}, bf16[48,4096]{1,0:T(8,128)(2,1)S(1)}, u32[]{:S(2)}, u32[]{:S(2)}) collective-permute-start(bf16[48,4096]{1,0:T(8,128)(2,1)S(1)} %add_convert_fusion), channel_id=1, source_target_pairs={{0,6},{2,4},{4,2},{6,0},{1,7},{3,5},{5,3},{7,1},{8,14},{10,12},{12... | collective-permute-start | bytes 1179656 | tf_op jit(solution)/shard_map/ppermute | solution.py:194
  117.7 18.4 %collective-permute-start.33 = (bf16[48,4096]{1,0:T(8,128)(2,1)S(1)}, bf16[48,4096]{1,0:T(8,128)(2,1)S(1)}, u32[]{:S(2)}, u32[]{:S(2)}) collective-permute-start(bf16[48,4096]{1,0:T(8,128)(2,1)S(1)} %add_convert_fusion.1.refs_0_), channel_id=1, source_target_pairs={{0,1},{1,0},{2,3},{3,2},{4,5},{5,4},{6,7},{7,6},{8,9},{9,8},{10,11... | collective-permute-start | bytes 1179656 | tf_op jit(solution)/shard_map/ppermute | solution.py:283
  118.7 17.3 %collective-permute-start.35 = (bf16[48,4096]{1,0:T(8,128)(2,1)S(1)}, bf16[48,4096]{1,0:T(8,128)(2,1)S(1)}, u32[]{:S(2)}, u32[]{:S(2)}) collective-permute-start(bf16[48,4096]{1,0:T(8,128)(2,1)S(1)} %collective-permute-done.30.refs_2_), channel_id=1, source_target_pairs={{0,1},{1,0},{2,3},{3,2},{4,5},{5,4},{6,7},{7,6},{8,9},{9,8},{10,11... | collective-permute-start | bytes 1179656 | tf_op jit(solution)/shard_map/ppermute | solution.py:283
  119.2 16.8 %collective-permute-start.34 = (bf16[48,4096]{1,0:T(8,128)(2,1)S(1)}, bf16[48,4096]{1,0:T(8,128)(2,1)S(1)}, u32[]{:S(2)}, u32[]{:S(2)}) collective-permute-start(bf16[48,4096]{1,0:T(8,128)(2,1)S(1)} %collective-permute-done.29.refs_1_), channel_id=1, source_target_pairs={{0,1},{1,0},{2,3},{3,2},{4,5},{5,4},{6,7},{7,6},{8,9},{9,8},{10,11... | collective-permute-start | bytes 1179656 | tf_op jit(solution)/shard_map/ppermute | solution.py:283
  134.5 2.9 %collective-permute-start.36 = (bf16[48,4096]{1,0:T(8,128)(2,1)S(1)}, bf16[48,4096]{1,0:T(8,128)(2,1)S(1)}, u32[]{:S(2)}, u32[]{:S(2)}) collective-permute-start(bf16[48,4096]{1,0:T(8,128)(2,1)S(1)} %collective-permute-done.32.refs_3_), channel_id=1, source_target_pairs={{0,1},{1,0},{2,3},{3,2},{4,5},{5,4},{6,7},{7,6},{8,9},{9,8},{10,11... | collective-permute-start | bytes 1179656 | tf_op jit(solution)/shard_map/ppermute | solution.py:283

commit v3 on v2

--- a/solution.py
+++ b/solution.py
@@ -20,7 +20,8 @@
 
 
 def select_kernel(n_experts, halves, shards, cluster_hbm, gate_hbm, up_hbm, down_hbm, *refs):
-    out_refs, scratch, sems = refs[:n_experts], refs[n_experts:-1], refs[-1]
+    out_refs, scratch = refs[:n_experts], refs[n_experts:-3]
+    chosen_ref, sems, out_sems = refs[-3:]
     sources = (cluster_hbm, gate_hbm, up_hbm, down_hbm)
     copies = [pltpu.make_async_copy(a, b, sems.at[i]) for i, (a, b) in enumerate(zip(sources, scratch))]
     for copy in copies:
@@ -48,11 +49,16 @@
     neuron = lax.broadcasted_iota(jnp.int32, (rows, wide), 0)
     table = jnp.where(neuron == local, 1.0, 0.0).astype(BF16)
     per = halves * run
+    sent = []
     for w, ref in enumerate(weight_refs):
         copies[w + 1].wait()
-        chosen = lax.dot_general(table, ref[...], FIRST, preferred_element_type=F32).astype(BF16)
+        chosen_ref[w] = lax.dot_general(table, ref[...], FIRST, preferred_element_type=F32).astype(BF16)
         for k in range(n_experts):
-            out_refs[k][w * per:(w + 1) * per, :] = chosen[k * per:(k + 1) * per]
+            part, place = chosen_ref.at[w, pl.ds(k * per, per)], out_refs[k].at[pl.ds(w * per, per)]
+            sent.append(pltpu.make_async_copy(part, place, out_sems.at[w, k]))
+            sent[-1].start()
+    for copy in sent:
+        copy.wait()
 
 
 def slot_table(routes, n_experts, capacity):
@@ -85,30 +91,34 @@
     pl.when(core != 0)(lambda: send(cotangent_ref))
 
 
-def merge_kernel(n_experts, capacity, routes_ref, *refs):
+def merge_kernel(order, capacity, blocks, *refs):
+    n_experts = len(order)
     mine_refs, other_refs = refs[:n_experts], refs[n_experts:2 * n_experts]
-    out_ref, grad_ref, table_ref = refs[2 * n_experts:]
-
-    @pl.when(pl.program_id(0) == 0)
-    def _():
-        table_ref[...] = slot_table(routes_ref[...], n_experts, capacity)
-
-    def home(parts):
-        rows = jnp.concatenate([part[...] for part in parts], axis=0)
-        return lax.dot_general(table_ref[...], rows, FIRST, preferred_element_type=F32).astype(BF16)
-
-    def both(first, second):
-        out_ref[...] = home(first)
-        grad_ref[...] = home(second)
-
-    core = lax.axis_index("tensor")
-    pl.when(core == 0)(lambda: both(mine_refs, other_refs))
-    pl.when(core != 0)(lambda: both(other_refs, mine_refs))
-
-
-def expert_kernel(n_experts, n_dp, n_rows, *refs):
+    routes_ref, out_ref, grad_ref, held_ref, sems = refs[2 * n_experts:]
+    table = slot_table(routes_ref[...], n_experts, capacity)
+    width = out_ref.shape[1] // blocks
+    first = lax.axis_index("tensor") == 0
+    copies = []
+    for i in range(blocks):
+        at = pl.ds(i * width, width)
+
+        def rows(refs):
+            return jnp.concatenate([refs[order.index(k)][:, at] for k in range(n_experts)], axis=0)
+
+        mine, other = rows(mine_refs), rows(other_refs)
+        for w, (a, b, ref) in enumerate(((mine, other, out_ref), (other, mine, grad_ref))):
+            total = lax.dot_general(table, jnp.where(first, a, b), FIRST, preferred_element_type=F32)
+            held_ref[w, :, at] = total.astype(BF16)
+            copies.append(pltpu.make_async_copy(held_ref.at[w, :, at], ref.at[:, at], sems.at[w, i]))
+            copies[-1].start()
+    for copy in copies:
+        copy.wait()
+
+
+def expert_kernel(n_parts, n_dp, n_rows, *refs):
     refs = list(refs)
-    weights = [[refs.pop(0) for _ in range(n_dp + 1)] for _ in range(n_experts)]
+    n_experts = len(n_parts)
+    weights = [[refs.pop(0) for _ in range(count)] for count in n_parts]
     mine_refs = [refs.pop(0) for _ in range(n_rows)]
     other_refs = [refs.pop(0) for _ in range(n_rows)]
     keep_refs = [refs.pop(0) for _ in range(n_rows)]
@@ -126,7 +136,7 @@
         parts = []
         lower, upper = w * per, (w + 1) * per
         for k in range(n_experts):
-            if j < n_dp - 1:
+            if j < n_dp - 1 or n_parts[k] == n_dp:
                 parts.append(weights[k][j][lower:upper, :])
                 continue
             if lower < cut:
@@ -182,47 +192,17 @@
         functools.partial(select_kernel, n_experts, halves, shards),
         out_shape=[shape((3 * per, width_part), BF16)] * n_experts,
         in_specs=[pl.BlockSpec(memory_space=pltpu.HBM)] * 4,
-        out_specs=[vmem] * n_experts,
+        out_specs=[pl.BlockSpec(memory_space=pltpu.HBM)] * n_experts,
         scratch_shapes=[pltpu.VMEM(cluster.shape, jnp.int32)]
         + [pltpu.VMEM(w_gate.shape, BF16)] * 3
-        + [pltpu.SemaphoreType.DMA((4,))],
+        + [
+            pltpu.VMEM((3, n_experts * per, width_part), BF16),
+            pltpu.SemaphoreType.DMA((4,)),
+            pltpu.SemaphoreType.DMA((3, n_experts)),
+        ],
         compiler_params=pltpu.CompilerParams(vmem_limit_bytes=MOST_VMEM),
         name="select_rows",
     )(cluster, w_gate, w_up, w_down)
-
-    def planes(chunk, k):
-        return lax.ppermute(chunk, "expert", flips(n_experts, k))
-
-    weights = [None] * n_experts
-    arrived = {}
-    near_far = {}
-
-    def over_dp(k, awaited):
-        (chunk,) = after([arrived[k]], [awaited])
-        near_far[k] = (
-            lax.ppermute(chunk, "dp", flips(n_dp, 1)),
-            lax.ppermute(chunk, "dp", flips(n_dp, 2)),
-        )
-
-    def over_dp_far(k):
-        near, far = near_far[k]
-        cut = near.shape[0] // 2
-        low = lax.ppermute(near[:cut], "dp", flips(n_dp, 2))
-        high = lax.ppermute(far[cut:], "dp", flips(n_dp, 1))
-        weights[k] = [arrived[k], near, far, low, high]
-
-    arrived[0] = sent_w[0]
-    arrived[3] = planes(sent_w[3], 3)
-    arrived[1] = planes(sent_w[1], 1)
-    over_dp(0, [])
-    over_dp_far(0)
-    arrived[2] = planes(after([sent_w[2]], [arrived[1]])[0], 2)
-    over_dp(1, near_far[0])
-    over_dp_far(1)
-    over_dp(3, (near_far[1], weights[0][3:]))
-    over_dp_far(3)
-    over_dp(2, (near_far[3], weights[1][3:]))
-    over_dp_far(2)
 
     route_row = routes.reshape(1, tok_count)
     block = width // 4
@@ -242,58 +222,98 @@
     )(route_row, tokens, cotangent)
 
     swap = flips(halves, 1)
-    rows = {0: sent[0]}
-    early = after([sent[2], sent[1]], [arrived[3], arrived[1]])
-    rows[2] = planes(early[0], 2)
-    rows[1] = planes(early[1], 1)
-    (late,) = after([sent[3]], [arrived[2]])
-    rows[3] = planes(late, 3)
-    others = {k: lax.ppermute(rows[k], "tensor", swap) for k in (0, 2, 1, 3)}
-
+
+    def planes(chunk, k):
+        return lax.ppermute(chunk, "expert", flips(n_experts, k))
+
+    def spread(chunk, step):
+        return lax.ppermute(chunk, "dp", flips(n_dp, step))
+
+    def swapped(chunk):
+        return lax.ppermute(chunk, "tensor", swap)
+
+    def direct(chunk):
+        return [chunk, spread(chunk, 1), spread(chunk, 2), spread(chunk, 3)]
+
+    def near_far(chunk):
+        return [chunk, spread(chunk, 1), spread(chunk, 2)]
+
+    def diagonal(pieces):
+        cut = pieces[0].shape[0] // 2
+        return [spread(pieces[1][:cut], 2), spread(pieces[2][cut:], 1)]
+
+    weights = [None] * n_experts
+    rows, others = {0: sent[0]}, {}
+    chunk3 = planes(sent_w[3], 3)
+    chunk1 = planes(sent_w[1], 1)
+    (sent_w2,) = after([sent_w[2]], [chunk3])
+    chunk2 = planes(sent_w2, 2)
+    weights[0] = direct(sent_w[0])
+    (chunk3,) = after([chunk3], weights[0][1:3])
+    pieces3 = near_far(chunk3)
+    (chunk1,) = after([chunk1], weights[0][1:])
+    pieces1 = near_far(chunk1)
+    others[0] = swapped(rows[0])
+    (sent_2, sent_1) = after([sent[2], sent[1]], [chunk2, others[0]])
+    rows[2] = planes(sent_2, 2)
+    rows[1] = planes(sent_1, 1)
+    (chunk2,) = after([chunk2], pieces3[1:] + pieces1[1:])
+    pieces2 = near_far(chunk2)
+    weights[3] = pieces3 + [spread(pieces3[2], 1)]
+    weights[1] = pieces1 + [spread(pieces1[1], 2)]
+    held2 = after(pieces2[1:], [weights[1][3], weights[3][3]])
+    weights[2] = pieces2 + diagonal([chunk2, *held2])
+    (sent_3,) = after([sent[3]], [rows[2]])
+    rows[3] = planes(sent_3, 3)
+    for k in (2, 1, 3):
+        others[k] = swapped(rows[k])
+
+    chunk_order = (2, 3, 1, 0)
     mine, other = {}, {}
     returned = []
     for members in ((2, 1), (3, 0)):
         count = len(members)
         here = {k: rows[k] for k in members}
         if returned:
-            here[members[0]] = after([rows[members[0]]], returned)[0]
+            (here[3],) = after([rows[3]], returned)
         results = pl.pallas_call(
-            functools.partial(expert_kernel, n_experts, n_dp, count),
+            functools.partial(expert_kernel, [len(weights[k]) for k in chunk_order], n_dp, count),
             out_shape=[shape((capacity, width), BF16)] * (2 * count),
-            in_specs=[vmem] * (n_experts * (n_dp + 1) + 2 * count),
+            in_specs=[vmem] * (sum(len(parts) for parts in weights) + 2 * count),
             out_specs=[vmem] * (2 * count),
             compiler_params=params,
-            cost_estimate=pl.CostEstimate(flops=1000, bytes_accessed=1000, transcendentals=0),
             name="expert_math",
         )(
-            *[part for parts in weights for part in parts],
+            *[part for k in chunk_order for part in weights[k]],
             *[here[k] for k in members],
             *[others[k] for k in members],
         )
         for i, k in enumerate(members):
             kept, given = results[i], results[count + i]
-            got = lax.ppermute(given, "tensor", swap)
+            got = swapped(given)
             total = (kept.astype(F32) + got.astype(F32)).astype(BF16)
             returned.append(total)
-            if k == 3:
-                (total,) = after([total], [mine[2]])
-            if k:
-                total = planes(total, k)
-            mine[k] = total
-            other[k] = lax.ppermute(total, "tensor", swap)
-
+            mine[k] = planes(total, k) if k else total
+    other[0] = swapped(mine[0])
+    other[2] = swapped(mine[2])
+    other[1] = swapped(after([mine[1]], [other[2]])[0])
+    other[3] = swapped(after([mine[3]], [other[1]])[0])
+
+    home_order = (2, 1, 0, 3)
+    blocks = 8
     return tuple(
         pl.pallas_call(
-            functools.partial(merge_kernel, n_experts, capacity),
-            grid=(width // block,),
+            functools.partial(merge_kernel, home_order, capacity, blocks),
             out_shape=[shape((tok_count, width), BF16)] * 2,
-            in_specs=[pl.BlockSpec((1, tok_count), lambda i: (0, 0))]
-            + [pl.BlockSpec((capacity, block), lambda i: (0, i))] * (2 * n_experts),
-            out_specs=[pl.BlockSpec((tok_count, block), lambda i: (0, i))] * 2,
-            scratch_shapes=[pltpu.VMEM((n_experts * capacity, tok_count), BF16)],
+            in_specs=[vmem] * (2 * n_experts + 1),
+            out_specs=[pl.BlockSpec(memory_space=pltpu.HBM)] * 2,
+            scratch_shapes=[
+                pltpu.VMEM((2, tok_count, width), BF16),
+                pltpu.SemaphoreType.DMA((2, blocks)),
+            ],
             compiler_params=params,
             name="merge_rows",
-        )(route_row, *[mine[k] for k in range(n_experts)], *[other[k] for k in range(n_experts)])
+        )(*[mine[k] for k in home_order], *[other[k] for k in home_order], route_row)
     )
 
 

time: 141 us -> 127 us (0.901)
  waiting for transfers between devices: 84.7 us -> 76.1 us
  starting transfers between devices: 38.9 us -> 34.6 us
  Pallas kernels: 15.6 us -> 14.1 us
    ppermute x28 -> x25, waiting for transfers between devices: 20.6 us -> 7.54 us  [the longest x13 5.04 us: spread(): return lax.ppermute(chunk, 'dp', flips(n_dp, step))]
    ppermute x9, starting transfers between devices: 17 us -> 8.02 us  [planes(): return lax.ppermute(chunk, 'expert', flips(n_experts, k))]
    ppermute x28 -> x25, starting transfers between devices: 21.8 us -> 26.6 us  [the longest x13 14.3 us: spread(): return lax.ppermute(chunk, 'dp', flips(n_dp, step))]
    ppermute x9, waiting for transfers between devices: 64 us -> 68.6 us  [planes(): return lax.ppermute(chunk, 'expert', flips(n_experts, k))]
  transfers between devices with their start and end apart: 37 -> 34, of which waited for: 16 -> 13; matrix products, arithmetic and copies ran while one was open for 0% -> 0% of each run, Pallas kernels for 4% -> 7%
where the time goes in v3:
time: 127 us
  waiting for transfers between devices  76.1 us (60%)
  starting transfers between devices  34.6 us (27%)
  Pallas kernels  14.1 us (11%)
  local copies, waits for them, and re-layouts  1.27 us (1%)
    ppermute x9, waiting for transfers between devices, planes(): return lax.ppermute(chunk, 'expert', flips(n_experts, k))  68.6 us
    ppermute x13, starting transfers between devices, spread(): return lax.ppermute(chunk, 'dp', flips(n_dp, step))  14.3 us
    ppermute x12, starting transfers between devices, swapped(): return lax.ppermute(chunk, 'tensor', swap)  12.4 us
    ppermute x9, starting transfers between devices, planes(): return lax.ppermute(chunk, 'expert', flips(n_experts, k))  8.02 us
    pallas_call x2, Pallas kernels, aligned_plan(): pl.pallas_call(functools.partial(expert_kernel, [len(weights[k]) for k in...  7.76 us
    ppermute x13, waiting for transfers between devices, spread(): return lax.ppermute(chunk, 'dp', flips(n_dp, step))  5.04 us
    pallas_call x1, Pallas kernels, aligned_plan(): pl.pallas_call(functools.partial(select_kernel, n_experts, halves, shards...  2.98 us
  transfers between devices with their start and end apart: 34, of which 13 were waited for; matrix products, arithmetic and copies ran while one was open for 0% of the time, Pallas kernels for 7%

profile of v3, /device:TPU:9, one launch (start us, length us, event | category | flops | bytes accessed | tf_op | source)
XLA Modules:
  0.0 127.3 jit_solution(16322593469775261935)
XLA Ops:
  0.6 3.0 %select_rows.1 = (bf16[192,1024]{1,0:T(8,128)(2,1)}, bf16[192,1024]{1,0:T(8,128)(2,1)}, bf16[192,1024]{1,0:T(8,128)(2,1)}, bf16[192,1024]{1,0:T(8,128)(2,1)}) custom-call(s32[4,512]{1,0:T(4,128)} %cluster_hbm.1, bf16[231,1024]{1,0:T(8,128)(2,1)} %gate_hbm.1, bf16[231,1024]{1,0:T(8,128)(2,1)} %up_hbm.1, bf16[231,1024]{1,0:T(8,128)(2,1)} %down_hbm.1), custom_call_target="tpu_custom_call" | custom-call | tf_op jit(solution)/shard_map/select_rows/pallas_call | solution.py:191
  3.6 1.4 %collective-permute-start = (bf16[192,1024]{1,0:T(8,128)(2,1)}, bf16[192,1024]{1,0:T(8,128)(2,1)S(1)}, u32[]{:S(2)}, u32[]{:S(2)}) collective-permute-start(bf16[192,1024]{1,0:T(8,128)(2,1)} %get-tuple-element.31), channel_id=1, source_target_pairs={{0,6},{2,4},{4,2},{6,0},{1,7},{3,5},{5,3},{7,1},{8,14},{10,12},{12... | collective-permute-start | bytes 1179656 | tf_op jit(solution)/shard_map/ppermute | solution.py:227
  5.0 1.2 collective-permute-start.2
  6.2 1.2 collective-permute-start.3
  7.4 2.2 %collective-permute-start.6 = (bf16[192,1024]{1,0:T(8,128)(2,1)}, bf16[192,1024]{1,0:T(8,128)(2,1)S(1)}, u32[]{:S(2)}, u32[]{:S(2)}) collective-permute-start(bf16[192,1024]{1,0:T(8,128)(2,1)} %get-tuple-element.35), channel_id=1, source_target_pairs={{0,2},{2,0},{4,6},{6,4},{1,3},{3,1},{5,7},{7,5},{8,10},{10,8},{12,... | collective-permute-start | bytes 1179656 | tf_op jit(solution)/shard_map/ppermute | solution.py:227
  9.6 0.2 collective-permute-start.7
  9.8 12.7 %collective-permute-done.refs_5_ = bf16[192,1024]{1,0:T(8,128)(2,1)S(1)} collective-permute-done((bf16[192,1024]{1,0:T(8,128)(2,1)}, bf16[192,1024]{1,0:T(8,128)(2,1)S(1)}, u32[]{:S(2)}, u32[]{:S(2)}) %collective-permute-start) | collective-permute-done | bytes 393248 | tf_op jit(solution)/shard_map/ppermute | solution.py:227
  22.5 1.3 collective-permute-start.4
  23.8 1.2 collective-permute-start.5
  25.0 0.6 collective-permute-start.8
  25.6 1.2 collective-permute-start.9
  26.9 1.2 copy-done.2
  28.1 1.5 %dispatch_rows.1 = (bf16[48,4096]{1,0:T(8,128)(2,1)S(1)}, bf16[48,4096]{1,0:T(8,128)(2,1)S(1)}, bf16[48,4096]{1,0:T(8,128)(2,1)S(1)}, bf16[48,4096]{1,0:T(8,128)(2,1)S(1)}) custom-call(s32[1,128]{1,0:T(1,128)S(1)} %bitcast.1, bf16[128,4096]{1,0:T(8,128)(2,1)S(1)} %copy-done.1, bf16[128,4096]{1,0:T(8,128)(2,1)S(1)} %copy-done.2), custom_call_target="tpu_custom_call" | custom-call | tf_op jit(solution)/shard_map/dispatch_rows/pallas_call | solution.py:209
  29.6 9.0 %collective-permute-done.1.refs_0_ = bf16[192,1024]{1,0:T(8,128)(2,1)S(1)} collective-permute-done((bf16[192,1024]{1,0:T(8,128)(2,1)}, bf16[192,1024]{1,0:T(8,128)(2,1)S(1)}, u32[]{:S(2)}, u32[]{:S(2)}) %collective-permute-start.1) | collective-permute-done | bytes 393248 | tf_op jit(solution)/shard_map/ppermute | solution.py:227
  38.7 2.0 %collective-permute-start.16 = (bf16[48,4096]{1,0:T(8,128)(2,1)S(1)}, bf16[48,4096]{1,0:T(8,128)(2,1)S(1)}, u32[]{:S(2)}, u32[]{:S(2)}) collective-permute-start(bf16[48,4096]{1,0:T(8,128)(2,1)S(1)} %get-tuple-element.42.refs_18_), channel_id=1, source_target_pairs={{0,1},{1,0},{2,3},{3,2},{4,5},{5,4},{6,7},{7,6},{8,9},{9,8},{10,11... | collective-permute-start | bytes 1179656 | tf_op jit(solution)/shard_map/ppermute | solution.py:233
  40.6 1.3 collective-permute-start.10
  42.0 3.0 %collective-permute-start.17 = (bf16[48,4096]{1,0:T(8,128)(2,1)S(1)}, bf16[48,4096]{1,0:T(8,128)(2,1)S(1)}, u32[]{:S(2)}, u32[]{:S(2)}) collective-permute-start(bf16[48,4096]{1,0:T(8,128)(2,1)S(1)} %get-tuple-element.43), channel_id=1, source_target_pairs={{0,4},{2,6},{4,0},{6,2},{1,5},{3,7},{5,1},{7,3},{8,12},{10,14},{12... | collective-permute-start | bytes 1179656 | tf_op jit(solution)/shard_map/ppermute | solution.py:227
  45.0 1.2 collective-permute-start.11
  46.2 0.2 collective-permute-start.12
  46.4 1.8 %collective-permute-done.10.refs_1_ = bf16[192,1024]{1,0:T(8,128)(2,1)S(1)} collective-permute-done((bf16[192,1024]{1,0:T(8,128)(2,1)S(1)}, bf16[192,1024]{1,0:T(8,128)(2,1)S(1)}, u32[]{:S(2)}, u32[]{:S(2)}) %collective-permute-start.10) | collective-permute-done | bytes 393248 | tf_op jit(solution)/shard_map/ppermute | solution.py:230
  48.3 2.0 %collective-permute-start.13 = (bf16[192,1024]{1,0:T(8,128)(2,1)S(1)}, bf16[192,1024]{1,0:T(8,128)(2,1)S(1)}, u32[]{:S(2)}, u32[]{:S(2)}) collective-permute-start(bf16[192,1024]{1,0:T(8,128)(2,1)S(1)} %collective-permute-done.5.refs_7_), channel_id=1, source_target_pairs={{0,8},{8,0},{16,24},{24,16},{1,9},{9,1},{17,25},{25,17},{2,10},{10... | collective-permute-start | bytes 1179656 | tf_op jit(solution)/shard_map/ppermute | solution.py:230
  50.3 11.6 %collective-permute-done.17.refs_17_ = bf16[48,4096]{1,0:T(8,128)(2,1)S(1)} collective-permute-done((bf16[48,4096]{1,0:T(8,128)(2,1)S(1)}, bf16[48,4096]{1,0:T(8,128)(2,1)S(1)}, u32[]{:S(2)}, u32[]{:S(2)}) %collective-permute-start.17) | collective-permute-done | bytes 393248 | tf_op jit(solution)/shard_map/ppermute | solution.py:227
  61.9 0.5 collective-permute-start.19
  62.4 1.0 collective-permute-start.20
  63.4 1.3 %collective-permute-start.14 = (bf16[96,1024]{1,0:T(8,128)(2,1)S(1)}, bf16[96,1024]{1,0:T(8,128)(2,1)S(1)}, u32[]{:S(2)}, u32[]{:S(2)}) collective-permute-start(bf16[96,1024]{1,0:T(8,128)(2,1)S(1)} %slice.6), channel_id=1, source_target_pairs={{0,16},{8,24},{16,0},{24,8},{1,17},{9,25},{17,1},{25,9},{2,18},{10... | collective-permute-start | bytes 589832 | tf_op jit(solution)/shard_map/ppermute | solution.py:230
  64.7 1.3 %collective-permute-start.15 = (bf16[96,1024]{1,0:T(8,128)(2,1)S(1)}, bf16[96,1024]{1,0:T(8,128)(2,1)S(1)}, u32[]{:S(2)}, u32[]{:S(2)}) collective-permute-start(bf16[96,1024]{1,0:T(8,128)(2,1)S(1)} %slice.7), channel_id=1, source_target_pairs={{0,8},{8,0},{16,24},{24,16},{1,9},{9,1},{17,25},{25,17},{2,10},{10... | collective-permute-start | bytes 589832 | tf_op jit(solution)/shard_map/ppermute | solution.py:230
  66.0 0.4 collective-permute-start.25
  66.5 1.9 %collective-permute-done.14.refs_3_ = bf16[96,1024]{1,0:T(8,128)(2,1)S(1)} collective-permute-done((bf16[96,1024]{1,0:T(8,128)(2,1)S(1)}, bf16[96,1024]{1,0:T(8,128)(2,1)S(1)}, u32[]{:S(2)}, u32[]{:S(2)}) %collective-permute-start.14) | collective-permute-done | bytes 196640 | tf_op jit(solution)/shard_map/ppermute | solution.py:230
  68.3 1.3 %collective-permute-done.15.refs_4_ = bf16[96,1024]{1,0:T(8,128)(2,1)S(1)} collective-permute-done((bf16[96,1024]{1,0:T(8,128)(2,1)S(1)}, bf16[96,1024]{1,0:T(8,128)(2,1)S(1)}, u32[]{:S(2)}, u32[]{:S(2)}) %collective-permute-start.15) | collective-permute-done | bytes 196640 | tf_op jit(solution)/shard_map/ppermute | solution.py:230
  69.6 3.9 %expert_math.2 = (bf16[48,4096]{1,0:T(8,128)(2,1)S(1)}, bf16[48,4096]{1,0:T(8,128)(2,1)S(1)}, bf16[48,4096]{1,0:T(8,128)(2,1)S(1)}, bf16[48,4096]{1,0:T(8,128)(2,1)S(1)}) custom-call(bf16[192,1024]{1,0:T(8,128)(2,1)S(1)} %collective-permute-done.1.refs_0_, bf16[192,1024]{1,0:T(8,128)(2,1)S(1)} %collective-permute-done.10.refs_1_, ...), custom_call_target="tpu_custom_call" | custom-call | tf_op jit(solution)/shard_map/expert_math/pallas_call | solution.py:279
  73.5 2.7 %collective-permute-start.21 = (bf16[48,4096]{1,0:T(8,128)(2,1)S(1)}, bf16[48,4096]{1,0:T(8,128)(2,1)S(1)}, u32[]{:S(2)}, u32[]{:S(2)}) collective-permute-start(bf16[48,4096]{1,0:T(8,128)(2,1)S(1)} %get-tuple-element.46), channel_id=1, source_target_pairs={{0,1},{1,0},{2,3},{3,2},{4,5},{5,4},{6,7},{7,6},{8,9},{9,8},{10,11... | collective-permute-start | bytes 1179656 | tf_op jit(solution)/shard_map/ppermute | solution.py:233
  76.3 7.0 %collective-permute-done.25.refs_17_ = bf16[48,4096]{1,0:T(8,128)(2,1)S(1)} collective-permute-done((bf16[48,4096]{1,0:T(8,128)(2,1)S(1)}, bf16[48,4096]{1,0:T(8,128)(2,1)S(1)}, u32[]{:S(2)}, u32[]{:S(2)}) %collective-permute-start.25) | collective-permute-done | bytes 393248 | tf_op jit(solution)/shard_map/ppermute | solution.py:227
  83.3 2.7 %collective-permute-start.26 = (bf16[48,4096]{1,0:T(8,128)(2,1)S(1)}, bf16[48,4096]{1,0:T(8,128)(2,1)S(1)}, u32[]{:S(2)}, u32[]{:S(2)}) collective-permute-start(bf16[48,4096]{1,0:T(8,128)(2,1)S(1)} %collective-permute-done.25.refs_17_), channel_id=1, source_target_pairs={{0,1},{1,0},{2,3},{3,2},{4,5},{5,4},{6,7},{7,6},{8,9},{9,8},{10,11... | collective-permute-start | bytes 1179656 | tf_op jit(solution)/shard_map/ppermute | solution.py:233
  86.3 1.1 collective-permute-done.26.refs_19_
  87.3 3.9 %expert_math.3 = (bf16[48,4096]{1,0:T(8,128)(2,1)S(1)}, bf16[48,4096]{1,0:T(8,128)(2,1)S(1)}, bf16[48,4096]{1,0:T(8,128)(2,1)S(1)}, bf16[48,4096]{1,0:T(8,128)(2,1)S(1)}) custom-call(bf16[192,1024]{1,0:T(8,128)(2,1)S(1)} %collective-permute-done.1.refs_0_, bf16[192,1024]{1,0:T(8,128)(2,1)S(1)} %collective-permute-done.10.refs_1_, ...), custom_call_target="tpu_custom_call" | custom-call | tf_op jit(solution)/shard_map/expert_math/pallas_call | solution.py:279
  91.2 0.4 collective-permute-start.28
  91.7 0.5 collective-permute-start.24
  92.1 0.5 collective-permute-start.27
  92.6 10.7 %collective-permute-done.22.refs_0_ = bf16[48,4096]{1,0:T(8,128)(2,1)S(1)} collective-permute-done((bf16[48,4096]{1,0:T(8,128)(2,1)S(1)}, bf16[48,4096]{1,0:T(8,128)(2,1)S(1)}, u32[]{:S(2)}, u32[]{:S(2)}) %collective-permute-start.22) | collective-permute-done | bytes 393248 | tf_op jit(solution)/shard_map/ppermute | solution.py:227
  103.4 0.6 collective-permute-start.30
  104.0 0.1 add_convert_fusion
  104.1 0.5 collective-permute-start.29
  104.6 2.3 %collective-permute-done.24.refs_1_ = bf16[48,4096]{1,0:T(8,128)(2,1)S(1)} collective-permute-done((bf16[48,4096]{1,0:T(8,128)(2,1)S(1)}, bf16[48,4096]{1,0:T(8,128)(2,1)S(1)}, u32[]{:S(2)}, u32[]{:S(2)}) %collective-permute-start.24) | collective-permute-done | bytes 393248 | tf_op jit(solution)/shard_map/ppermute | solution.py:227
  106.8 1.0 collective-permute-start.31
  108.0 15.3 %collective-permute-done.29.refs_3_ = bf16[48,4096]{1,0:T(8,128)(2,1)S(1)} collective-permute-done((bf16[48,4096]{1,0:T(8,128)(2,1)S(1)}, bf16[48,4096]{1,0:T(8,128)(2,1)S(1)}, u32[]{:S(2)}, u32[]{:S(2)}) %collective-permute-start.29) | collective-permute-done | bytes 393248 | tf_op jit(solution)/shard_map/ppermute | solution.py:227
  123.3 0.8 collective-permute-start.33
  124.1 1.3 %collective-permute-done.33.refs_7_ = bf16[48,4096]{1,0:T(8,128)(2,1)S(1)} collective-permute-done((bf16[48,4096]{1,0:T(8,128)(2,1)S(1)}, bf16[48,4096]{1,0:T(8,128)(2,1)S(1)}, u32[]{:S(2)}, u32[]{:S(2)}) %collective-permute-start.33) | collective-permute-done | bytes 393248 | tf_op jit(solution)/shard_map/ppermute | solution.py:233
  125.4 1.9 %merge_rows.1 = (bf16[128,4096]{1,0:T(8,128)(2,1)}, bf16[128,4096]{1,0:T(8,128)(2,1)}) custom-call(bf16[48,4096]{1,0:T(8,128)(2,1)S(1)} %collective-permute-done.22.refs_0_, bf16[48,4096]{1,0:T(8,128)(2,1)S(1)} %collective-permute-done.24.refs_1_, bf16[48,4096]{1,0:T(8,128)(2,1)S(1)} %add_convert_fusion.1.refs_2_, ...), custom_call_target="tpu_custom_call" | custom-call | tf_op jit(solution)/shard_map/merge_rows/pallas_call | solution.py:305
  (39 shorter events, 0.7 us)
Async XLA Ops:
  0.6 26.3 %copy-start.1 = (bf16[128,4096]{1,0:T(8,128)(2,1)S(1)}, bf16[128,4096]{1,0:T(8,128)(2,1)}, u32[]{:S(2)}) copy-start(bf16[128,4096]{1,0:T(8,128)(2,1)} %tokens_ref.1) | copy-start | bytes 3145732
  3.6 18.9 %collective-permute-start = (bf16[192,1024]{1,0:T(8,128)(2,1)}, bf16[192,1024]{1,0:T(8,128)(2,1)S(1)}, u32[]{:S(2)}, u32[]{:S(2)}) collective-permute-start(bf16[192,1024]{1,0:T(8,128)(2,1)} %get-tuple-element.31), channel_id=1, source_target_pairs={{0,6},{2,4},{4,2},{6,0},{1,7},{3,5},{5,3},{7,1},{8,14},{10,12},{12... | collective-permute-start | bytes 1179656 | tf_op jit(solution)/shard_map/ppermute | solution.py:227
  5.0 17.5 %collective-permute-start.2 = (bf16[192,1024]{1,0:T(8,128)(2,1)}, bf16[192,1024]{1,0:T(8,128)(2,1)S(1)}, u32[]{:S(2)}, u32[]{:S(2)}) collective-permute-start(bf16[192,1024]{1,0:T(8,128)(2,1)} %get-tuple-element.33.refs_13_), channel_id=1, source_target_pairs={{0,8},{8,0},{16,24},{24,16},{1,9},{9,1},{17,25},{25,17},{2,10},{10... | collective-permute-start | bytes 1179656 | tf_op jit(solution)/shard_map/ppermute | solution.py:230
  6.2 16.3 %collective-permute-start.3 = (bf16[192,1024]{1,0:T(8,128)(2,1)}, bf16[192,1024]{1,0:T(8,128)(2,1)S(1)}, u32[]{:S(2)}, u32[]{:S(2)}) collective-permute-start(bf16[192,1024]{1,0:T(8,128)(2,1)} %get-tuple-element.33.refs_13_), channel_id=1, source_target_pairs={{0,16},{8,24},{16,0},{24,8},{1,17},{9,25},{17,1},{25,9},{2,18},{10... | collective-permute-start | bytes 1179656 | tf_op jit(solution)/shard_map/ppermute | solution.py:230
  7.4 17.6 %collective-permute-start.6 = (bf16[192,1024]{1,0:T(8,128)(2,1)}, bf16[192,1024]{1,0:T(8,128)(2,1)S(1)}, u32[]{:S(2)}, u32[]{:S(2)}) collective-permute-start(bf16[192,1024]{1,0:T(8,128)(2,1)} %get-tuple-element.35), channel_id=1, source_target_pairs={{0,2},{2,0},{4,6},{6,4},{1,3},{3,1},{5,7},{7,5},{8,10},{10,8},{12,... | collective-permute-start | bytes 1179656 | tf_op jit(solution)/shard_map/ppermute | solution.py:227
  9.6 15.4 %collective-permute-start.7 = (bf16[192,1024]{1,0:T(8,128)(2,1)}, bf16[192,1024]{1,0:T(8,128)(2,1)S(1)}, u32[]{:S(2)}, u32[]{:S(2)}) collective-permute-start(bf16[192,1024]{1,0:T(8,128)(2,1)} %get-tuple-element.33.refs_13_), channel_id=1, source_target_pairs={{0,24},{8,16},{16,8},{24,0},{1,25},{9,17},{17,9},{25,1},{2,26},{10... | collective-permute-start | bytes 1179656 | tf_op jit(solution)/shard_map/ppermute | solution.py:230
  22.5 4.4 %copy-start.3 = (s32[128,1]{0,1:T(1,128)S(1)}, s32[128,1]{0,1:T(1,128)}, u32[]{:S(2)}) copy-start(s32[128,1]{0,1:T(1,128)} %param.9) | copy-start | bytes 1540
  22.5 16.2 %collective-permute-start.1 = (bf16[192,1024]{1,0:T(8,128)(2,1)}, bf16[192,1024]{1,0:T(8,128)(2,1)S(1)}, u32[]{:S(2)}, u32[]{:S(2)}) collective-permute-start(bf16[192,1024]{1,0:T(8,128)(2,1)} %get-tuple-element.32), channel_id=1, source_target_pairs={{0,4},{2,6},{4,0},{6,2},{1,5},{3,7},{5,1},{7,3},{8,12},{10,14},{12... | collective-permute-start | bytes 1179656 | tf_op jit(solution)/shard_map/ppermute | solution.py:227
  22.5 18.1 %collective-permute-start.4 = (bf16[192,1024]{1,0:T(8,128)(2,1)S(1)}, bf16[192,1024]{1,0:T(8,128)(2,1)S(1)}, u32[]{:S(2)}, u32[]{:S(2)}) collective-permute-start(bf16[192,1024]{1,0:T(8,128)(2,1)S(1)} %collective-permute-done.refs_5_), channel_id=1, source_target_pairs={{0,8},{8,0},{16,24},{24,16},{1,9},{9,1},{17,25},{25,17},{2,10},{10... | collective-permute-start | bytes 1179656 | tf_op jit(solution)/shard_map/ppermute | solution.py:230
  23.8 16.8 %collective-permute-start.5 = (bf16[192,1024]{1,0:T(8,128)(2,1)S(1)}, bf16[192,1024]{1,0:T(8,128)(2,1)S(1)}, u32[]{:S(2)}, u32[]{:S(2)}) collective-permute-start(bf16[192,1024]{1,0:T(8,128)(2,1)S(1)} %collective-permute-done.refs_5_), channel_id=1, source_target_pairs={{0,16},{8,24},{16,0},{24,8},{1,17},{9,25},{17,1},{25,9},{2,18},{10... | collective-permute-start | bytes 1179656 | tf_op jit(solution)/shard_map/ppermute | solution.py:230
  25.0 15.6 %collective-permute-start.8 = (bf16[192,1024]{1,0:T(8,128)(2,1)S(1)}, bf16[192,1024]{1,0:T(8,128)(2,1)S(1)}, u32[]{:S(2)}, u32[]{:S(2)}) collective-permute-start(bf16[192,1024]{1,0:T(8,128)(2,1)S(1)} %collective-permute-done.6.refs_9_), channel_id=1, source_target_pairs={{0,8},{8,0},{16,24},{24,16},{1,9},{9,1},{17,25},{25,17},{2,10},{10... | collective-permute-start | bytes 1179656 | tf_op jit(solution)/shard_map/ppermute | solution.py:230
  25.6 15.0 %collective-permute-start.9 = (bf16[192,1024]{1,0:T(8,128)(2,1)S(1)}, bf16[192,1024]{1,0:T(8,128)(2,1)S(1)}, u32[]{:S(2)}, u32[]{:S(2)}) collective-permute-start(bf16[192,1024]{1,0:T(8,128)(2,1)S(1)} %collective-permute-done.6.refs_9_), channel_id=1, source_target_pairs={{0,16},{8,24},{16,0},{24,8},{1,17},{9,25},{17,1},{25,9},{2,18},{10... | collective-permute-start | bytes 1179656 | tf_op jit(solution)/shard_map/ppermute | solution.py:230
  26.9 1.2 copy-start.2
  38.7 3.3 %collective-permute-start.16 = (bf16[48,4096]{1,0:T(8,128)(2,1)S(1)}, bf16[48,4096]{1,0:T(8,128)(2,1)S(1)}, u32[]{:S(2)}, u32[]{:S(2)}) collective-permute-start(bf16[48,4096]{1,0:T(8,128)(2,1)S(1)} %get-tuple-element.42.refs_18_), channel_id=1, source_target_pairs={{0,1},{1,0},{2,3},{3,2},{4,5},{5,4},{6,7},{7,6},{8,9},{9,8},{10,11... | collective-permute-start | bytes 1179656 | tf_op jit(solution)/shard_map/ppermute | solution.py:233
  40.6 7.6 %collective-permute-start.10 = (bf16[192,1024]{1,0:T(8,128)(2,1)S(1)}, bf16[192,1024]{1,0:T(8,128)(2,1)S(1)}, u32[]{:S(2)}, u32[]{:S(2)}) collective-permute-start(bf16[192,1024]{1,0:T(8,128)(2,1)S(1)} %collective-permute-done.1.refs_0_), channel_id=1, source_target_pairs={{0,8},{8,0},{16,24},{24,16},{1,9},{9,1},{17,25},{25,17},{2,10},{10... | collective-permute-start | bytes 1179656 | tf_op jit(solution)/shard_map/ppermute | solution.py:230
  42.0 27.7 %copy-start = (bf16[192,1024]{1,0:T(8,128)(2,1)S(1)}, bf16[192,1024]{1,0:T(8,128)(2,1)}, u32[]{:S(2)}) copy-start(bf16[192,1024]{1,0:T(8,128)(2,1)} %get-tuple-element.33.refs_13_) | copy-start | bytes 1179652
  42.0 19.9 %collective-permute-start.17 = (bf16[48,4096]{1,0:T(8,128)(2,1)S(1)}, bf16[48,4096]{1,0:T(8,128)(2,1)S(1)}, u32[]{:S(2)}, u32[]{:S(2)}) collective-permute-start(bf16[48,4096]{1,0:T(8,128)(2,1)S(1)} %get-tuple-element.43), channel_id=1, source_target_pairs={{0,4},{2,6},{4,0},{6,2},{1,5},{3,7},{5,1},{7,3},{8,12},{10,14},{12... | collective-permute-start | bytes 1179656 | tf_op jit(solution)/shard_map/ppermute | solution.py:227
  45.0 17.4 %collective-permute-start.18 = (bf16[48,4096]{1,0:T(8,128)(2,1)S(1)}, bf16[48,4096]{1,0:T(8,128)(2,1)S(1)}, u32[]{:S(2)}, u32[]{:S(2)}) collective-permute-start(bf16[48,4096]{1,0:T(8,128)(2,1)S(1)} %get-tuple-element.44), channel_id=1, source_target_pairs={{0,2},{2,0},{4,6},{6,4},{1,3},{3,1},{5,7},{7,5},{8,10},{10,8},{12,... | collective-permute-start | bytes 1179656 | tf_op jit(solution)/shard_map/ppermute | solution.py:227
  45.0 18.4 %collective-permute-start.11 = (bf16[192,1024]{1,0:T(8,128)(2,1)S(1)}, bf16[192,1024]{1,0:T(8,128)(2,1)S(1)}, u32[]{:S(2)}, u32[]{:S(2)}) collective-permute-start(bf16[192,1024]{1,0:T(8,128)(2,1)S(1)} %collective-permute-done.1.refs_0_), channel_id=1, source_target_pairs={{0,16},{8,24},{16,0},{24,8},{1,17},{9,25},{17,1},{25,9},{2,18},{10... | collective-permute-start | bytes 1179656 | tf_op jit(solution)/shard_map/ppermute | solution.py:230
  46.2 17.2 %collective-permute-start.12 = (bf16[192,1024]{1,0:T(8,128)(2,1)S(1)}, bf16[192,1024]{1,0:T(8,128)(2,1)S(1)}, u32[]{:S(2)}, u32[]{:S(2)}) collective-permute-start(bf16[192,1024]{1,0:T(8,128)(2,1)S(1)} %collective-permute-done.8.refs_10_), channel_id=1, source_target_pairs={{0,16},{8,24},{16,0},{24,8},{1,17},{9,25},{17,1},{25,9},{2,18},{10... | collective-permute-start | bytes 1179656 | tf_op jit(solution)/shard_map/ppermute | solution.py:230
  48.3 15.1 %collective-permute-start.13 = (bf16[192,1024]{1,0:T(8,128)(2,1)S(1)}, bf16[192,1024]{1,0:T(8,128)(2,1)S(1)}, u32[]{:S(2)}, u32[]{:S(2)}) collective-permute-start(bf16[192,1024]{1,0:T(8,128)(2,1)S(1)} %collective-permute-done.5.refs_7_), channel_id=1, source_target_pairs={{0,8},{8,0},{16,24},{24,16},{1,9},{9,1},{17,25},{25,17},{2,10},{10... | collective-permute-start | bytes 1179656 | tf_op jit(solution)/shard_map/ppermute | solution.py:230
  61.9 7.7 %collective-permute-start.19 = (bf16[48,4096]{1,0:T(8,128)(2,1)S(1)}, bf16[48,4096]{1,0:T(8,128)(2,1)S(1)}, u32[]{:S(2)}, u32[]{:S(2)}) collective-permute-start(bf16[48,4096]{1,0:T(8,128)(2,1)S(1)} %collective-permute-done.17.refs_17_), channel_id=1, source_target_pairs={{0,1},{1,0},{2,3},{3,2},{4,5},{5,4},{6,7},{7,6},{8,9},{9,8},{10,11... | collective-permute-start | bytes 1179656 | tf_op jit(solution)/shard_map/ppermute | solution.py:233
  62.4 7.3 %collective-permute-start.20 = (bf16[48,4096]{1,0:T(8,128)(2,1)S(1)}, bf16[48,4096]{1,0:T(8,128)(2,1)S(1)}, u32[]{:S(2)}, u32[]{:S(2)}) collective-permute-start(bf16[48,4096]{1,0:T(8,128)(2,1)S(1)} %collective-permute-done.18.refs_18_), channel_id=1, source_target_pairs={{0,1},{1,0},{2,3},{3,2},{4,5},{5,4},{6,7},{7,6},{8,9},{9,8},{10,11... | collective-permute-start | bytes 1179656 | tf_op jit(solution)/shard_map/ppermute | solution.py:233
  63.4 4.9 %collective-permute-start.14 = (bf16[96,1024]{1,0:T(8,128)(2,1)S(1)}, bf16[96,1024]{1,0:T(8,128)(2,1)S(1)}, u32[]{:S(2)}, u32[]{:S(2)}) collective-permute-start(bf16[96,1024]{1,0:T(8,128)(2,1)S(1)} %slice.6), channel_id=1, source_target_pairs={{0,16},{8,24},{16,0},{24,8},{1,17},{9,25},{17,1},{25,9},{2,18},{10... | collective-permute-start | bytes 589832 | tf_op jit(solution)/shard_map/ppermute | solution.py:230
  64.7 4.9 %collective-permute-start.15 = (bf16[96,1024]{1,0:T(8,128)(2,1)S(1)}, bf16[96,1024]{1,0:T(8,128)(2,1)S(1)}, u32[]{:S(2)}, u32[]{:S(2)}) collective-permute-start(bf16[96,1024]{1,0:T(8,128)(2,1)S(1)} %slice.7), channel_id=1, source_target_pairs={{0,8},{8,0},{16,24},{24,16},{1,9},{9,1},{17,25},{25,17},{2,10},{10... | collective-permute-start | bytes 589832 | tf_op jit(solution)/shard_map/ppermute | solution.py:230
  66.0 17.3 %collective-permute-start.25 = (bf16[48,4096]{1,0:T(8,128)(2,1)S(1)}, bf16[48,4096]{1,0:T(8,128)(2,1)S(1)}, u32[]{:S(2)}, u32[]{:S(2)}) collective-permute-start(bf16[48,4096]{1,0:T(8,128)(2,1)S(1)} %get-tuple-element.50), channel_id=1, source_target_pairs={{0,6},{2,4},{4,2},{6,0},{1,7},{3,5},{5,3},{7,1},{8,14},{10,12},{12... | collective-permute-start | bytes 1179656 | tf_op jit(solution)/shard_map/ppermute | solution.py:227
  73.5 12.4 %collective-permute-start.21 = (bf16[48,4096]{1,0:T(8,128)(2,1)S(1)}, bf16[48,4096]{1,0:T(8,128)(2,1)S(1)}, u32[]{:S(2)}, u32[]{:S(2)}) collective-permute-start(bf16[48,4096]{1,0:T(8,128)(2,1)S(1)} %get-tuple-element.46), channel_id=1, source_target_pairs={{0,1},{1,0},{2,3},{3,2},{4,5},{5,4},{6,7},{7,6},{8,9},{9,8},{10,11... | collective-permute-start | bytes 1179656 | tf_op jit(solution)/shard_map/ppermute | solution.py:233
  76.3 9.9 %collective-permute-start.23 = (bf16[48,4096]{1,0:T(8,128)(2,1)S(1)}, bf16[48,4096]{1,0:T(8,128)(2,1)S(1)}, u32[]{:S(2)}, u32[]{:S(2)}) collective-permute-start(bf16[48,4096]{1,0:T(8,128)(2,1)S(1)} %get-tuple-element.48), channel_id=1, source_target_pairs={{0,1},{1,0},{2,3},{3,2},{4,5},{5,4},{6,7},{7,6},{8,9},{9,8},{10,11... | collective-permute-start | bytes 1179656 | tf_op jit(solution)/shard_map/ppermute | solution.py:233
  83.3 4.0 %collective-permute-start.26 = (bf16[48,4096]{1,0:T(8,128)(2,1)S(1)}, bf16[48,4096]{1,0:T(8,128)(2,1)S(1)}, u32[]{:S(2)}, u32[]{:S(2)}) collective-permute-start(bf16[48,4096]{1,0:T(8,128)(2,1)S(1)} %collective-permute-done.25.refs_17_), channel_id=1, source_target_pairs={{0,1},{1,0},{2,3},{3,2},{4,5},{5,4},{6,7},{7,6},{8,9},{9,8},{10,11... | collective-permute-start | bytes 1179656 | tf_op jit(solution)/shard_map/ppermute | solution.py:233
  86.1 17.3 %collective-permute-start.22 = (bf16[48,4096]{1,0:T(8,128)(2,1)S(1)}, bf16[48,4096]{1,0:T(8,128)(2,1)S(1)}, u32[]{:S(2)}, u32[]{:S(2)}) collective-permute-start(bf16[48,4096]{1,0:T(8,128)(2,1)S(1)} %add_convert_fusion.3), channel_id=1, source_target_pairs={{0,4},{2,6},{4,0},{6,2},{1,5},{3,7},{5,1},{7,3},{8,12},{10,14},{12... | collective-permute-start | bytes 1179656 | tf_op jit(solution)/shard_map/ppermute | solution.py:227
  91.2 12.7 %collective-permute-start.28 = (bf16[48,4096]{1,0:T(8,128)(2,1)S(1)}, bf16[48,4096]{1,0:T(8,128)(2,1)S(1)}, u32[]{:S(2)}, u32[]{:S(2)}) collective-permute-start(bf16[48,4096]{1,0:T(8,128)(2,1)S(1)} %get-tuple-element.55), channel_id=1, source_target_pairs={{0,1},{1,0},{2,3},{3,2},{4,5},{5,4},{6,7},{7,6},{8,9},{9,8},{10,11... | collective-permute-start | bytes 1179656 | tf_op jit(solution)/shard_map/ppermute | solution.py:233
  91.7 15.2 %collective-permute-start.24 = (bf16[48,4096]{1,0:T(8,128)(2,1)S(1)}, bf16[48,4096]{1,0:T(8,128)(2,1)S(1)}, u32[]{:S(2)}, u32[]{:S(2)}) collective-permute-start(bf16[48,4096]{1,0:T(8,128)(2,1)S(1)} %add_convert_fusion.2), channel_id=1, source_target_pairs={{0,2},{2,0},{4,6},{6,4},{1,3},{3,1},{5,7},{7,5},{8,10},{10,8},{12,... | collective-permute-start | bytes 1179656 | tf_op jit(solution)/shard_map/ppermute | solution.py:227
  92.1 15.7 %collective-permute-start.27 = (bf16[48,4096]{1,0:T(8,128)(2,1)S(1)}, bf16[48,4096]{1,0:T(8,128)(2,1)S(1)}, u32[]{:S(2)}, u32[]{:S(2)}) collective-permute-start(bf16[48,4096]{1,0:T(8,128)(2,1)S(1)} %get-tuple-element.53), channel_id=1, source_target_pairs={{0,1},{1,0},{2,3},{3,2},{4,5},{5,4},{6,7},{7,6},{8,9},{9,8},{10,11... | collective-permute-start | bytes 1179656 | tf_op jit(solution)/shard_map/ppermute | solution.py:233
  103.4 3.4 %collective-permute-start.30 = (bf16[48,4096]{1,0:T(8,128)(2,1)S(1)}, bf16[48,4096]{1,0:T(8,128)(2,1)S(1)}, u32[]{:S(2)}, u32[]{:S(2)}) collective-permute-start(bf16[48,4096]{1,0:T(8,128)(2,1)S(1)} %collective-permute-done.22.refs_0_), channel_id=1, source_target_pairs={{0,1},{1,0},{2,3},{3,2},{4,5},{5,4},{6,7},{7,6},{8,9},{9,8},{10,11... | collective-permute-start | bytes 1179656 | tf_op jit(solution)/shard_map/ppermute | solution.py:233
  104.1 19.2 %collective-permute-start.29 = (bf16[48,4096]{1,0:T(8,128)(2,1)S(1)}, bf16[48,4096]{1,0:T(8,128)(2,1)S(1)}, u32[]{:S(2)}, u32[]{:S(2)}) collective-permute-start(bf16[48,4096]{1,0:T(8,128)(2,1)S(1)} %add_convert_fusion), channel_id=1, source_target_pairs={{0,6},{2,4},{4,2},{6,0},{1,7},{3,5},{5,3},{7,1},{8,14},{10,12},{12... | collective-permute-start | bytes 1179656 | tf_op jit(solution)/shard_map/ppermute | solution.py:227
  106.8 16.5 %collective-permute-start.31 = (bf16[48,4096]{1,0:T(8,128)(2,1)S(1)}, bf16[48,4096]{1,0:T(8,128)(2,1)S(1)}, u32[]{:S(2)}, u32[]{:S(2)}) collective-permute-start(bf16[48,4096]{1,0:T(8,128)(2,1)S(1)} %collective-permute-done.24.refs_1_), channel_id=1, source_target_pairs={{0,1},{1,0},{2,3},{3,2},{4,5},{5,4},{6,7},{7,6},{8,9},{9,8},{10,11... | collective-permute-start | bytes 1179656 | tf_op jit(solution)/shard_map/ppermute | solution.py:233
  107.9 16.1 %collective-permute-start.32 = (bf16[48,4096]{1,0:T(8,128)(2,1)S(1)}, bf16[48,4096]{1,0:T(8,128)(2,1)S(1)}, u32[]{:S(2)}, u32[]{:S(2)}) collective-permute-start(bf16[48,4096]{1,0:T(8,128)(2,1)S(1)} %add_convert_fusion.1.refs_2_), channel_id=1, source_target_pairs={{0,1},{1,0},{2,3},{3,2},{4,5},{5,4},{6,7},{7,6},{8,9},{9,8},{10,11... | collective-permute-start | bytes 1179656 | tf_op jit(solution)/shard_map/ppermute | solution.py:233
  123.3 2.1 %collective-permute-start.33 = (bf16[48,4096]{1,0:T(8,128)(2,1)S(1)}, bf16[48,4096]{1,0:T(8,128)(2,1)S(1)}, u32[]{:S(2)}, u32[]{:S(2)}) collective-permute-start(bf16[48,4096]{1,0:T(8,128)(2,1)S(1)} %collective-permute-done.29.refs_3_), channel_id=1, source_target_pairs={{0,1},{1,0},{2,3},{3,2},{4,5},{5,4},{6,7},{7,6},{8,9},{9,8},{10,11... | collective-permute-start | bytes 1179656 | tf_op jit(solution)/shard_map/ppermute | solution.py:233

commit v4 on v3

--- a/solution.py
+++ b/solution.py
@@ -75,26 +75,30 @@
 
 
 def dispatch_kernel(n_experts, capacity, routes_ref, tokens_ref, cotangent_ref, *refs):
-    out_refs, table_ref = refs[:-1], refs[-1]
+    out_refs, local_ref, table_ref = refs[:n_experts], *refs[n_experts:]
 
     @pl.when(pl.program_id(0) == 0)
     def _():
         table_ref[...] = slot_table(routes_ref[...], n_experts, capacity)
 
-    def send(source_ref):
-        sent = jnp.dot(table_ref[...], source_ref[...], preferred_element_type=F32).astype(BF16)
+    def rows(source_ref, count):
+        return jnp.dot(table_ref[:count], source_ref[...], preferred_element_type=F32).astype(BF16)
+
+    def send(mine_ref, other_ref):
+        sent = rows(mine_ref, n_experts * capacity)
         for k in range(n_experts):
             out_refs[k][...] = sent[k * capacity:(k + 1) * capacity]
+        local_ref[...] = rows(other_ref, capacity)
 
     core = lax.axis_index("tensor")
-    pl.when(core == 0)(lambda: send(tokens_ref))
-    pl.when(core != 0)(lambda: send(cotangent_ref))
+    pl.when(core == 0)(lambda: send(tokens_ref, cotangent_ref))
+    pl.when(core != 0)(lambda: send(cotangent_ref, tokens_ref))
 
 
 def merge_kernel(order, capacity, blocks, *refs):
-    n_experts = len(order)
-    mine_refs, other_refs = refs[:n_experts], refs[n_experts:2 * n_experts]
-    routes_ref, out_ref, grad_ref, held_ref, sems = refs[2 * n_experts:]
+    n_experts, count = len(order) + 1, len(order)
+    mine_refs, other_refs = refs[:count], refs[count:2 * count]
+    kept_ref, got_ref, routes_ref, out_ref, grad_ref, held_ref, sems = refs[2 * count:]
     table = slot_table(routes_ref[...], n_experts, capacity)
     width = out_ref.shape[1] // blocks
     first = lax.axis_index("tensor") == 0
@@ -102,10 +106,15 @@
     for i in range(blocks):
         at = pl.ds(i * width, width)
 
-        def rows(refs):
-            return jnp.concatenate([refs[order.index(k)][:, at] for k in range(n_experts)], axis=0)
-
-        mine, other = rows(mine_refs), rows(other_refs)
+        def half(ref, h):
+            return ref[h * capacity:(h + 1) * capacity, at].astype(F32)
+
+        def rows(refs, h):
+            parts = [refs[order.index(k)][:, at] for k in range(1, n_experts)]
+            stayed = (half(kept_ref, h) + half(got_ref, 1 - h)).astype(BF16)
+            return jnp.concatenate([stayed, *parts], axis=0)
+
+        mine, other = rows(mine_refs, 0), rows(other_refs, 1)
         for w, (a, b, ref) in enumerate(((mine, other, out_ref), (other, mine, grad_ref))):
             total = lax.dot_general(table, jnp.where(first, a, b), FIRST, preferred_element_type=F32)
             held_ref[w, :, at] = total.astype(BF16)
@@ -115,18 +124,23 @@
         copy.wait()
 
 
-def expert_kernel(n_parts, n_dp, n_rows, *refs):
+def expert_kernel(n_parts, n_dp, n_rows, stacked, *refs):
     refs = list(refs)
     n_experts = len(n_parts)
     weights = [[refs.pop(0) for _ in range(count)] for count in n_parts]
     mine_refs = [refs.pop(0) for _ in range(n_rows)]
     other_refs = [refs.pop(0) for _ in range(n_rows)]
-    keep_refs = [refs.pop(0) for _ in range(n_rows)]
-    give_refs = [refs.pop(0) for _ in range(n_rows)]
+    capacity = mine_refs[0].shape[0]
+    out_refs = []
+    for i in range(n_rows):
+        if i == stacked:
+            ref = refs.pop(0)
+            out_refs.append((ref.at[pl.ds(0, capacity)], ref.at[pl.ds(capacity, capacity)]))
+        else:
+            out_refs.append((refs.pop(0), refs.pop(0)))
     me = lax.axis_index("dp")
     first = lax.axis_index("tensor") == 0
     deep, width = weights[0][0].shape
-    capacity = mine_refs[0].shape[0]
     per, cut = deep // 3, deep // 2
 
     def columns(j):
@@ -166,8 +180,9 @@
         given = jnp.where(first, grad, out).astype(BF16)
         for i in range(n_rows):
             at = slice(i * capacity, (i + 1) * capacity)
-            keep_refs[i][:, columns(j)] = kept[at]
-            give_refs[i][:, columns(j)] = given[at]
+            keep_ref, give_ref = out_refs[i]
+            keep_ref[:, columns(j)] = kept[at]
+            give_ref[:, columns(j)] = given[at]
 
 
 def after(values, awaited):
@@ -206,16 +221,16 @@
 
     route_row = routes.reshape(1, tok_count)
     block = width // 4
-    sent = pl.pallas_call(
+    *sent, local = pl.pallas_call(
         functools.partial(dispatch_kernel, n_experts, capacity),
         grid=(width // block,),
-        out_shape=[shape((capacity, width), BF16)] * n_experts,
+        out_shape=[shape((capacity, width), BF16)] * (n_experts + 1),
         in_specs=[
             pl.BlockSpec((1, tok_count), lambda i: (0, 0)),
             pl.BlockSpec((tok_count, block), lambda i: (0, i)),
             pl.BlockSpec((tok_count, block), lambda i: (0, i)),
         ],
-        out_specs=[pl.BlockSpec((capacity, block), lambda i: (0, i))] * n_experts,
+        out_specs=[pl.BlockSpec((capacity, block), lambda i: (0, i))] * (n_experts + 1),
         scratch_shapes=[pltpu.VMEM((n_experts * capacity, tok_count), BF16)],
         compiler_params=params,
         name="dispatch_rows",
@@ -242,68 +257,75 @@
         cut = pieces[0].shape[0] // 2
         return [spread(pieces[1][:cut], 2), spread(pieces[2][cut:], 1)]
 
-    weights = [None] * n_experts
-    rows, others = {0: sent[0]}, {}
-    chunk3 = planes(sent_w[3], 3)
-    chunk1 = planes(sent_w[1], 1)
+    rows, others = {0: sent[0]}, {0: local}
+    chunk3, chunk1 = planes(sent_w[3], 3), planes(sent_w[1], 1)
+    pieces0 = direct(sent_w[0])
     (sent_w2,) = after([sent_w[2]], [chunk3])
     chunk2 = planes(sent_w2, 2)
-    weights[0] = direct(sent_w[0])
-    (chunk3,) = after([chunk3], weights[0][1:3])
+    (chunk1,) = after([chunk1], [*pieces0[1:], local])
+    pieces1 = near_far(chunk1)
+    (chunk3,) = after([chunk3], pieces0[1:3])
     pieces3 = near_far(chunk3)
-    (chunk1,) = after([chunk1], weights[0][1:])
-    pieces1 = near_far(chunk1)
-    others[0] = swapped(rows[0])
-    (sent_2, sent_1) = after([sent[2], sent[1]], [chunk2, others[0]])
-    rows[2] = planes(sent_2, 2)
-    rows[1] = planes(sent_1, 1)
-    (chunk2,) = after([chunk2], pieces3[1:] + pieces1[1:])
-    pieces2 = near_far(chunk2)
-    weights[3] = pieces3 + [spread(pieces3[2], 1)]
-    weights[1] = pieces1 + [spread(pieces1[1], 2)]
-    held2 = after(pieces2[1:], [weights[1][3], weights[3][3]])
-    weights[2] = pieces2 + diagonal([chunk2, *held2])
-    (sent_3,) = after([sent[3]], [rows[2]])
-    rows[3] = planes(sent_3, 3)
+    (held,) = after([chunk2], pieces3[1:] + pieces1[1:])
+    pieces2 = near_far(held)
+    for k, awaited in ((2, chunk2), (1, chunk2), (3, None)):
+        (row,) = after([sent[k]], [rows[2] if awaited is None else awaited])
+        rows[k] = planes(row, k)
+    pieces1.append(spread(pieces1[1], 2))
+    pieces3.append(spread(pieces3[2], 1))
+    held2 = after(pieces2[1:], [pieces1[3], pieces3[3]])
+    pieces2 += diagonal([pieces2[0], *held2])
     for k in (2, 1, 3):
         others[k] = swapped(rows[k])
 
-    chunk_order = (2, 3, 1, 0)
-    mine, other = {}, {}
-    returned = []
+    weights = (pieces3, pieces0, pieces1, pieces2)
+    mine, other, returned = {}, {}, []
     for members in ((2, 1), (3, 0)):
         count = len(members)
         here = {k: rows[k] for k in members}
         if returned:
-            (here[3],) = after([rows[3]], returned)
+            (here[3],) = after([rows[3]], returned[:1])
+        out_shape = []
+        for k in members:
+            out_shape += [shape((capacity, width), BF16)] * 2 if k else [shape((2 * capacity, width), BF16)]
         results = pl.pallas_call(
-            functools.partial(expert_kernel, [len(weights[k]) for k in chunk_order], n_dp, count),
-            out_shape=[shape((capacity, width), BF16)] * (2 * count),
-            in_specs=[vmem] * (sum(len(parts) for parts in weights) + 2 * count),
-            out_specs=[vmem] * (2 * count),
+            functools.partial(
+                expert_kernel,
+                [len(pieces) for pieces in weights],
+                n_dp,
+                count,
+                members.index(0) if 0 in members else None,
+            ),
+            out_shape=out_shape,
+            in_specs=[vmem] * (sum(len(pieces) for pieces in weights) + 2 * count),
+            out_specs=[vmem] * len(out_shape),
             compiler_params=params,
             name="expert_math",
         )(
-            *[part for k in chunk_order for part in weights[k]],
+            *[piece for pieces in weights for piece in pieces],
             *[here[k] for k in members],
             *[others[k] for k in members],
         )
-        for i, k in enumerate(members):
-            kept, given = results[i], results[count + i]
-            got = swapped(given)
-            total = (kept.astype(F32) + got.astype(F32)).astype(BF16)
+        results = list(results)
+        for k in members:
+            if not k:
+                stayed = results.pop(0)
+                stayed = (stayed, swapped(stayed))
+                continue
+            kept, given = results.pop(0), results.pop(0)
+            total = (kept.astype(F32) + swapped(given).astype(F32)).astype(BF16)
             returned.append(total)
-            mine[k] = planes(total, k) if k else total
-    other[0] = swapped(mine[0])
-    other[2] = swapped(mine[2])
-    other[1] = swapped(after([mine[1]], [other[2]])[0])
-    other[3] = swapped(after([mine[3]], [other[1]])[0])
-
-    home_order = (2, 1, 0, 3)
+            mine[k] = planes(total, k)
+    awaited = []
+    for k in (2, 1, 3):
+        other[k] = swapped(after([mine[k]], awaited)[0])
+        awaited = [other[k]]
+
+    order = (2, 1, 3)
     blocks = 8
     return tuple(
         pl.pallas_call(
-            functools.partial(merge_kernel, home_order, capacity, blocks),
+            functools.partial(merge_kernel, order, capacity, blocks),
             out_shape=[shape((tok_count, width), BF16)] * 2,
             in_specs=[vmem] * (2 * n_experts + 1),
             out_specs=[pl.BlockSpec(memory_space=pltpu.HBM)] * 2,
@@ -313,7 +335,7 @@
             ],
             compiler_params=params,
             name="merge_rows",
-        )(*[mine[k] for k in home_order], *[other[k] for k in home_order], route_row)
+        )(*[mine[k] for k in order], *[other[k] for k in order], *stayed, route_row)
     )
 
 

time: 127 us -> 125 us (0.984)
  starting transfers between devices: 34.6 us -> 32.6 us
    ppermute x9, waiting for transfers between devices: 68.6 us -> 67.2 us  [planes(): return lax.ppermute(chunk, 'expert', flips(n_experts, k))]
    ppermute x12 -> x10, starting transfers between devices: 12.4 us -> 11.5 us  [swapped(): return lax.ppermute(chunk, 'tensor', swap)]
  transfers between devices with their start and end apart: 34 -> 32, of which waited for: 13 -> 13; matrix products, arithmetic and copies ran while one was open for 0% -> 0% of each run, Pallas kernels for 7% -> 8%
where the time goes in v4:
time: 125 us; the launch traced here: 124 us
  waiting for transfers between devices  75.2 us (60%)
  starting transfers between devices  32.6 us (26%)
  Pallas kernels  14.3 us (11%)
  local copies, waits for them, and re-layouts  1.27 us (1%)
    ppermute x9, waiting for transfers between devices, planes(): return lax.ppermute(chunk, 'expert', flips(n_experts, k))  67.2 us
    ppermute x13, starting transfers between devices, spread(): return lax.ppermute(chunk, 'dp', flips(n_dp, step))  14.3 us
    ppermute x10, starting transfers between devices, swapped(): return lax.ppermute(chunk, 'tensor', swap)  11.5 us
    pallas_call x2, Pallas kernels, aligned_plan(): pl.pallas_call(functools.partial(expert_kernel, [len(pieces) for pieces i...  7.76 us
    ppermute x9, starting transfers between devices, planes(): return lax.ppermute(chunk, 'expert', flips(n_experts, k))  6.84 us
    ppermute x13, waiting for transfers between devices, spread(): return lax.ppermute(chunk, 'dp', flips(n_dp, step))  5.45 us
    pallas_call x1, Pallas kernels, aligned_plan(): pl.pallas_call(functools.partial(select_kernel, n_experts, halves, shards...  2.97 us
    ppermute x10, waiting for transfers between devices, swapped(): return lax.ppermute(chunk, 'tensor', swap)  2.54 us
  transfers between devices with their start and end apart: 32, of which 13 were waited for; matrix products, arithmetic and copies ran while one was open for 0% of the time, Pallas kernels for 8%

profile of v4, /device:TPU:9, one launch (start us, length us, event | category | flops | bytes accessed | tf_op | source)
XLA Modules:
  0.0 124.4 jit_solution(17423366093275283861)
XLA Ops:
  0.6 3.0 %select_rows.1 = (bf16[192,1024]{1,0:T(8,128)(2,1)}, bf16[192,1024]{1,0:T(8,128)(2,1)}, bf16[192,1024]{1,0:T(8,128)(2,1)}, bf16[192,1024]{1,0:T(8,128)(2,1)}) custom-call(s32[4,512]{1,0:T(4,128)} %cluster_hbm.1, bf16[231,1024]{1,0:T(8,128)(2,1)} %gate_hbm.1, bf16[231,1024]{1,0:T(8,128)(2,1)} %up_hbm.1, bf16[231,1024]{1,0:T(8,128)(2,1)} %down_hbm.1), custom_call_target="tpu_custom_call" | custom-call | tf_op jit(solution)/shard_map/select_rows/pallas_call | solution.py:206
  3.6 1.4 %collective-permute-start = (bf16[192,1024]{1,0:T(8,128)(2,1)}, bf16[192,1024]{1,0:T(8,128)(2,1)S(1)}, u32[]{:S(2)}, u32[]{:S(2)}) collective-permute-start(bf16[192,1024]{1,0:T(8,128)(2,1)} %get-tuple-element.30), channel_id=1, source_target_pairs={{0,6},{2,4},{4,2},{6,0},{1,7},{3,5},{5,3},{7,1},{8,14},{10,12},{12... | collective-permute-start | bytes 1179656 | tf_op jit(solution)/shard_map/ppermute | solution.py:242
  5.0 1.2 collective-permute-start.1
  6.2 1.2 collective-permute-start.2
  7.4 0.2 collective-permute-start.6
  7.6 2.2 %collective-permute-start.7 = (bf16[192,1024]{1,0:T(8,128)(2,1)}, bf16[192,1024]{1,0:T(8,128)(2,1)S(1)}, u32[]{:S(2)}, u32[]{:S(2)}) collective-permute-start(bf16[192,1024]{1,0:T(8,128)(2,1)} %get-tuple-element.33), channel_id=1, source_target_pairs={{0,2},{2,0},{4,6},{6,4},{1,3},{3,1},{5,7},{7,5},{8,10},{10,8},{12,... | collective-permute-start | bytes 1179656 | tf_op jit(solution)/shard_map/ppermute | solution.py:242
  9.8 12.7 %collective-permute-done.refs_0_ = bf16[192,1024]{1,0:T(8,128)(2,1)S(1)} collective-permute-done((bf16[192,1024]{1,0:T(8,128)(2,1)}, bf16[192,1024]{1,0:T(8,128)(2,1)S(1)}, u32[]{:S(2)}, u32[]{:S(2)}) %collective-permute-start) | collective-permute-done | bytes 393248 | tf_op jit(solution)/shard_map/ppermute | solution.py:242
  22.5 1.2 collective-permute-start.4
  23.7 1.2 collective-permute-start.3
  25.0 1.2 copy-done.2
  26.2 1.7 %dispatch_rows.1 = (bf16[48,4096]{1,0:T(8,128)(2,1)S(1)}, bf16[48,4096]{1,0:T(8,128)(2,1)S(1)}, bf16[48,4096]{1,0:T(8,128)(2,1)S(1)}, bf16[48,4096]{1,0:T(8,128)(2,1)S(1)}, bf16[48,4096]{1,0:T(8,128)(2,1)S(1)}) custom-call(s32[1,128]{1,0:T(1,128)S(1)} %bitcast.1, bf16[128,4096]{1,0:T(8,128)(2,1)S(1)} %copy-done.1, bf16[128,4096]{1,0:T(8,128)(2,1)S(1)} %copy-done.2), custom_call_target="tpu_custom_call" | custom-call | tf_op jit(solution)/shard_map/dispatch_rows/pallas_call | solution.py:224
  27.9 0.7 collective-permute-start.8
  28.6 0.2 collective-permute-start.9
  28.8 1.8 %collective-permute-done.4.refs_2_ = bf16[192,1024]{1,0:T(8,128)(2,1)S(1)} collective-permute-done((bf16[192,1024]{1,0:T(8,128)(2,1)S(1)}, bf16[192,1024]{1,0:T(8,128)(2,1)S(1)}, u32[]{:S(2)}, u32[]{:S(2)}) %collective-permute-start.4) | collective-permute-done | bytes 393248 | tf_op jit(solution)/shard_map/ppermute | solution.py:245
  30.6 2.3 %collective-permute-start.5 = (bf16[192,1024]{1,0:T(8,128)(2,1)S(1)}, bf16[192,1024]{1,0:T(8,128)(2,1)S(1)}, u32[]{:S(2)}, u32[]{:S(2)}) collective-permute-start(bf16[192,1024]{1,0:T(8,128)(2,1)S(1)} %collective-permute-done.4.refs_2_), channel_id=1, source_target_pairs={{0,8},{8,0},{16,24},{24,16},{1,9},{9,1},{17,25},{25,17},{2,10},{10... | collective-permute-start | bytes 1179656 | tf_op jit(solution)/shard_map/ppermute | solution.py:245
  32.9 5.9 %collective-permute-done.11.refs_12_ = bf16[192,1024]{1,0:T(8,128)(2,1)S(1)} collective-permute-done((bf16[192,1024]{1,0:T(8,128)(2,1)}, bf16[192,1024]{1,0:T(8,128)(2,1)S(1)}, u32[]{:S(2)}, u32[]{:S(2)}) %collective-permute-start.11) | collective-permute-done | bytes 393248 | tf_op jit(solution)/shard_map/ppermute | solution.py:242
  38.9 3.0 %collective-permute-start.16 = (bf16[48,4096]{1,0:T(8,128)(2,1)S(1)}, bf16[48,4096]{1,0:T(8,128)(2,1)S(1)}, u32[]{:S(2)}, u32[]{:S(2)}) collective-permute-start(bf16[48,4096]{1,0:T(8,128)(2,1)S(1)} %get-tuple-element.42), channel_id=1, source_target_pairs={{0,4},{2,6},{4,0},{6,2},{1,5},{3,7},{5,1},{7,3},{8,12},{10,14},{12... | collective-permute-start | bytes 1179656 | tf_op jit(solution)/shard_map/ppermute | solution.py:242
  41.9 0.1 collective-permute-start.17
  41.9 2.3 %collective-permute-start.12 = (bf16[192,1024]{1,0:T(8,128)(2,1)S(1)}, bf16[192,1024]{1,0:T(8,128)(2,1)S(1)}, u32[]{:S(2)}, u32[]{:S(2)}) collective-permute-start(bf16[192,1024]{1,0:T(8,128)(2,1)S(1)} %collective-permute-done.11.refs_12_), channel_id=1, source_target_pairs={{0,8},{8,0},{16,24},{24,16},{1,9},{9,1},{17,25},{25,17},{2,10},{10... | collective-permute-start | bytes 1179656 | tf_op jit(solution)/shard_map/ppermute | solution.py:245
  44.2 0.2 collective-permute-start.10
  44.4 0.6 collective-permute-done.5.refs_3_
  45.1 0.7 collective-permute-start.13
  45.8 13.1 %collective-permute-done.16.refs_17_ = bf16[48,4096]{1,0:T(8,128)(2,1)S(1)} collective-permute-done((bf16[48,4096]{1,0:T(8,128)(2,1)S(1)}, bf16[48,4096]{1,0:T(8,128)(2,1)S(1)}, u32[]{:S(2)}, u32[]{:S(2)}) %collective-permute-start.16) | collective-permute-done | bytes 393248 | tf_op jit(solution)/shard_map/ppermute | solution.py:242
  58.9 0.5 collective-permute-start.18
  59.4 1.0 collective-permute-start.19
  60.4 0.8 collective-permute-start.14
  61.2 1.8 %collective-permute-start.15 = (bf16[96,1024]{1,0:T(8,128)(2,1)S(1)}, bf16[96,1024]{1,0:T(8,128)(2,1)S(1)}, u32[]{:S(2)}, u32[]{:S(2)}) collective-permute-start(bf16[96,1024]{1,0:T(8,128)(2,1)S(1)} %slice.7), channel_id=1, source_target_pairs={{0,8},{8,0},{16,24},{24,16},{1,9},{9,1},{17,25},{25,17},{2,10},{10... | collective-permute-start | bytes 589832 | tf_op jit(solution)/shard_map/ppermute | solution.py:245
  63.1 2.5 %collective-permute-done.14.refs_15_ = bf16[96,1024]{1,0:T(8,128)(2,1)S(1)} collective-permute-done((bf16[96,1024]{1,0:T(8,128)(2,1)S(1)}, bf16[96,1024]{1,0:T(8,128)(2,1)S(1)}, u32[]{:S(2)}, u32[]{:S(2)}) %collective-permute-start.14) | collective-permute-done | bytes 196640 | tf_op jit(solution)/shard_map/ppermute | solution.py:245
  65.6 0.6 collective-permute-done.15.refs_16_
  66.2 3.9 %expert_math.2 = (bf16[48,4096]{1,0:T(8,128)(2,1)S(1)}, bf16[48,4096]{1,0:T(8,128)(2,1)S(1)}, bf16[48,4096]{1,0:T(8,128)(2,1)S(1)}, bf16[48,4096]{1,0:T(8,128)(2,1)S(1)}) custom-call(bf16[192,1024]{1,0:T(8,128)(2,1)S(1)} %collective-permute-done.refs_0_, bf16[192,1024]{1,0:T(8,128)(2,1)S(1)} %collective-permute-done.3.refs_1_, ...), custom_call_target="tpu_custom_call" | custom-call | tf_op jit(solution)/shard_map/expert_math/pallas_call | solution.py:291
  70.1 4.5 %collective-permute-start.20 = (bf16[48,4096]{1,0:T(8,128)(2,1)S(1)}, bf16[48,4096]{1,0:T(8,128)(2,1)S(1)}, u32[]{:S(2)}, u32[]{:S(2)}) collective-permute-start(bf16[48,4096]{1,0:T(8,128)(2,1)S(1)} %get-tuple-element.46), channel_id=1, source_target_pairs={{0,1},{1,0},{2,3},{3,2},{4,5},{5,4},{6,7},{7,6},{8,9},{9,8},{10,11... | collective-permute-start | bytes 1179656 | tf_op jit(solution)/shard_map/ppermute | solution.py:248
  74.5 0.1 collective-permute-start.22
  74.6 5.8 %collective-permute-done.24.refs_17_ = bf16[48,4096]{1,0:T(8,128)(2,1)S(1)} collective-permute-done((bf16[48,4096]{1,0:T(8,128)(2,1)S(1)}, bf16[48,4096]{1,0:T(8,128)(2,1)S(1)}, u32[]{:S(2)}, u32[]{:S(2)}) %collective-permute-start.24) | collective-permute-done | bytes 393248 | tf_op jit(solution)/shard_map/ppermute | solution.py:242
  80.4 2.7 %collective-permute-start.25 = (bf16[48,4096]{1,0:T(8,128)(2,1)S(1)}, bf16[48,4096]{1,0:T(8,128)(2,1)S(1)}, u32[]{:S(2)}, u32[]{:S(2)}) collective-permute-start(bf16[48,4096]{1,0:T(8,128)(2,1)S(1)} %collective-permute-done.24.refs_17_), channel_id=1, source_target_pairs={{0,1},{1,0},{2,3},{3,2},{4,5},{5,4},{6,7},{7,6},{8,9},{9,8},{10,11... | collective-permute-start | bytes 1179656 | tf_op jit(solution)/shard_map/ppermute | solution.py:248
  83.0 0.1 add_convert_fusion.2
  83.2 1.2 collective-permute-done.25.refs_19_
  84.4 3.9 %expert_math.3 = (bf16[48,4096]{1,0:T(8,128)(2,1)S(1)}, bf16[48,4096]{1,0:T(8,128)(2,1)S(1)}, bf16[96,4096]{1,0:T(8,128)(2,1)S(1)}) custom-call(bf16[192,1024]{1,0:T(8,128)(2,1)S(1)} %collective-permute-done.refs_0_, bf16[192,1024]{1,0:T(8,128)(2,1)S(1)} %collective-permute-done.3.refs_1_, bf16[192,1024]{1,0:T(8,128)(2,1)S(1)} %collective-permute-done.4.refs_2_, ...), custom_call_target="tpu_custom_call" | custom-call | tf_op jit(solution)/shard_map/expert_math/pallas_call | solution.py:291
  88.3 0.4 collective-permute-start.26
  88.7 0.1 add_convert_fusion.1
  88.9 11.5 %collective-permute-done.21.refs_0_ = bf16[48,4096]{1,0:T(8,128)(2,1)S(1)} collective-permute-done((bf16[48,4096]{1,0:T(8,128)(2,1)S(1)}, bf16[48,4096]{1,0:T(8,128)(2,1)S(1)}, u32[]{:S(2)}, u32[]{:S(2)}) %collective-permute-start.21) | collective-permute-done | bytes 393248 | tf_op jit(solution)/shard_map/ppermute | solution.py:242
  100.4 0.6 collective-permute-start.28
  101.0 0.1 add_convert_fusion
  101.2 2.1 %collective-permute-done.23.refs_1_ = bf16[48,4096]{1,0:T(8,128)(2,1)S(1)} collective-permute-done((bf16[48,4096]{1,0:T(8,128)(2,1)S(1)}, bf16[48,4096]{1,0:T(8,128)(2,1)S(1)}, u32[]{:S(2)}, u32[]{:S(2)}) %collective-permute-start.23) | collective-permute-done | bytes 393248 | tf_op jit(solution)/shard_map/ppermute | solution.py:242
  103.3 0.9 collective-permute-start.29
  104.2 16.2 %collective-permute-done.27.refs_2_ = bf16[48,4096]{1,0:T(8,128)(2,1)S(1)} collective-permute-done((bf16[48,4096]{1,0:T(8,128)(2,1)S(1)}, bf16[48,4096]{1,0:T(8,128)(2,1)S(1)}, u32[]{:S(2)}, u32[]{:S(2)}) %collective-permute-start.27) | collective-permute-done | bytes 393248 | tf_op jit(solution)/shard_map/ppermute | solution.py:242
  120.4 0.8 collective-permute-start.30
  121.1 1.3 %collective-permute-done.30.refs_5_ = bf16[48,4096]{1,0:T(8,128)(2,1)S(1)} collective-permute-done((bf16[48,4096]{1,0:T(8,128)(2,1)S(1)}, bf16[48,4096]{1,0:T(8,128)(2,1)S(1)}, u32[]{:S(2)}, u32[]{:S(2)}) %collective-permute-start.30) | collective-permute-done | bytes 393248 | tf_op jit(solution)/shard_map/ppermute | solution.py:248
  122.5 1.9 %merge_rows.1 = (bf16[128,4096]{1,0:T(8,128)(2,1)}, bf16[128,4096]{1,0:T(8,128)(2,1)}) custom-call(bf16[48,4096]{1,0:T(8,128)(2,1)S(1)} %collective-permute-done.21.refs_0_, bf16[48,4096]{1,0:T(8,128)(2,1)S(1)} %collective-permute-done.23.refs_1_, bf16[48,4096]{1,0:T(8,128)(2,1)S(1)} %collective-permute-done.27.refs_2_, ...), custom_call_target="tpu_custom_call" | custom-call | tf_op jit(solution)/shard_map/merge_rows/pallas_call | solution.py:327
  (34 shorter events, 0.3 us)
Async XLA Ops:
  0.6 24.3 %copy-start.1 = (bf16[128,4096]{1,0:T(8,128)(2,1)S(1)}, bf16[128,4096]{1,0:T(8,128)(2,1)}, u32[]{:S(2)}) copy-start(bf16[128,4096]{1,0:T(8,128)(2,1)} %tokens_ref.1) | copy-start | bytes 3145732
  3.6 18.9 %collective-permute-start = (bf16[192,1024]{1,0:T(8,128)(2,1)}, bf16[192,1024]{1,0:T(8,128)(2,1)S(1)}, u32[]{:S(2)}, u32[]{:S(2)}) collective-permute-start(bf16[192,1024]{1,0:T(8,128)(2,1)} %get-tuple-element.30), channel_id=1, source_target_pairs={{0,6},{2,4},{4,2},{6,0},{1,7},{3,5},{5,3},{7,1},{8,14},{10,12},{12... | collective-permute-start | bytes 1179656 | tf_op jit(solution)/shard_map/ppermute | solution.py:242
  5.0 17.5 %collective-permute-start.1 = (bf16[192,1024]{1,0:T(8,128)(2,1)}, bf16[192,1024]{1,0:T(8,128)(2,1)S(1)}, u32[]{:S(2)}, u32[]{:S(2)}) collective-permute-start(bf16[192,1024]{1,0:T(8,128)(2,1)} %get-tuple-element.31.refs_4_), channel_id=1, source_target_pairs={{0,8},{8,0},{16,24},{24,16},{1,9},{9,1},{17,25},{25,17},{2,10},{10... | collective-permute-start | bytes 1179656 | tf_op jit(solution)/shard_map/ppermute | solution.py:245
  6.2 16.3 %collective-permute-start.2 = (bf16[192,1024]{1,0:T(8,128)(2,1)}, bf16[192,1024]{1,0:T(8,128)(2,1)S(1)}, u32[]{:S(2)}, u32[]{:S(2)}) collective-permute-start(bf16[192,1024]{1,0:T(8,128)(2,1)} %get-tuple-element.31.refs_4_), channel_id=1, source_target_pairs={{0,16},{8,24},{16,0},{24,8},{1,17},{9,25},{17,1},{25,9},{2,18},{10... | collective-permute-start | bytes 1179656 | tf_op jit(solution)/shard_map/ppermute | solution.py:245
  7.4 20.4 %collective-permute-start.6 = (bf16[192,1024]{1,0:T(8,128)(2,1)}, bf16[192,1024]{1,0:T(8,128)(2,1)S(1)}, u32[]{:S(2)}, u32[]{:S(2)}) collective-permute-start(bf16[192,1024]{1,0:T(8,128)(2,1)} %get-tuple-element.31.refs_4_), channel_id=1, source_target_pairs={{0,24},{8,16},{16,8},{24,0},{1,25},{9,17},{17,9},{25,1},{2,26},{10... | collective-permute-start | bytes 1179656 | tf_op jit(solution)/shard_map/ppermute | solution.py:245
  7.6 20.2 %collective-permute-start.7 = (bf16[192,1024]{1,0:T(8,128)(2,1)}, bf16[192,1024]{1,0:T(8,128)(2,1)S(1)}, u32[]{:S(2)}, u32[]{:S(2)}) collective-permute-start(bf16[192,1024]{1,0:T(8,128)(2,1)} %get-tuple-element.33), channel_id=1, source_target_pairs={{0,2},{2,0},{4,6},{6,4},{1,3},{3,1},{5,7},{7,5},{8,10},{10,8},{12,... | collective-permute-start | bytes 1179656 | tf_op jit(solution)/shard_map/ppermute | solution.py:242
  22.5 8.1 %collective-permute-start.4 = (bf16[192,1024]{1,0:T(8,128)(2,1)S(1)}, bf16[192,1024]{1,0:T(8,128)(2,1)S(1)}, u32[]{:S(2)}, u32[]{:S(2)}) collective-permute-start(bf16[192,1024]{1,0:T(8,128)(2,1)S(1)} %collective-permute-done.refs_0_), channel_id=1, source_target_pairs={{0,16},{8,24},{16,0},{24,8},{1,17},{9,25},{17,1},{25,9},{2,18},{10... | collective-permute-start | bytes 1179656 | tf_op jit(solution)/shard_map/ppermute | solution.py:245
  23.7 1.2 copy-start.3
  23.7 15.1 %collective-permute-start.11 = (bf16[192,1024]{1,0:T(8,128)(2,1)}, bf16[192,1024]{1,0:T(8,128)(2,1)S(1)}, u32[]{:S(2)}, u32[]{:S(2)}) collective-permute-start(bf16[192,1024]{1,0:T(8,128)(2,1)} %get-tuple-element.37), channel_id=1, source_target_pairs={{0,4},{2,6},{4,0},{6,2},{1,5},{3,7},{5,1},{7,3},{8,12},{10,14},{12... | collective-permute-start | bytes 1179656 | tf_op jit(solution)/shard_map/ppermute | solution.py:242
  23.7 18.1 %collective-permute-start.3 = (bf16[192,1024]{1,0:T(8,128)(2,1)S(1)}, bf16[192,1024]{1,0:T(8,128)(2,1)S(1)}, u32[]{:S(2)}, u32[]{:S(2)}) collective-permute-start(bf16[192,1024]{1,0:T(8,128)(2,1)S(1)} %collective-permute-done.refs_0_), channel_id=1, source_target_pairs={{0,8},{8,0},{16,24},{24,16},{1,9},{9,1},{17,25},{25,17},{2,10},{10... | collective-permute-start | bytes 1179656 | tf_op jit(solution)/shard_map/ppermute | solution.py:245
  25.0 1.2 copy-start.2
  27.9 14.1 %collective-permute-start.8 = (bf16[192,1024]{1,0:T(8,128)(2,1)S(1)}, bf16[192,1024]{1,0:T(8,128)(2,1)S(1)}, u32[]{:S(2)}, u32[]{:S(2)}) collective-permute-start(bf16[192,1024]{1,0:T(8,128)(2,1)S(1)} %collective-permute-done.7.refs_8_), channel_id=1, source_target_pairs={{0,8},{8,0},{16,24},{24,16},{1,9},{9,1},{17,25},{25,17},{2,10},{10... | collective-permute-start | bytes 1179656 | tf_op jit(solution)/shard_map/ppermute | solution.py:245
  28.6 13.3 %collective-permute-start.9 = (bf16[192,1024]{1,0:T(8,128)(2,1)S(1)}, bf16[192,1024]{1,0:T(8,128)(2,1)S(1)}, u32[]{:S(2)}, u32[]{:S(2)}) collective-permute-start(bf16[192,1024]{1,0:T(8,128)(2,1)S(1)} %collective-permute-done.7.refs_8_), channel_id=1, source_target_pairs={{0,16},{8,24},{16,0},{24,8},{1,17},{9,25},{17,1},{25,9},{2,18},{10... | collective-permute-start | bytes 1179656 | tf_op jit(solution)/shard_map/ppermute | solution.py:245
  30.6 14.5 %collective-permute-start.5 = (bf16[192,1024]{1,0:T(8,128)(2,1)S(1)}, bf16[192,1024]{1,0:T(8,128)(2,1)S(1)}, u32[]{:S(2)}, u32[]{:S(2)}) collective-permute-start(bf16[192,1024]{1,0:T(8,128)(2,1)S(1)} %collective-permute-done.4.refs_2_), channel_id=1, source_target_pairs={{0,8},{8,0},{16,24},{24,16},{1,9},{9,1},{17,25},{25,17},{2,10},{10... | collective-permute-start | bytes 1179656 | tf_op jit(solution)/shard_map/ppermute | solution.py:245
  38.9 20.0 %collective-permute-start.16 = (bf16[48,4096]{1,0:T(8,128)(2,1)S(1)}, bf16[48,4096]{1,0:T(8,128)(2,1)S(1)}, u32[]{:S(2)}, u32[]{:S(2)}) collective-permute-start(bf16[48,4096]{1,0:T(8,128)(2,1)S(1)} %get-tuple-element.42), channel_id=1, source_target_pairs={{0,4},{2,6},{4,0},{6,2},{1,5},{3,7},{5,1},{7,3},{8,12},{10,14},{12... | collective-permute-start | bytes 1179656 | tf_op jit(solution)/shard_map/ppermute | solution.py:242
  41.8 24.3 %copy-start = (bf16[192,1024]{1,0:T(8,128)(2,1)S(1)}, bf16[192,1024]{1,0:T(8,128)(2,1)}, u32[]{:S(2)}) copy-start(bf16[192,1024]{1,0:T(8,128)(2,1)} %get-tuple-element.31.refs_4_) | copy-start | bytes 1179652
  41.9 17.5 %collective-permute-start.17 = (bf16[48,4096]{1,0:T(8,128)(2,1)S(1)}, bf16[48,4096]{1,0:T(8,128)(2,1)S(1)}, u32[]{:S(2)}, u32[]{:S(2)}) collective-permute-start(bf16[48,4096]{1,0:T(8,128)(2,1)S(1)} %get-tuple-element.44), channel_id=1, source_target_pairs={{0,2},{2,0},{4,6},{6,4},{1,3},{3,1},{5,7},{7,5},{8,10},{10,8},{12,... | collective-permute-start | bytes 1179656 | tf_op jit(solution)/shard_map/ppermute | solution.py:242
  41.9 18.5 %collective-permute-start.12 = (bf16[192,1024]{1,0:T(8,128)(2,1)S(1)}, bf16[192,1024]{1,0:T(8,128)(2,1)S(1)}, u32[]{:S(2)}, u32[]{:S(2)}) collective-permute-start(bf16[192,1024]{1,0:T(8,128)(2,1)S(1)} %collective-permute-done.11.refs_12_), channel_id=1, source_target_pairs={{0,8},{8,0},{16,24},{24,16},{1,9},{9,1},{17,25},{25,17},{2,10},{10... | collective-permute-start | bytes 1179656 | tf_op jit(solution)/shard_map/ppermute | solution.py:245
  44.2 16.2 %collective-permute-start.10 = (bf16[192,1024]{1,0:T(8,128)(2,1)S(1)}, bf16[192,1024]{1,0:T(8,128)(2,1)S(1)}, u32[]{:S(2)}, u32[]{:S(2)}) collective-permute-start(bf16[192,1024]{1,0:T(8,128)(2,1)S(1)} %collective-permute-done.8.refs_9_), channel_id=1, source_target_pairs={{0,16},{8,24},{16,0},{24,8},{1,17},{9,25},{17,1},{25,9},{2,18},{10... | collective-permute-start | bytes 1179656 | tf_op jit(solution)/shard_map/ppermute | solution.py:245
  45.1 15.3 %collective-permute-start.13 = (bf16[192,1024]{1,0:T(8,128)(2,1)S(1)}, bf16[192,1024]{1,0:T(8,128)(2,1)S(1)}, u32[]{:S(2)}, u32[]{:S(2)}) collective-permute-start(bf16[192,1024]{1,0:T(8,128)(2,1)S(1)} %collective-permute-done.11.refs_12_), channel_id=1, source_target_pairs={{0,16},{8,24},{16,0},{24,8},{1,17},{9,25},{17,1},{25,9},{2,18},{10... | collective-permute-start | bytes 1179656 | tf_op jit(solution)/shard_map/ppermute | solution.py:245
  58.9 7.3 %collective-permute-start.18 = (bf16[48,4096]{1,0:T(8,128)(2,1)S(1)}, bf16[48,4096]{1,0:T(8,128)(2,1)S(1)}, u32[]{:S(2)}, u32[]{:S(2)}) collective-permute-start(bf16[48,4096]{1,0:T(8,128)(2,1)S(1)} %collective-permute-done.16.refs_17_), channel_id=1, source_target_pairs={{0,1},{1,0},{2,3},{3,2},{4,5},{5,4},{6,7},{7,6},{8,9},{9,8},{10,11... | collective-permute-start | bytes 1179656 | tf_op jit(solution)/shard_map/ppermute | solution.py:248
  59.4 6.8 %collective-permute-start.19 = (bf16[48,4096]{1,0:T(8,128)(2,1)S(1)}, bf16[48,4096]{1,0:T(8,128)(2,1)S(1)}, u32[]{:S(2)}, u32[]{:S(2)}) collective-permute-start(bf16[48,4096]{1,0:T(8,128)(2,1)S(1)} %collective-permute-done.17.refs_18_), channel_id=1, source_target_pairs={{0,1},{1,0},{2,3},{3,2},{4,5},{5,4},{6,7},{7,6},{8,9},{9,8},{10,11... | collective-permute-start | bytes 1179656 | tf_op jit(solution)/shard_map/ppermute | solution.py:248
  60.4 5.2 %collective-permute-start.14 = (bf16[96,1024]{1,0:T(8,128)(2,1)S(1)}, bf16[96,1024]{1,0:T(8,128)(2,1)S(1)}, u32[]{:S(2)}, u32[]{:S(2)}) collective-permute-start(bf16[96,1024]{1,0:T(8,128)(2,1)S(1)} %slice.6), channel_id=1, source_target_pairs={{0,16},{8,24},{16,0},{24,8},{1,17},{9,25},{17,1},{25,9},{2,18},{10... | collective-permute-start | bytes 589832 | tf_op jit(solution)/shard_map/ppermute | solution.py:245
  61.2 4.9 %collective-permute-start.15 = (bf16[96,1024]{1,0:T(8,128)(2,1)S(1)}, bf16[96,1024]{1,0:T(8,128)(2,1)S(1)}, u32[]{:S(2)}, u32[]{:S(2)}) collective-permute-start(bf16[96,1024]{1,0:T(8,128)(2,1)S(1)} %slice.7), channel_id=1, source_target_pairs={{0,8},{8,0},{16,24},{24,16},{1,9},{9,1},{17,25},{25,17},{2,10},{10... | collective-permute-start | bytes 589832 | tf_op jit(solution)/shard_map/ppermute | solution.py:245
  63.1 17.3 %collective-permute-start.24 = (bf16[48,4096]{1,0:T(8,128)(2,1)S(1)}, bf16[48,4096]{1,0:T(8,128)(2,1)S(1)}, u32[]{:S(2)}, u32[]{:S(2)}) collective-permute-start(bf16[48,4096]{1,0:T(8,128)(2,1)S(1)} %get-tuple-element.50), channel_id=1, source_target_pairs={{0,6},{2,4},{4,2},{6,0},{1,7},{3,5},{5,3},{7,1},{8,14},{10,12},{12... | collective-permute-start | bytes 1179656 | tf_op jit(solution)/shard_map/ppermute | solution.py:242
  70.1 13.0 %collective-permute-start.20 = (bf16[48,4096]{1,0:T(8,128)(2,1)S(1)}, bf16[48,4096]{1,0:T(8,128)(2,1)S(1)}, u32[]{:S(2)}, u32[]{:S(2)}) collective-permute-start(bf16[48,4096]{1,0:T(8,128)(2,1)S(1)} %get-tuple-element.46), channel_id=1, source_target_pairs={{0,1},{1,0},{2,3},{3,2},{4,5},{5,4},{6,7},{7,6},{8,9},{9,8},{10,11... | collective-permute-start | bytes 1179656 | tf_op jit(solution)/shard_map/ppermute | solution.py:248
  74.5 14.2 %collective-permute-start.22 = (bf16[48,4096]{1,0:T(8,128)(2,1)S(1)}, bf16[48,4096]{1,0:T(8,128)(2,1)S(1)}, u32[]{:S(2)}, u32[]{:S(2)}) collective-permute-start(bf16[48,4096]{1,0:T(8,128)(2,1)S(1)} %get-tuple-element.48), channel_id=1, source_target_pairs={{0,1},{1,0},{2,3},{3,2},{4,5},{5,4},{6,7},{7,6},{8,9},{9,8},{10,11... | collective-permute-start | bytes 1179656 | tf_op jit(solution)/shard_map/ppermute | solution.py:248
  80.4 4.0 %collective-permute-start.25 = (bf16[48,4096]{1,0:T(8,128)(2,1)S(1)}, bf16[48,4096]{1,0:T(8,128)(2,1)S(1)}, u32[]{:S(2)}, u32[]{:S(2)}) collective-permute-start(bf16[48,4096]{1,0:T(8,128)(2,1)S(1)} %collective-permute-done.24.refs_17_), channel_id=1, source_target_pairs={{0,1},{1,0},{2,3},{3,2},{4,5},{5,4},{6,7},{7,6},{8,9},{9,8},{10,11... | collective-permute-start | bytes 1179656 | tf_op jit(solution)/shard_map/ppermute | solution.py:248
  83.1 17.3 %collective-permute-start.21 = (bf16[48,4096]{1,0:T(8,128)(2,1)S(1)}, bf16[48,4096]{1,0:T(8,128)(2,1)S(1)}, u32[]{:S(2)}, u32[]{:S(2)}) collective-permute-start(bf16[48,4096]{1,0:T(8,128)(2,1)S(1)} %add_convert_fusion.2), channel_id=1, source_target_pairs={{0,4},{2,6},{4,0},{6,2},{1,5},{3,7},{5,1},{7,3},{8,12},{10,14},{12... | collective-permute-start | bytes 1179656 | tf_op jit(solution)/shard_map/ppermute | solution.py:242
  88.3 12.7 %collective-permute-start.26 = (bf16[48,4096]{1,0:T(8,128)(2,1)S(1)}, bf16[48,4096]{1,0:T(8,128)(2,1)S(1)}, u32[]{:S(2)}, u32[]{:S(2)}) collective-permute-start(bf16[48,4096]{1,0:T(8,128)(2,1)S(1)} %get-tuple-element.54), channel_id=1, source_target_pairs={{0,1},{1,0},{2,3},{3,2},{4,5},{5,4},{6,7},{7,6},{8,9},{9,8},{10,11... | collective-permute-start | bytes 1179656 | tf_op jit(solution)/shard_map/ppermute | solution.py:248
  88.8 14.4 %collective-permute-start.23 = (bf16[48,4096]{1,0:T(8,128)(2,1)S(1)}, bf16[48,4096]{1,0:T(8,128)(2,1)S(1)}, u32[]{:S(2)}, u32[]{:S(2)}) collective-permute-start(bf16[48,4096]{1,0:T(8,128)(2,1)S(1)} %add_convert_fusion.1), channel_id=1, source_target_pairs={{0,2},{2,0},{4,6},{6,4},{1,3},{3,1},{5,7},{7,5},{8,10},{10,8},{12,... | collective-permute-start | bytes 1179656 | tf_op jit(solution)/shard_map/ppermute | solution.py:242
  100.4 2.8 %collective-permute-start.28 = (bf16[48,4096]{1,0:T(8,128)(2,1)S(1)}, bf16[48,4096]{1,0:T(8,128)(2,1)S(1)}, u32[]{:S(2)}, u32[]{:S(2)}) collective-permute-start(bf16[48,4096]{1,0:T(8,128)(2,1)S(1)} %collective-permute-done.21.refs_0_), channel_id=1, source_target_pairs={{0,1},{1,0},{2,3},{3,2},{4,5},{5,4},{6,7},{7,6},{8,9},{9,8},{10,11... | collective-permute-start | bytes 1179656 | tf_op jit(solution)/shard_map/ppermute | solution.py:248
  101.1 19.2 %collective-permute-start.27 = (bf16[48,4096]{1,0:T(8,128)(2,1)S(1)}, bf16[48,4096]{1,0:T(8,128)(2,1)S(1)}, u32[]{:S(2)}, u32[]{:S(2)}) collective-permute-start(bf16[48,4096]{1,0:T(8,128)(2,1)S(1)} %add_convert_fusion), channel_id=1, source_target_pairs={{0,6},{2,4},{4,2},{6,0},{1,7},{3,5},{5,3},{7,1},{8,14},{10,12},{12... | collective-permute-start | bytes 1179656 | tf_op jit(solution)/shard_map/ppermute | solution.py:242
  103.3 17.1 %collective-permute-start.29 = (bf16[48,4096]{1,0:T(8,128)(2,1)S(1)}, bf16[48,4096]{1,0:T(8,128)(2,1)S(1)}, u32[]{:S(2)}, u32[]{:S(2)}) collective-permute-start(bf16[48,4096]{1,0:T(8,128)(2,1)S(1)} %collective-permute-done.23.refs_1_), channel_id=1, source_target_pairs={{0,1},{1,0},{2,3},{3,2},{4,5},{5,4},{6,7},{7,6},{8,9},{9,8},{10,11... | collective-permute-start | bytes 1179656 | tf_op jit(solution)/shard_map/ppermute | solution.py:248
  104.2 17.0 %collective-permute-start.31 = (bf16[96,4096]{1,0:T(8,128)(2,1)S(1)}, bf16[96,4096]{1,0:T(8,128)(2,1)S(1)}, u32[]{:S(2)}, u32[]{:S(2)}) collective-permute-start(bf16[96,4096]{1,0:T(8,128)(2,1)S(1)} %get-tuple-element.57.refs_6_), channel_id=1, source_target_pairs={{0,1},{1,0},{2,3},{3,2},{4,5},{5,4},{6,7},{7,6},{8,9},{9,8},{10,11... | collective-permute-start | bytes 2359304 | tf_op jit(solution)/shard_map/ppermute | solution.py:248
  120.4 2.1 %collective-permute-start.30 = (bf16[48,4096]{1,0:T(8,128)(2,1)S(1)}, bf16[48,4096]{1,0:T(8,128)(2,1)S(1)}, u32[]{:S(2)}, u32[]{:S(2)}) collective-permute-start(bf16[48,4096]{1,0:T(8,128)(2,1)S(1)} %collective-permute-done.27.refs_2_), channel_id=1, source_target_pairs={{0,1},{1,0},{2,3},{3,2},{4,5},{5,4},{6,7},{7,6},{8,9},{9,8},{10,11... | collective-permute-start | bytes 1179656 | tf_op jit(solution)/shard_map/ppermute | solution.py:248

commit v5 on v4

--- a/solution.py
+++ b/solution.py
@@ -10,7 +10,6 @@
 BF16 = jnp.bfloat16
 F32 = jnp.float32
 LAST = (((1,), (1,)), ((), ()))
-FIRST = (((0,), (0,)), ((), ()))
 VMEM_LIMIT = 16 * 1024 * 1024
 MOST_VMEM = 60 * 1024 * 1024
 
@@ -46,13 +45,14 @@
             moved = pltpu.roll(row, shift, 1)
             picks = jnp.where((lane >= start) & (lane < start + run), moved, picks)
     local = jnp.where(picks >= 0, picks - source * rows, -1)[0:1, :wide]
-    neuron = lax.broadcasted_iota(jnp.int32, (rows, wide), 0)
-    table = jnp.where(neuron == local, 1.0, 0.0).astype(BF16)
+    down = jnp.transpose(jnp.broadcast_to(local, (wide, wide)))[:, :1]
+    neuron = lax.broadcasted_iota(jnp.int32, (wide, rows), 1)
+    table = jnp.where(neuron == down, 1.0, 0.0).astype(BF16)
     per = halves * run
     sent = []
     for w, ref in enumerate(weight_refs):
         copies[w + 1].wait()
-        chosen_ref[w] = lax.dot_general(table, ref[...], FIRST, preferred_element_type=F32).astype(BF16)
+        chosen_ref[w] = jnp.dot(table, ref[...], preferred_element_type=F32).astype(BF16)
         for k in range(n_experts):
             part, place = chosen_ref.at[w, pl.ds(k * per, per)], out_refs[k].at[pl.ds(w * per, per)]
             sent.append(pltpu.make_async_copy(part, place, out_sems.at[w, k]))
@@ -71,15 +71,17 @@
     position = jnp.sum(before, axis=0, keepdims=True)
     slot = (routes ^ lax.axis_index("expert")) * capacity + position
     number = lax.broadcasted_iota(jnp.int32, (n_experts * capacity, tokens), 0)
-    return jnp.where(number == slot, 1.0, 0.0).astype(BF16)
+    return jnp.where(number == slot, 1.0, 0.0)
 
 
 def dispatch_kernel(n_experts, capacity, routes_ref, tokens_ref, cotangent_ref, *refs):
-    out_refs, local_ref, table_ref = refs[:n_experts], *refs[n_experts:]
+    out_refs, local_ref, home_ref, table_ref = refs[:n_experts], *refs[n_experts:]
 
     @pl.when(pl.program_id(0) == 0)
     def _():
-        table_ref[...] = slot_table(routes_ref[...], n_experts, capacity)
+        table = slot_table(routes_ref[...], n_experts, capacity)
+        table_ref[...] = table.astype(BF16)
+        home_ref[...] = jnp.transpose(table).astype(BF16)
 
     def rows(source_ref, count):
         return jnp.dot(table_ref[:count], source_ref[...], preferred_element_type=F32).astype(BF16)
@@ -98,8 +100,8 @@
 def merge_kernel(order, capacity, blocks, *refs):
     n_experts, count = len(order) + 1, len(order)
     mine_refs, other_refs = refs[:count], refs[count:2 * count]
-    kept_ref, got_ref, routes_ref, out_ref, grad_ref, held_ref, sems = refs[2 * count:]
-    table = slot_table(routes_ref[...], n_experts, capacity)
+    kept_ref, got_ref, table_ref, out_ref, grad_ref, held_ref, sems = refs[2 * count:]
+    table = table_ref[...]
     width = out_ref.shape[1] // blocks
     first = lax.axis_index("tensor") == 0
     copies = []
@@ -116,7 +118,7 @@
 
         mine, other = rows(mine_refs, 0), rows(other_refs, 1)
         for w, (a, b, ref) in enumerate(((mine, other, out_ref), (other, mine, grad_ref))):
-            total = lax.dot_general(table, jnp.where(first, a, b), FIRST, preferred_element_type=F32)
+            total = jnp.dot(table, jnp.where(first, a, b), preferred_element_type=F32)
             held_ref[w, :, at] = total.astype(BF16)
             copies.append(pltpu.make_async_copy(held_ref.at[w, :, at], ref.at[:, at], sems.at[w, i]))
             copies[-1].start()
@@ -221,16 +223,18 @@
 
     route_row = routes.reshape(1, tok_count)
     block = width // 4
-    *sent, local = pl.pallas_call(
+    *sent, local, home_table = pl.pallas_call(
         functools.partial(dispatch_kernel, n_experts, capacity),
         grid=(width // block,),
-        out_shape=[shape((capacity, width), BF16)] * (n_experts + 1),
+        out_shape=[shape((capacity, width), BF16)] * (n_experts + 1)
+        + [shape((tok_count, n_experts * capacity), BF16)],
         in_specs=[
             pl.BlockSpec((1, tok_count), lambda i: (0, 0)),
             pl.BlockSpec((tok_count, block), lambda i: (0, i)),
             pl.BlockSpec((tok_count, block), lambda i: (0, i)),
         ],
-        out_specs=[pl.BlockSpec((capacity, block), lambda i: (0, i))] * (n_experts + 1),
+        out_specs=[pl.BlockSpec((capacity, block), lambda i: (0, i))] * (n_experts + 1)
+        + [pl.BlockSpec((tok_count, n_experts * capacity), lambda i: (0, 0))],
         scratch_shapes=[pltpu.VMEM((n_experts * capacity, tok_count), BF16)],
         compiler_params=params,
         name="dispatch_rows",
@@ -262,23 +266,23 @@
     pieces0 = direct(sent_w[0])
     (sent_w2,) = after([sent_w[2]], [chunk3])
     chunk2 = planes(sent_w2, 2)
-    (chunk1,) = after([chunk1], [*pieces0[1:], local])
+    (chunk1,) = after([chunk1], pieces0[1:])
     pieces1 = near_far(chunk1)
-    (chunk3,) = after([chunk3], pieces0[1:3])
+    (chunk3,) = after([chunk3], [*pieces0[1:3], local])
     pieces3 = near_far(chunk3)
     (held,) = after([chunk2], pieces3[1:] + pieces1[1:])
     pieces2 = near_far(held)
     for k, awaited in ((2, chunk2), (1, chunk2), (3, None)):
         (row,) = after([sent[k]], [rows[2] if awaited is None else awaited])
         rows[k] = planes(row, k)
-    pieces1.append(spread(pieces1[1], 2))
-    pieces3.append(spread(pieces3[2], 1))
+    pieces3.append(spread(pieces3[1], 2))
+    pieces1.append(spread(pieces1[2], 1))
     held2 = after(pieces2[1:], [pieces1[3], pieces3[3]])
     pieces2 += diagonal([pieces2[0], *held2])
     for k in (2, 1, 3):
         others[k] = swapped(rows[k])
 
-    weights = (pieces3, pieces0, pieces1, pieces2)
+    weights = (pieces3, pieces2, pieces0, pieces1)
     mine, other, returned = {}, {}, []
     for members in ((2, 1), (3, 0)):
         count = len(members)
@@ -335,7 +339,7 @@
             ],
             compiler_params=params,
             name="merge_rows",
-        )(*[mine[k] for k in order], *[other[k] for k in order], *stayed, route_row)
+        )(*[mine[k] for k in order], *[other[k] for k in order], *stayed, home_table)
     )
 
 

time: 125 us -> 124 us (level)
  starting transfers between devices: 32.6 us -> 29.6 us
  waiting for transfers between devices: 75.2 us -> 77.7 us
    ppermute x13, waiting for transfers between devices: 5.45 us -> 11.2 us  [spread(): return lax.ppermute(chunk, 'dp', flips(n_dp, step))]
    ppermute x13, starting transfers between devices: 14.3 us -> 10.5 us  [spread(): return lax.ppermute(chunk, 'dp', flips(n_dp, step))]
    ppermute x9, waiting for transfers between devices: 67.2 us -> 63.9 us  [planes(): return lax.ppermute(chunk, 'expert', flips(n_experts, k))]
where the time goes in v5:
time: 124 us
  waiting for transfers between devices  77.7 us (63%)
  starting transfers between devices  29.6 us (24%)
  Pallas kernels  14.2 us (11%)
  local copies, waits for them, and re-layouts  1.27 us (1%)
    ppermute x9, waiting for transfers between devices, planes(): return lax.ppermute(chunk, 'expert', flips(n_experts, k))  63.9 us
    ppermute x10, starting transfers between devices, swapped(): return lax.ppermute(chunk, 'tensor', swap)  11.5 us
    ppermute x13, waiting for transfers between devices, spread(): return lax.ppermute(chunk, 'dp', flips(n_dp, step))  11.2 us
    ppermute x13, starting transfers between devices, spread(): return lax.ppermute(chunk, 'dp', flips(n_dp, step))  10.5 us
    pallas_call x2, Pallas kernels, aligned_plan(): pl.pallas_call(functools.partial(expert_kernel, [len(pieces) for pieces i...  7.77 us
    ppermute x9, starting transfers between devices, planes(): return lax.ppermute(chunk, 'expert', flips(n_experts, k))  7.54 us
    pallas_call x1, Pallas kernels, aligned_plan(): pl.pallas_call(functools.partial(select_kernel, n_experts, halves, shards...  2.96 us
    ppermute x10, waiting for transfers between devices, swapped(): return lax.ppermute(chunk, 'tensor', swap)  2.54 us
  transfers between devices with their start and end apart: 32, of which 13 were waited for; matrix products, arithmetic and copies ran while one was open for 0% of the time, Pallas kernels for 8%

profile of v5, /device:TPU:9, one launch (start us, length us, event | category | flops | bytes accessed | tf_op | source)
XLA Modules:
  0.0 123.8 jit_solution(12815621567537184002)
XLA Ops:
  0.6 3.0 %select_rows.1 = (bf16[192,1024]{1,0:T(8,128)(2,1)}, bf16[192,1024]{1,0:T(8,128)(2,1)}, bf16[192,1024]{1,0:T(8,128)(2,1)}, bf16[192,1024]{1,0:T(8,128)(2,1)}) custom-call(s32[4,512]{1,0:T(4,128)} %cluster_hbm.1, bf16[231,1024]{1,0:T(8,128)(2,1)} %gate_hbm.1, bf16[231,1024]{1,0:T(8,128)(2,1)} %up_hbm.1, bf16[231,1024]{1,0:T(8,128)(2,1)} %down_hbm.1), custom_call_target="tpu_custom_call" | custom-call | tf_op jit(solution)/shard_map/select_rows/pallas_call | solution.py:208
  3.6 1.4 %collective-permute-start = (bf16[192,1024]{1,0:T(8,128)(2,1)}, bf16[192,1024]{1,0:T(8,128)(2,1)S(1)}, u32[]{:S(2)}, u32[]{:S(2)}) collective-permute-start(bf16[192,1024]{1,0:T(8,128)(2,1)} %get-tuple-element.31), channel_id=1, source_target_pairs={{0,6},{2,4},{4,2},{6,0},{1,7},{3,5},{5,3},{7,1},{8,14},{10,12},{12... | collective-permute-start | bytes 1179656 | tf_op jit(solution)/shard_map/ppermute | solution.py:246
  5.0 1.2 collective-permute-start.1
  6.2 1.2 %collective-permute-start.2 = (bf16[192,1024]{1,0:T(8,128)(2,1)}, bf16[192,1024]{1,0:T(8,128)(2,1)S(1)}, u32[]{:S(2)}, u32[]{:S(2)}) collective-permute-start(bf16[192,1024]{1,0:T(8,128)(2,1)} %get-tuple-element.32.refs_9_), channel_id=1, source_target_pairs={{0,16},{8,24},{16,0},{24,8},{1,17},{9,25},{17,1},{25,9},{2,18},{10... | collective-permute-start | bytes 1179656 | tf_op jit(solution)/shard_map/ppermute | solution.py:249
  7.4 0.2 collective-permute-start.8
  7.6 2.2 %collective-permute-start.7 = (bf16[192,1024]{1,0:T(8,128)(2,1)}, bf16[192,1024]{1,0:T(8,128)(2,1)S(1)}, u32[]{:S(2)}, u32[]{:S(2)}) collective-permute-start(bf16[192,1024]{1,0:T(8,128)(2,1)} %get-tuple-element.37), channel_id=1, source_target_pairs={{0,2},{2,0},{4,6},{6,4},{1,3},{3,1},{5,7},{7,5},{8,10},{10,8},{12,... | collective-permute-start | bytes 1179656 | tf_op jit(solution)/shard_map/ppermute | solution.py:246
  9.8 1.2 copy-done.2
  11.0 1.8 %dispatch_rows.1 = (bf16[48,4096]{1,0:T(8,128)(2,1)S(1)}, bf16[48,4096]{1,0:T(8,128)(2,1)S(1)}, bf16[48,4096]{1,0:T(8,128)(2,1)S(1)}, bf16[48,4096]{1,0:T(8,128)...) custom-call(s32[1,128]{1,0:T(1,128)S(1)} %bitcast.1, bf16[128,4096]{1,0:T(8,128)(2,1)S(1)} %copy-done.1, ...), custom_call_target="tpu_custom_call" | custom-call | tf_op jit(solution)/shard_map/dispatch_rows/pallas_call | solution.py:226
  12.8 9.6 %collective-permute-done.refs_0_ = bf16[192,1024]{1,0:T(8,128)(2,1)S(1)} collective-permute-done((bf16[192,1024]{1,0:T(8,128)(2,1)}, bf16[192,1024]{1,0:T(8,128)(2,1)S(1)}, u32[]{:S(2)}, u32[]{:S(2)}) %collective-permute-start) | collective-permute-done | bytes 393248 | tf_op jit(solution)/shard_map/ppermute | solution.py:246
  22.5 1.2 collective-permute-start.3
  23.7 1.2 %collective-permute-start.4 = (bf16[192,1024]{1,0:T(8,128)(2,1)S(1)}, bf16[192,1024]{1,0:T(8,128)(2,1)S(1)}, u32[]{:S(2)}, u32[]{:S(2)}) collective-permute-start(bf16[192,1024]{1,0:T(8,128)(2,1)S(1)} %collective-permute-done.refs_0_), channel_id=1, source_target_pairs={{0,16},{8,24},{16,0},{24,8},{1,17},{9,25},{17,1},{25,9},{2,18},{10... | collective-permute-start | bytes 1179656 | tf_op jit(solution)/shard_map/ppermute | solution.py:249
  25.0 0.7 collective-permute-start.9
  25.7 1.2 collective-permute-start.10
  26.9 2.9 %collective-permute-done.3.refs_1_ = bf16[192,1024]{1,0:T(8,128)(2,1)S(1)} collective-permute-done((bf16[192,1024]{1,0:T(8,128)(2,1)S(1)}, bf16[192,1024]{1,0:T(8,128)(2,1)S(1)}, u32[]{:S(2)}, u32[]{:S(2)}) %collective-permute-start.3) | collective-permute-done | bytes 393248 | tf_op jit(solution)/shard_map/ppermute | solution.py:249
  29.8 0.7 collective-permute-start.5
  30.5 8.5 %collective-permute-done.6.refs_4_ = bf16[192,1024]{1,0:T(8,128)(2,1)S(1)} collective-permute-done((bf16[192,1024]{1,0:T(8,128)(2,1)S(1)}, bf16[192,1024]{1,0:T(8,128)(2,1)S(1)}, u32[]{:S(2)}, u32[]{:S(2)}) %collective-permute-start.6) | collective-permute-done | bytes 393248 | tf_op jit(solution)/shard_map/ppermute | solution.py:246
  39.0 3.1 %collective-permute-start.16 = (bf16[48,4096]{1,0:T(8,128)(2,1)S(1)}, bf16[48,4096]{1,0:T(8,128)(2,1)S(1)}, u32[]{:S(2)}, u32[]{:S(2)}) collective-permute-start(bf16[48,4096]{1,0:T(8,128)(2,1)S(1)} %get-tuple-element.43), channel_id=1, source_target_pairs={{0,4},{2,6},{4,0},{6,2},{1,5},{3,7},{5,1},{7,3},{8,12},{10,14},{12... | collective-permute-start | bytes 1179656 | tf_op jit(solution)/shard_map/ppermute | solution.py:246
  42.1 0.6 collective-permute-start.17
  42.7 0.2 collective-permute-start.11
  43.0 1.1 collective-permute-start.12
  44.1 3.6 %collective-permute-done.5.refs_3_ = bf16[192,1024]{1,0:T(8,128)(2,1)S(1)} collective-permute-done((bf16[192,1024]{1,0:T(8,128)(2,1)S(1)}, bf16[192,1024]{1,0:T(8,128)(2,1)S(1)}, u32[]{:S(2)}, u32[]{:S(2)}) %collective-permute-start.5) | collective-permute-done | bytes 393248 | tf_op jit(solution)/shard_map/ppermute | solution.py:249
  47.7 11.5 %collective-permute-done.16.refs_17_ = bf16[48,4096]{1,0:T(8,128)(2,1)S(1)} collective-permute-done((bf16[48,4096]{1,0:T(8,128)(2,1)S(1)}, bf16[48,4096]{1,0:T(8,128)(2,1)S(1)}, u32[]{:S(2)}, u32[]{:S(2)}) %collective-permute-start.16) | collective-permute-done | bytes 393248 | tf_op jit(solution)/shard_map/ppermute | solution.py:246
  59.2 0.7 collective-permute-start.18
  59.9 1.3 %collective-permute-start.19 = (bf16[48,4096]{1,0:T(8,128)(2,1)S(1)}, bf16[48,4096]{1,0:T(8,128)(2,1)S(1)}, u32[]{:S(2)}, u32[]{:S(2)}) collective-permute-start(bf16[48,4096]{1,0:T(8,128)(2,1)S(1)} %collective-permute-done.17.refs_18_), channel_id=1, source_target_pairs={{0,1},{1,0},{2,3},{3,2},{4,5},{5,4},{6,7},{7,6},{8,9},{9,8},{10,11... | collective-permute-start | bytes 1179656 | tf_op jit(solution)/shard_map/ppermute | solution.py:252
  61.2 1.3 %collective-permute-start.14 = (bf16[96,1024]{1,0:T(8,128)(2,1)S(1)}, bf16[96,1024]{1,0:T(8,128)(2,1)S(1)}, u32[]{:S(2)}, u32[]{:S(2)}) collective-permute-start(bf16[96,1024]{1,0:T(8,128)(2,1)S(1)} %slice.6), channel_id=1, source_target_pairs={{0,16},{8,24},{16,0},{24,8},{1,17},{9,25},{17,1},{25,9},{2,18},{10... | collective-permute-start | bytes 589832 | tf_op jit(solution)/shard_map/ppermute | solution.py:249
  62.6 0.1 collective-permute-start.24
  62.7 3.1 %collective-permute-done.14.refs_7_ = bf16[96,1024]{1,0:T(8,128)(2,1)S(1)} collective-permute-done((bf16[96,1024]{1,0:T(8,128)(2,1)S(1)}, bf16[96,1024]{1,0:T(8,128)(2,1)S(1)}, u32[]{:S(2)}, u32[]{:S(2)}) %collective-permute-start.14) | collective-permute-done | bytes 196640 | tf_op jit(solution)/shard_map/ppermute | solution.py:249
  65.8 1.6 %collective-permute-done.15.refs_8_ = bf16[96,1024]{1,0:T(8,128)(2,1)S(1)} collective-permute-done((bf16[96,1024]{1,0:T(8,128)(2,1)S(1)}, bf16[96,1024]{1,0:T(8,128)(2,1)S(1)}, u32[]{:S(2)}, u32[]{:S(2)}) %collective-permute-start.15) | collective-permute-done | bytes 196640 | tf_op jit(solution)/shard_map/ppermute | solution.py:249
  67.5 3.9 %expert_math.2 = (bf16[48,4096]{1,0:T(8,128)(2,1)S(1)}, bf16[48,4096]{1,0:T(8,128)(2,1)S(1)}, bf16[48,4096]{1,0:T(8,128)(2,1)S(1)}, bf16[48,4096]{1,0:T(8,128)(2,1)S(1)}) custom-call(bf16[192,1024]{1,0:T(8,128)(2,1)S(1)} %collective-permute-done.refs_0_, bf16[192,1024]{1,0:T(8,128)(2,1)S(1)} %collective-permute-done.3.refs_1_, ...), custom_call_target="tpu_custom_call" | custom-call | tf_op jit(solution)/shard_map/expert_math/pallas_call | solution.py:295
  71.4 4.1 %collective-permute-start.20 = (bf16[48,4096]{1,0:T(8,128)(2,1)S(1)}, bf16[48,4096]{1,0:T(8,128)(2,1)S(1)}, u32[]{:S(2)}, u32[]{:S(2)}) collective-permute-start(bf16[48,4096]{1,0:T(8,128)(2,1)S(1)} %get-tuple-element.47), channel_id=1, source_target_pairs={{0,1},{1,0},{2,3},{3,2},{4,5},{5,4},{6,7},{7,6},{8,9},{9,8},{10,11... | collective-permute-start | bytes 1179656 | tf_op jit(solution)/shard_map/ppermute | solution.py:252
  75.4 0.1 collective-permute-start.22
  75.5 4.5 %collective-permute-done.24.refs_17_ = bf16[48,4096]{1,0:T(8,128)(2,1)S(1)} collective-permute-done((bf16[48,4096]{1,0:T(8,128)(2,1)S(1)}, bf16[48,4096]{1,0:T(8,128)(2,1)S(1)}, u32[]{:S(2)}, u32[]{:S(2)}) %collective-permute-start.24) | collective-permute-done | bytes 393248 | tf_op jit(solution)/shard_map/ppermute | solution.py:246
  80.0 2.7 %collective-permute-start.25 = (bf16[48,4096]{1,0:T(8,128)(2,1)S(1)}, bf16[48,4096]{1,0:T(8,128)(2,1)S(1)}, u32[]{:S(2)}, u32[]{:S(2)}) collective-permute-start(bf16[48,4096]{1,0:T(8,128)(2,1)S(1)} %collective-permute-done.24.refs_17_), channel_id=1, source_target_pairs={{0,1},{1,0},{2,3},{3,2},{4,5},{5,4},{6,7},{7,6},{8,9},{9,8},{10,11... | collective-permute-start | bytes 1179656 | tf_op jit(solution)/shard_map/ppermute | solution.py:252
  82.7 0.1 add_convert_fusion.2
  82.8 1.2 collective-permute-done.25.refs_19_
  84.0 3.9 %expert_math.3 = (bf16[48,4096]{1,0:T(8,128)(2,1)S(1)}, bf16[48,4096]{1,0:T(8,128)(2,1)S(1)}, bf16[96,4096]{1,0:T(8,128)(2,1)S(1)}) custom-call(bf16[192,1024]{1,0:T(8,128)(2,1)S(1)} %collective-permute-done.refs_0_, bf16[192,1024]{1,0:T(8,128)(2,1)S(1)} %collective-permute-done.3.refs_1_, bf16[192,1024]{1,0:T(8,128)(2,1)S(1)} %collective-permute-done.4.refs_2_, ...), custom_call_target="tpu_custom_call" | custom-call | tf_op jit(solution)/shard_map/expert_math/pallas_call | solution.py:295
  87.9 0.4 collective-permute-start.26
  88.3 0.1 add_convert_fusion.1
  88.5 11.5 %collective-permute-done.21.refs_0_ = bf16[48,4096]{1,0:T(8,128)(2,1)S(1)} collective-permute-done((bf16[48,4096]{1,0:T(8,128)(2,1)S(1)}, bf16[48,4096]{1,0:T(8,128)(2,1)S(1)}, u32[]{:S(2)}, u32[]{:S(2)}) %collective-permute-start.21) | collective-permute-done | bytes 393248 | tf_op jit(solution)/shard_map/ppermute | solution.py:246
  100.1 0.6 collective-permute-start.28
  100.6 0.1 add_convert_fusion
  100.7 0.1 collective-permute-start.27
  100.8 2.1 %collective-permute-done.23.refs_1_ = bf16[48,4096]{1,0:T(8,128)(2,1)S(1)} collective-permute-done((bf16[48,4096]{1,0:T(8,128)(2,1)S(1)}, bf16[48,4096]{1,0:T(8,128)(2,1)S(1)}, u32[]{:S(2)}, u32[]{:S(2)}) %collective-permute-start.23) | collective-permute-done | bytes 393248 | tf_op jit(solution)/shard_map/ppermute | solution.py:246
  102.9 0.9 collective-permute-start.29
  103.8 16.2 %collective-permute-done.27.refs_2_ = bf16[48,4096]{1,0:T(8,128)(2,1)S(1)} collective-permute-done((bf16[48,4096]{1,0:T(8,128)(2,1)S(1)}, bf16[48,4096]{1,0:T(8,128)(2,1)S(1)}, u32[]{:S(2)}, u32[]{:S(2)}) %collective-permute-start.27) | collective-permute-done | bytes 393248 | tf_op jit(solution)/shard_map/ppermute | solution.py:246
  120.0 0.8 collective-permute-start.30
  120.8 1.3 %collective-permute-done.30.refs_5_ = bf16[48,4096]{1,0:T(8,128)(2,1)S(1)} collective-permute-done((bf16[48,4096]{1,0:T(8,128)(2,1)S(1)}, bf16[48,4096]{1,0:T(8,128)(2,1)S(1)}, u32[]{:S(2)}, u32[]{:S(2)}) %collective-permute-start.30) | collective-permute-done | bytes 393248 | tf_op jit(solution)/shard_map/ppermute | solution.py:252
  122.1 1.7 %merge_rows.1 = (bf16[128,4096]{1,0:T(8,128)(2,1)}, bf16[128,4096]{1,0:T(8,128)(2,1)}) custom-call(bf16[48,4096]{1,0:T(8,128)(2,1)S(1)} %collective-permute-done.21.refs_0_, bf16[48,4096]{1,0:T(8,128)(2,1)S(1)} %collective-permute-done.23.refs_1_, bf16[48,4096]{1,0:T(8,128)(2,1)S(1)} %collective-permute-done.27.refs_2_, ...), custom_call_target="tpu_custom_call" | custom-call | tf_op jit(solution)/shard_map/merge_rows/pallas_call | solution.py:331
  (36 shorter events, 0.3 us)
Async XLA Ops:
  0.6 9.2 %copy-start.1 = (bf16[128,4096]{1,0:T(8,128)(2,1)S(1)}, bf16[128,4096]{1,0:T(8,128)(2,1)}, u32[]{:S(2)}) copy-start(bf16[128,4096]{1,0:T(8,128)(2,1)} %tokens_ref.1) | copy-start | bytes 3145732
  3.6 18.9 %collective-permute-start = (bf16[192,1024]{1,0:T(8,128)(2,1)}, bf16[192,1024]{1,0:T(8,128)(2,1)S(1)}, u32[]{:S(2)}, u32[]{:S(2)}) collective-permute-start(bf16[192,1024]{1,0:T(8,128)(2,1)} %get-tuple-element.31), channel_id=1, source_target_pairs={{0,6},{2,4},{4,2},{6,0},{1,7},{3,5},{5,3},{7,1},{8,14},{10,12},{12... | collective-permute-start | bytes 1179656 | tf_op jit(solution)/shard_map/ppermute | solution.py:246
  5.0 17.5 %collective-permute-start.1 = (bf16[192,1024]{1,0:T(8,128)(2,1)}, bf16[192,1024]{1,0:T(8,128)(2,1)S(1)}, u32[]{:S(2)}, u32[]{:S(2)}) collective-permute-start(bf16[192,1024]{1,0:T(8,128)(2,1)} %get-tuple-element.32.refs_9_), channel_id=1, source_target_pairs={{0,8},{8,0},{16,24},{24,16},{1,9},{9,1},{17,25},{25,17},{2,10},{10... | collective-permute-start | bytes 1179656 | tf_op jit(solution)/shard_map/ppermute | solution.py:249
  6.2 16.3 %collective-permute-start.2 = (bf16[192,1024]{1,0:T(8,128)(2,1)}, bf16[192,1024]{1,0:T(8,128)(2,1)S(1)}, u32[]{:S(2)}, u32[]{:S(2)}) collective-permute-start(bf16[192,1024]{1,0:T(8,128)(2,1)} %get-tuple-element.32.refs_9_), channel_id=1, source_target_pairs={{0,16},{8,24},{16,0},{24,8},{1,17},{9,25},{17,1},{25,9},{2,18},{10... | collective-permute-start | bytes 1179656 | tf_op jit(solution)/shard_map/ppermute | solution.py:249
  7.4 17.5 %collective-permute-start.8 = (bf16[192,1024]{1,0:T(8,128)(2,1)}, bf16[192,1024]{1,0:T(8,128)(2,1)S(1)}, u32[]{:S(2)}, u32[]{:S(2)}) collective-permute-start(bf16[192,1024]{1,0:T(8,128)(2,1)} %get-tuple-element.32.refs_9_), channel_id=1, source_target_pairs={{0,24},{8,16},{16,8},{24,0},{1,25},{9,17},{17,9},{25,1},{2,26},{10... | collective-permute-start | bytes 1179656 | tf_op jit(solution)/shard_map/ppermute | solution.py:249
  7.6 2.2 %copy-start.3 = (s32[128,1]{0,1:T(1,128)S(1)}, s32[128,1]{0,1:T(1,128)}, u32[]{:S(2)}) copy-start(s32[128,1]{0,1:T(1,128)} %param.9) | copy-start | bytes 1540
  7.6 17.3 %collective-permute-start.7 = (bf16[192,1024]{1,0:T(8,128)(2,1)}, bf16[192,1024]{1,0:T(8,128)(2,1)S(1)}, u32[]{:S(2)}, u32[]{:S(2)}) collective-permute-start(bf16[192,1024]{1,0:T(8,128)(2,1)} %get-tuple-element.37), channel_id=1, source_target_pairs={{0,2},{2,0},{4,6},{6,4},{1,3},{3,1},{5,7},{7,5},{8,10},{10,8},{12,... | collective-permute-start | bytes 1179656 | tf_op jit(solution)/shard_map/ppermute | solution.py:246
  9.8 1.2 copy-start.2
  11.0 12.7 %copy-start.4 = (bf16[192,1024]{1,0:T(8,128)(2,1)S(1)}, bf16[192,1024]{1,0:T(8,128)(2,1)}, u32[]{:S(2)}) copy-start(bf16[192,1024]{1,0:T(8,128)(2,1)} %get-tuple-element.36) | copy-start | bytes 1179652
  22.5 7.3 %collective-permute-start.3 = (bf16[192,1024]{1,0:T(8,128)(2,1)S(1)}, bf16[192,1024]{1,0:T(8,128)(2,1)S(1)}, u32[]{:S(2)}, u32[]{:S(2)}) collective-permute-start(bf16[192,1024]{1,0:T(8,128)(2,1)S(1)} %collective-permute-done.refs_0_), channel_id=1, source_target_pairs={{0,8},{8,0},{16,24},{24,16},{1,9},{9,1},{17,25},{25,17},{2,10},{10... | collective-permute-start | bytes 1179656 | tf_op jit(solution)/shard_map/ppermute | solution.py:249
  23.7 15.3 %collective-permute-start.6 = (bf16[192,1024]{1,0:T(8,128)(2,1)S(1)}, bf16[192,1024]{1,0:T(8,128)(2,1)S(1)}, u32[]{:S(2)}, u32[]{:S(2)}) collective-permute-start(bf16[192,1024]{1,0:T(8,128)(2,1)S(1)} %copy-done.4), channel_id=1, source_target_pairs={{0,4},{2,6},{4,0},{6,2},{1,5},{3,7},{5,1},{7,3},{8,12},{10,14},{12... | collective-permute-start | bytes 1179656 | tf_op jit(solution)/shard_map/ppermute | solution.py:246
  23.7 18.4 %collective-permute-start.4 = (bf16[192,1024]{1,0:T(8,128)(2,1)S(1)}, bf16[192,1024]{1,0:T(8,128)(2,1)S(1)}, u32[]{:S(2)}, u32[]{:S(2)}) collective-permute-start(bf16[192,1024]{1,0:T(8,128)(2,1)S(1)} %collective-permute-done.refs_0_), channel_id=1, source_target_pairs={{0,16},{8,24},{16,0},{24,8},{1,17},{9,25},{17,1},{25,9},{2,18},{10... | collective-permute-start | bytes 1179656 | tf_op jit(solution)/shard_map/ppermute | solution.py:249
  25.0 17.8 %collective-permute-start.9 = (bf16[192,1024]{1,0:T(8,128)(2,1)S(1)}, bf16[192,1024]{1,0:T(8,128)(2,1)S(1)}, u32[]{:S(2)}, u32[]{:S(2)}) collective-permute-start(bf16[192,1024]{1,0:T(8,128)(2,1)S(1)} %collective-permute-done.7.refs_13_), channel_id=1, source_target_pairs={{0,8},{8,0},{16,24},{24,16},{1,9},{9,1},{17,25},{25,17},{2,10},{10... | collective-permute-start | bytes 1179656 | tf_op jit(solution)/shard_map/ppermute | solution.py:249
  25.7 17.0 %collective-permute-start.10 = (bf16[192,1024]{1,0:T(8,128)(2,1)S(1)}, bf16[192,1024]{1,0:T(8,128)(2,1)S(1)}, u32[]{:S(2)}, u32[]{:S(2)}) collective-permute-start(bf16[192,1024]{1,0:T(8,128)(2,1)S(1)} %collective-permute-done.7.refs_13_), channel_id=1, source_target_pairs={{0,16},{8,24},{16,0},{24,8},{1,17},{9,25},{17,1},{25,9},{2,18},{10... | collective-permute-start | bytes 1179656 | tf_op jit(solution)/shard_map/ppermute | solution.py:249
  29.8 17.9 %collective-permute-start.5 = (bf16[192,1024]{1,0:T(8,128)(2,1)S(1)}, bf16[192,1024]{1,0:T(8,128)(2,1)S(1)}, u32[]{:S(2)}, u32[]{:S(2)}) collective-permute-start(bf16[192,1024]{1,0:T(8,128)(2,1)S(1)} %collective-permute-done.3.refs_1_), channel_id=1, source_target_pairs={{0,16},{8,24},{16,0},{24,8},{1,17},{9,25},{17,1},{25,9},{2,18},{10... | collective-permute-start | bytes 1179656 | tf_op jit(solution)/shard_map/ppermute | solution.py:249
  39.0 20.2 %collective-permute-start.16 = (bf16[48,4096]{1,0:T(8,128)(2,1)S(1)}, bf16[48,4096]{1,0:T(8,128)(2,1)S(1)}, u32[]{:S(2)}, u32[]{:S(2)}) collective-permute-start(bf16[48,4096]{1,0:T(8,128)(2,1)S(1)} %get-tuple-element.43), channel_id=1, source_target_pairs={{0,4},{2,6},{4,0},{6,2},{1,5},{3,7},{5,1},{7,3},{8,12},{10,14},{12... | collective-permute-start | bytes 1179656 | tf_op jit(solution)/shard_map/ppermute | solution.py:246
  42.1 25.3 %copy-start = (bf16[192,1024]{1,0:T(8,128)(2,1)S(1)}, bf16[192,1024]{1,0:T(8,128)(2,1)}, u32[]{:S(2)}) copy-start(bf16[192,1024]{1,0:T(8,128)(2,1)} %get-tuple-element.32.refs_9_) | copy-start | bytes 1179652
  42.1 17.8 %collective-permute-start.17 = (bf16[48,4096]{1,0:T(8,128)(2,1)S(1)}, bf16[48,4096]{1,0:T(8,128)(2,1)S(1)}, u32[]{:S(2)}, u32[]{:S(2)}) collective-permute-start(bf16[48,4096]{1,0:T(8,128)(2,1)S(1)} %get-tuple-element.45), channel_id=1, source_target_pairs={{0,2},{2,0},{4,6},{6,4},{1,3},{3,1},{5,7},{7,5},{8,10},{10,8},{12,... | collective-permute-start | bytes 1179656 | tf_op jit(solution)/shard_map/ppermute | solution.py:246
  42.7 18.5 %collective-permute-start.11 = (bf16[192,1024]{1,0:T(8,128)(2,1)S(1)}, bf16[192,1024]{1,0:T(8,128)(2,1)S(1)}, u32[]{:S(2)}, u32[]{:S(2)}) collective-permute-start(bf16[192,1024]{1,0:T(8,128)(2,1)S(1)} %collective-permute-done.6.refs_4_), channel_id=1, source_target_pairs={{0,8},{8,0},{16,24},{24,16},{1,9},{9,1},{17,25},{25,17},{2,10},{10... | collective-permute-start | bytes 1179656 | tf_op jit(solution)/shard_map/ppermute | solution.py:249
  43.0 18.2 %collective-permute-start.12 = (bf16[192,1024]{1,0:T(8,128)(2,1)S(1)}, bf16[192,1024]{1,0:T(8,128)(2,1)S(1)}, u32[]{:S(2)}, u32[]{:S(2)}) collective-permute-start(bf16[192,1024]{1,0:T(8,128)(2,1)S(1)} %collective-permute-done.6.refs_4_), channel_id=1, source_target_pairs={{0,16},{8,24},{16,0},{24,8},{1,17},{9,25},{17,1},{25,9},{2,18},{10... | collective-permute-start | bytes 1179656 | tf_op jit(solution)/shard_map/ppermute | solution.py:249
  47.7 13.5 %collective-permute-start.13 = (bf16[192,1024]{1,0:T(8,128)(2,1)S(1)}, bf16[192,1024]{1,0:T(8,128)(2,1)S(1)}, u32[]{:S(2)}, u32[]{:S(2)}) collective-permute-start(bf16[192,1024]{1,0:T(8,128)(2,1)S(1)} %collective-permute-done.10.refs_15_), channel_id=1, source_target_pairs={{0,8},{8,0},{16,24},{24,16},{1,9},{9,1},{17,25},{25,17},{2,10},{10... | collective-permute-start | bytes 1179656 | tf_op jit(solution)/shard_map/ppermute | solution.py:249
  59.2 8.3 %collective-permute-start.18 = (bf16[48,4096]{1,0:T(8,128)(2,1)S(1)}, bf16[48,4096]{1,0:T(8,128)(2,1)S(1)}, u32[]{:S(2)}, u32[]{:S(2)}) collective-permute-start(bf16[48,4096]{1,0:T(8,128)(2,1)S(1)} %collective-permute-done.16.refs_17_), channel_id=1, source_target_pairs={{0,1},{1,0},{2,3},{3,2},{4,5},{5,4},{6,7},{7,6},{8,9},{9,8},{10,11... | collective-permute-start | bytes 1179656 | tf_op jit(solution)/shard_map/ppermute | solution.py:252
  59.9 7.5 %collective-permute-start.19 = (bf16[48,4096]{1,0:T(8,128)(2,1)S(1)}, bf16[48,4096]{1,0:T(8,128)(2,1)S(1)}, u32[]{:S(2)}, u32[]{:S(2)}) collective-permute-start(bf16[48,4096]{1,0:T(8,128)(2,1)S(1)} %collective-permute-done.17.refs_18_), channel_id=1, source_target_pairs={{0,1},{1,0},{2,3},{3,2},{4,5},{5,4},{6,7},{7,6},{8,9},{9,8},{10,11... | collective-permute-start | bytes 1179656 | tf_op jit(solution)/shard_map/ppermute | solution.py:252
  61.2 4.6 %collective-permute-start.14 = (bf16[96,1024]{1,0:T(8,128)(2,1)S(1)}, bf16[96,1024]{1,0:T(8,128)(2,1)S(1)}, u32[]{:S(2)}, u32[]{:S(2)}) collective-permute-start(bf16[96,1024]{1,0:T(8,128)(2,1)S(1)} %slice.6), channel_id=1, source_target_pairs={{0,16},{8,24},{16,0},{24,8},{1,17},{9,25},{17,1},{25,9},{2,18},{10... | collective-permute-start | bytes 589832 | tf_op jit(solution)/shard_map/ppermute | solution.py:249
  62.6 4.9 %collective-permute-start.15 = (bf16[96,1024]{1,0:T(8,128)(2,1)S(1)}, bf16[96,1024]{1,0:T(8,128)(2,1)S(1)}, u32[]{:S(2)}, u32[]{:S(2)}) collective-permute-start(bf16[96,1024]{1,0:T(8,128)(2,1)S(1)} %slice.7), channel_id=1, source_target_pairs={{0,8},{8,0},{16,24},{24,16},{1,9},{9,1},{17,25},{25,17},{2,10},{10... | collective-permute-start | bytes 589832 | tf_op jit(solution)/shard_map/ppermute | solution.py:249
  62.6 17.4 %collective-permute-start.24 = (bf16[48,4096]{1,0:T(8,128)(2,1)S(1)}, bf16[48,4096]{1,0:T(8,128)(2,1)S(1)}, u32[]{:S(2)}, u32[]{:S(2)}) collective-permute-start(bf16[48,4096]{1,0:T(8,128)(2,1)S(1)} %get-tuple-element.51), channel_id=1, source_target_pairs={{0,6},{2,4},{4,2},{6,0},{1,7},{3,5},{5,3},{7,1},{8,14},{10,12},{12... | collective-permute-start | bytes 1179656 | tf_op jit(solution)/shard_map/ppermute | solution.py:246
  71.4 11.3 %collective-permute-start.20 = (bf16[48,4096]{1,0:T(8,128)(2,1)S(1)}, bf16[48,4096]{1,0:T(8,128)(2,1)S(1)}, u32[]{:S(2)}, u32[]{:S(2)}) collective-permute-start(bf16[48,4096]{1,0:T(8,128)(2,1)S(1)} %get-tuple-element.47), channel_id=1, source_target_pairs={{0,1},{1,0},{2,3},{3,2},{4,5},{5,4},{6,7},{7,6},{8,9},{9,8},{10,11... | collective-permute-start | bytes 1179656 | tf_op jit(solution)/shard_map/ppermute | solution.py:252
  75.4 12.9 %collective-permute-start.22 = (bf16[48,4096]{1,0:T(8,128)(2,1)S(1)}, bf16[48,4096]{1,0:T(8,128)(2,1)S(1)}, u32[]{:S(2)}, u32[]{:S(2)}) collective-permute-start(bf16[48,4096]{1,0:T(8,128)(2,1)S(1)} %get-tuple-element.49), channel_id=1, source_target_pairs={{0,1},{1,0},{2,3},{3,2},{4,5},{5,4},{6,7},{7,6},{8,9},{9,8},{10,11... | collective-permute-start | bytes 1179656 | tf_op jit(solution)/shard_map/ppermute | solution.py:252
  80.0 4.0 %collective-permute-start.25 = (bf16[48,4096]{1,0:T(8,128)(2,1)S(1)}, bf16[48,4096]{1,0:T(8,128)(2,1)S(1)}, u32[]{:S(2)}, u32[]{:S(2)}) collective-permute-start(bf16[48,4096]{1,0:T(8,128)(2,1)S(1)} %collective-permute-done.24.refs_17_), channel_id=1, source_target_pairs={{0,1},{1,0},{2,3},{3,2},{4,5},{5,4},{6,7},{7,6},{8,9},{9,8},{10,11... | collective-permute-start | bytes 1179656 | tf_op jit(solution)/shard_map/ppermute | solution.py:252
  82.8 17.3 %collective-permute-start.21 = (bf16[48,4096]{1,0:T(8,128)(2,1)S(1)}, bf16[48,4096]{1,0:T(8,128)(2,1)S(1)}, u32[]{:S(2)}, u32[]{:S(2)}) collective-permute-start(bf16[48,4096]{1,0:T(8,128)(2,1)S(1)} %add_convert_fusion.2), channel_id=1, source_target_pairs={{0,4},{2,6},{4,0},{6,2},{1,5},{3,7},{5,1},{7,3},{8,12},{10,14},{12... | collective-permute-start | bytes 1179656 | tf_op jit(solution)/shard_map/ppermute | solution.py:246
  87.9 12.7 %collective-permute-start.26 = (bf16[48,4096]{1,0:T(8,128)(2,1)S(1)}, bf16[48,4096]{1,0:T(8,128)(2,1)S(1)}, u32[]{:S(2)}, u32[]{:S(2)}) collective-permute-start(bf16[48,4096]{1,0:T(8,128)(2,1)S(1)} %get-tuple-element.55), channel_id=1, source_target_pairs={{0,1},{1,0},{2,3},{3,2},{4,5},{5,4},{6,7},{7,6},{8,9},{9,8},{10,11... | collective-permute-start | bytes 1179656 | tf_op jit(solution)/shard_map/ppermute | solution.py:252
  88.4 14.4 %collective-permute-start.23 = (bf16[48,4096]{1,0:T(8,128)(2,1)S(1)}, bf16[48,4096]{1,0:T(8,128)(2,1)S(1)}, u32[]{:S(2)}, u32[]{:S(2)}) collective-permute-start(bf16[48,4096]{1,0:T(8,128)(2,1)S(1)} %add_convert_fusion.1), channel_id=1, source_target_pairs={{0,2},{2,0},{4,6},{6,4},{1,3},{3,1},{5,7},{7,5},{8,10},{10,8},{12,... | collective-permute-start | bytes 1179656 | tf_op jit(solution)/shard_map/ppermute | solution.py:246
  100.1 2.8 %collective-permute-start.28 = (bf16[48,4096]{1,0:T(8,128)(2,1)S(1)}, bf16[48,4096]{1,0:T(8,128)(2,1)S(1)}, u32[]{:S(2)}, u32[]{:S(2)}) collective-permute-start(bf16[48,4096]{1,0:T(8,128)(2,1)S(1)} %collective-permute-done.21.refs_0_), channel_id=1, source_target_pairs={{0,1},{1,0},{2,3},{3,2},{4,5},{5,4},{6,7},{7,6},{8,9},{9,8},{10,11... | collective-permute-start | bytes 1179656 | tf_op jit(solution)/shard_map/ppermute | solution.py:252
  100.7 19.2 %collective-permute-start.27 = (bf16[48,4096]{1,0:T(8,128)(2,1)S(1)}, bf16[48,4096]{1,0:T(8,128)(2,1)S(1)}, u32[]{:S(2)}, u32[]{:S(2)}) collective-permute-start(bf16[48,4096]{1,0:T(8,128)(2,1)S(1)} %add_convert_fusion), channel_id=1, source_target_pairs={{0,6},{2,4},{4,2},{6,0},{1,7},{3,5},{5,3},{7,1},{8,14},{10,12},{12... | collective-permute-start | bytes 1179656 | tf_op jit(solution)/shard_map/ppermute | solution.py:246
  102.9 17.1 %collective-permute-start.29 = (bf16[48,4096]{1,0:T(8,128)(2,1)S(1)}, bf16[48,4096]{1,0:T(8,128)(2,1)S(1)}, u32[]{:S(2)}, u32[]{:S(2)}) collective-permute-start(bf16[48,4096]{1,0:T(8,128)(2,1)S(1)} %collective-permute-done.23.refs_1_), channel_id=1, source_target_pairs={{0,1},{1,0},{2,3},{3,2},{4,5},{5,4},{6,7},{7,6},{8,9},{9,8},{10,11... | collective-permute-start | bytes 1179656 | tf_op jit(solution)/shard_map/ppermute | solution.py:252
  103.8 16.9 %collective-permute-start.31 = (bf16[96,4096]{1,0:T(8,128)(2,1)S(1)}, bf16[96,4096]{1,0:T(8,128)(2,1)S(1)}, u32[]{:S(2)}, u32[]{:S(2)}) collective-permute-start(bf16[96,4096]{1,0:T(8,128)(2,1)S(1)} %get-tuple-element.58.refs_6_), channel_id=1, source_target_pairs={{0,1},{1,0},{2,3},{3,2},{4,5},{5,4},{6,7},{7,6},{8,9},{9,8},{10,11... | collective-permute-start | bytes 2359304 | tf_op jit(solution)/shard_map/ppermute | solution.py:252
  120.0 2.1 %collective-permute-start.30 = (bf16[48,4096]{1,0:T(8,128)(2,1)S(1)}, bf16[48,4096]{1,0:T(8,128)(2,1)S(1)}, u32[]{:S(2)}, u32[]{:S(2)}) collective-permute-start(bf16[48,4096]{1,0:T(8,128)(2,1)S(1)} %collective-permute-done.27.refs_2_), channel_id=1, source_target_pairs={{0,1},{1,0},{2,3},{3,2},{4,5},{5,4},{6,7},{7,6},{8,9},{9,8},{10,11... | collective-permute-start | bytes 1179656 | tf_op jit(solution)/shard_map/ppermute | solution.py:252

commit v6 on v5

--- a/solution.py
+++ b/solution.py
@@ -222,7 +222,7 @@
     )(cluster, w_gate, w_up, w_down)
 
     route_row = routes.reshape(1, tok_count)
-    block = width // 4
+    block = width // 2
     *sent, local, home_table = pl.pallas_call(
         functools.partial(dispatch_kernel, n_experts, capacity),
         grid=(width // block,),
@@ -270,7 +270,7 @@
     pieces1 = near_far(chunk1)
     (chunk3,) = after([chunk3], [*pieces0[1:3], local])
     pieces3 = near_far(chunk3)
-    (held,) = after([chunk2], pieces3[1:] + pieces1[1:])
+    (held,) = after([chunk2], pieces3[2:3] + pieces1[1:2])
     pieces2 = near_far(held)
     for k, awaited in ((2, chunk2), (1, chunk2), (3, None)):
         (row,) = after([sent[k]], [rows[2] if awaited is None else awaited])
@@ -326,7 +326,7 @@
         awaited = [other[k]]
 
     order = (2, 1, 3)
-    blocks = 8
+    blocks = 4
     return tuple(
         pl.pallas_call(
             functools.partial(merge_kernel, order, capacity, blocks),

time: 124 us -> 124 us (level)
  transfers between devices with their start and end apart: 32 -> 32, of which waited for: 13 -> 13; matrix products, arithmetic and copies ran while one was open for 0% -> 0% of each run, Pallas kernels for 8% -> 7%
where the time goes in v6:
time: 124 us
  waiting for transfers between devices  78.1 us (63%)
  starting transfers between devices  29.6 us (24%)
  Pallas kernels  13.8 us (11%)
  local copies, waits for them, and re-layouts  1.27 us (1%)
    ppermute x9, waiting for transfers between devices, planes(): return lax.ppermute(chunk, 'expert', flips(n_experts, k))  64.3 us
    ppermute x10, starting transfers between devices, swapped(): return lax.ppermute(chunk, 'tensor', swap)  11.5 us
    ppermute x13, waiting for transfers between devices, spread(): return lax.ppermute(chunk, 'dp', flips(n_dp, step))  11.2 us
    ppermute x13, starting transfers between devices, spread(): return lax.ppermute(chunk, 'dp', flips(n_dp, step))  10.5 us
    pallas_call x2, Pallas kernels, aligned_plan(): pl.pallas_call(functools.partial(expert_kernel, [len(pieces) for pieces i...  7.77 us
    ppermute x9, starting transfers between devices, planes(): return lax.ppermute(chunk, 'expert', flips(n_experts, k))  7.54 us
    pallas_call x1, Pallas kernels, aligned_plan(): pl.pallas_call(functools.partial(select_kernel, n_experts, halves, shards...  2.96 us
    ppermute x10, waiting for transfers between devices, swapped(): return lax.ppermute(chunk, 'tensor', swap)  2.54 us
  transfers between devices with their start and end apart: 32, of which 13 were waited for; matrix products, arithmetic and copies ran while one was open for 0% of the time, Pallas kernels for 7%

profile of v6, /device:TPU:9, one launch (start us, length us, event | category | flops | bytes accessed | tf_op | source)
XLA Modules:
  0.0 123.8 jit_solution(16419287615897059136)
XLA Ops:
  0.6 3.0 %select_rows.1 = (bf16[192,1024]{1,0:T(8,128)(2,1)}, bf16[192,1024]{1,0:T(8,128)(2,1)}, bf16[192,1024]{1,0:T(8,128)(2,1)}, bf16[192,1024]{1,0:T(8,128)(2,1)}) custom-call(s32[4,512]{1,0:T(4,128)} %cluster_hbm.1, bf16[231,1024]{1,0:T(8,128)(2,1)} %gate_hbm.1, bf16[231,1024]{1,0:T(8,128)(2,1)} %up_hbm.1, bf16[231,1024]{1,0:T(8,128)(2,1)} %down_hbm.1), custom_call_target="tpu_custom_call" | custom-call | tf_op jit(solution)/shard_map/select_rows/pallas_call | solution.py:208
  3.6 1.4 %collective-permute-start = (bf16[192,1024]{1,0:T(8,128)(2,1)}, bf16[192,1024]{1,0:T(8,128)(2,1)S(1)}, u32[]{:S(2)}, u32[]{:S(2)}) collective-permute-start(bf16[192,1024]{1,0:T(8,128)(2,1)} %get-tuple-element.31), channel_id=1, source_target_pairs={{0,6},{2,4},{4,2},{6,0},{1,7},{3,5},{5,3},{7,1},{8,14},{10,12},{12... | collective-permute-start | bytes 1179656 | tf_op jit(solution)/shard_map/ppermute | solution.py:246
  5.0 1.2 collective-permute-start.1
  6.2 1.2 %collective-permute-start.2 = (bf16[192,1024]{1,0:T(8,128)(2,1)}, bf16[192,1024]{1,0:T(8,128)(2,1)S(1)}, u32[]{:S(2)}, u32[]{:S(2)}) collective-permute-start(bf16[192,1024]{1,0:T(8,128)(2,1)} %get-tuple-element.32.refs_9_), channel_id=1, source_target_pairs={{0,16},{8,24},{16,0},{24,8},{1,17},{9,25},{17,1},{25,9},{2,18},{10... | collective-permute-start | bytes 1179656 | tf_op jit(solution)/shard_map/ppermute | solution.py:249
  7.4 0.2 collective-permute-start.8
  7.6 2.2 %collective-permute-start.7 = (bf16[192,1024]{1,0:T(8,128)(2,1)}, bf16[192,1024]{1,0:T(8,128)(2,1)S(1)}, u32[]{:S(2)}, u32[]{:S(2)}) collective-permute-start(bf16[192,1024]{1,0:T(8,128)(2,1)} %get-tuple-element.37), channel_id=1, source_target_pairs={{0,2},{2,0},{4,6},{6,4},{1,3},{3,1},{5,7},{7,5},{8,10},{10,8},{12,... | collective-permute-start | bytes 1179656 | tf_op jit(solution)/shard_map/ppermute | solution.py:246
  9.8 1.2 copy-done.2
  11.0 1.4 %dispatch_rows.1 = (bf16[48,4096]{1,0:T(8,128)(2,1)S(1)}, bf16[48,4096]{1,0:T(8,128)(2,1)S(1)}, bf16[48,4096]{1,0:T(8,128)(2,1)S(1)}, bf16[48,4096]{1,0:T(8,128)...) custom-call(s32[1,128]{1,0:T(1,128)S(1)} %bitcast.1, bf16[128,4096]{1,0:T(8,128)(2,1)S(1)} %copy-done.1, ...), custom_call_target="tpu_custom_call" | custom-call | tf_op jit(solution)/shard_map/dispatch_rows/pallas_call | solution.py:226
  12.5 10.0 %collective-permute-done.refs_0_ = bf16[192,1024]{1,0:T(8,128)(2,1)S(1)} collective-permute-done((bf16[192,1024]{1,0:T(8,128)(2,1)}, bf16[192,1024]{1,0:T(8,128)(2,1)S(1)}, u32[]{:S(2)}, u32[]{:S(2)}) %collective-permute-start) | collective-permute-done | bytes 393248 | tf_op jit(solution)/shard_map/ppermute | solution.py:246
  22.5 1.2 collective-permute-start.3
  23.7 1.2 %collective-permute-start.4 = (bf16[192,1024]{1,0:T(8,128)(2,1)S(1)}, bf16[192,1024]{1,0:T(8,128)(2,1)S(1)}, u32[]{:S(2)}, u32[]{:S(2)}) collective-permute-start(bf16[192,1024]{1,0:T(8,128)(2,1)S(1)} %collective-permute-done.refs_0_), channel_id=1, source_target_pairs={{0,16},{8,24},{16,0},{24,8},{1,17},{9,25},{17,1},{25,9},{2,18},{10... | collective-permute-start | bytes 1179656 | tf_op jit(solution)/shard_map/ppermute | solution.py:249
  25.0 0.7 collective-permute-start.9
  25.7 1.2 collective-permute-start.12
  26.9 2.9 %collective-permute-done.3.refs_1_ = bf16[192,1024]{1,0:T(8,128)(2,1)S(1)} collective-permute-done((bf16[192,1024]{1,0:T(8,128)(2,1)S(1)}, bf16[192,1024]{1,0:T(8,128)(2,1)S(1)}, u32[]{:S(2)}, u32[]{:S(2)}) %collective-permute-start.3) | collective-permute-done | bytes 393248 | tf_op jit(solution)/shard_map/ppermute | solution.py:249
  29.8 0.7 collective-permute-start.5
  30.5 8.5 %collective-permute-done.6.refs_4_ = bf16[192,1024]{1,0:T(8,128)(2,1)S(1)} collective-permute-done((bf16[192,1024]{1,0:T(8,128)(2,1)S(1)}, bf16[192,1024]{1,0:T(8,128)(2,1)S(1)}, u32[]{:S(2)}, u32[]{:S(2)}) %collective-permute-start.6) | collective-permute-done | bytes 393248 | tf_op jit(solution)/shard_map/ppermute | solution.py:246
  39.0 3.1 %collective-permute-start.16 = (bf16[48,4096]{1,0:T(8,128)(2,1)S(1)}, bf16[48,4096]{1,0:T(8,128)(2,1)S(1)}, u32[]{:S(2)}, u32[]{:S(2)}) collective-permute-start(bf16[48,4096]{1,0:T(8,128)(2,1)S(1)} %get-tuple-element.43), channel_id=1, source_target_pairs={{0,4},{2,6},{4,0},{6,2},{1,5},{3,7},{5,1},{7,3},{8,12},{10,14},{12... | collective-permute-start | bytes 1179656 | tf_op jit(solution)/shard_map/ppermute | solution.py:246
  42.1 0.6 collective-permute-start.17
  42.7 0.2 collective-permute-start.10
  43.0 1.1 collective-permute-start.11
  44.1 3.6 %collective-permute-done.5.refs_3_ = bf16[192,1024]{1,0:T(8,128)(2,1)S(1)} collective-permute-done((bf16[192,1024]{1,0:T(8,128)(2,1)S(1)}, bf16[192,1024]{1,0:T(8,128)(2,1)S(1)}, u32[]{:S(2)}, u32[]{:S(2)}) %collective-permute-start.5) | collective-permute-done | bytes 393248 | tf_op jit(solution)/shard_map/ppermute | solution.py:249
  47.7 11.5 %collective-permute-done.16.refs_17_ = bf16[48,4096]{1,0:T(8,128)(2,1)S(1)} collective-permute-done((bf16[48,4096]{1,0:T(8,128)(2,1)S(1)}, bf16[48,4096]{1,0:T(8,128)(2,1)S(1)}, u32[]{:S(2)}, u32[]{:S(2)}) %collective-permute-start.16) | collective-permute-done | bytes 393248 | tf_op jit(solution)/shard_map/ppermute | solution.py:246
  59.2 0.7 collective-permute-start.18
  59.9 1.3 %collective-permute-start.19 = (bf16[48,4096]{1,0:T(8,128)(2,1)S(1)}, bf16[48,4096]{1,0:T(8,128)(2,1)S(1)}, u32[]{:S(2)}, u32[]{:S(2)}) collective-permute-start(bf16[48,4096]{1,0:T(8,128)(2,1)S(1)} %collective-permute-done.17.refs_18_), channel_id=1, source_target_pairs={{0,1},{1,0},{2,3},{3,2},{4,5},{5,4},{6,7},{7,6},{8,9},{9,8},{10,11... | collective-permute-start | bytes 1179656 | tf_op jit(solution)/shard_map/ppermute | solution.py:252
  61.2 1.3 %collective-permute-start.14 = (bf16[96,1024]{1,0:T(8,128)(2,1)S(1)}, bf16[96,1024]{1,0:T(8,128)(2,1)S(1)}, u32[]{:S(2)}, u32[]{:S(2)}) collective-permute-start(bf16[96,1024]{1,0:T(8,128)(2,1)S(1)} %slice.6), channel_id=1, source_target_pairs={{0,16},{8,24},{16,0},{24,8},{1,17},{9,25},{17,1},{25,9},{2,18},{10... | collective-permute-start | bytes 589832 | tf_op jit(solution)/shard_map/ppermute | solution.py:249
  62.6 0.1 collective-permute-start.15
  62.7 3.1 %collective-permute-done.14.refs_7_ = bf16[96,1024]{1,0:T(8,128)(2,1)S(1)} collective-permute-done((bf16[96,1024]{1,0:T(8,128)(2,1)S(1)}, bf16[96,1024]{1,0:T(8,128)(2,1)S(1)}, u32[]{:S(2)}, u32[]{:S(2)}) %collective-permute-start.14) | collective-permute-done | bytes 196640 | tf_op jit(solution)/shard_map/ppermute | solution.py:249
  65.8 1.6 %collective-permute-done.15.refs_8_ = bf16[96,1024]{1,0:T(8,128)(2,1)S(1)} collective-permute-done((bf16[96,1024]{1,0:T(8,128)(2,1)S(1)}, bf16[96,1024]{1,0:T(8,128)(2,1)S(1)}, u32[]{:S(2)}, u32[]{:S(2)}) %collective-permute-start.15) | collective-permute-done | bytes 196640 | tf_op jit(solution)/shard_map/ppermute | solution.py:249
  67.5 3.9 %expert_math.2 = (bf16[48,4096]{1,0:T(8,128)(2,1)S(1)}, bf16[48,4096]{1,0:T(8,128)(2,1)S(1)}, bf16[48,4096]{1,0:T(8,128)(2,1)S(1)}, bf16[48,4096]{1,0:T(8,128)(2,1)S(1)}) custom-call(bf16[192,1024]{1,0:T(8,128)(2,1)S(1)} %collective-permute-done.refs_0_, bf16[192,1024]{1,0:T(8,128)(2,1)S(1)} %collective-permute-done.3.refs_1_, ...), custom_call_target="tpu_custom_call" | custom-call | tf_op jit(solution)/shard_map/expert_math/pallas_call | solution.py:295
  71.4 4.1 %collective-permute-start.20 = (bf16[48,4096]{1,0:T(8,128)(2,1)S(1)}, bf16[48,4096]{1,0:T(8,128)(2,1)S(1)}, u32[]{:S(2)}, u32[]{:S(2)}) collective-permute-start(bf16[48,4096]{1,0:T(8,128)(2,1)S(1)} %get-tuple-element.47), channel_id=1, source_target_pairs={{0,1},{1,0},{2,3},{3,2},{4,5},{5,4},{6,7},{7,6},{8,9},{9,8},{10,11... | collective-permute-start | bytes 1179656 | tf_op jit(solution)/shard_map/ppermute | solution.py:252
  75.4 0.1 collective-permute-start.22
  75.5 4.5 %collective-permute-done.24.refs_17_ = bf16[48,4096]{1,0:T(8,128)(2,1)S(1)} collective-permute-done((bf16[48,4096]{1,0:T(8,128)(2,1)S(1)}, bf16[48,4096]{1,0:T(8,128)(2,1)S(1)}, u32[]{:S(2)}, u32[]{:S(2)}) %collective-permute-start.24) | collective-permute-done | bytes 393248 | tf_op jit(solution)/shard_map/ppermute | solution.py:246
  80.0 2.7 %collective-permute-start.25 = (bf16[48,4096]{1,0:T(8,128)(2,1)S(1)}, bf16[48,4096]{1,0:T(8,128)(2,1)S(1)}, u32[]{:S(2)}, u32[]{:S(2)}) collective-permute-start(bf16[48,4096]{1,0:T(8,128)(2,1)S(1)} %collective-permute-done.24.refs_17_), channel_id=1, source_target_pairs={{0,1},{1,0},{2,3},{3,2},{4,5},{5,4},{6,7},{7,6},{8,9},{9,8},{10,11... | collective-permute-start | bytes 1179656 | tf_op jit(solution)/shard_map/ppermute | solution.py:252
  82.7 0.1 add_convert_fusion.2
  82.8 1.2 collective-permute-done.25.refs_19_
  84.0 3.9 %expert_math.3 = (bf16[48,4096]{1,0:T(8,128)(2,1)S(1)}, bf16[48,4096]{1,0:T(8,128)(2,1)S(1)}, bf16[96,4096]{1,0:T(8,128)(2,1)S(1)}) custom-call(bf16[192,1024]{1,0:T(8,128)(2,1)S(1)} %collective-permute-done.refs_0_, bf16[192,1024]{1,0:T(8,128)(2,1)S(1)} %collective-permute-done.3.refs_1_, bf16[192,1024]{1,0:T(8,128)(2,1)S(1)} %collective-permute-done.4.refs_2_, ...), custom_call_target="tpu_custom_call" | custom-call | tf_op jit(solution)/shard_map/expert_math/pallas_call | solution.py:295
  87.9 0.4 collective-permute-start.26
  88.3 0.1 add_convert_fusion.1
  88.5 11.5 %collective-permute-done.21.refs_0_ = bf16[48,4096]{1,0:T(8,128)(2,1)S(1)} collective-permute-done((bf16[48,4096]{1,0:T(8,128)(2,1)S(1)}, bf16[48,4096]{1,0:T(8,128)(2,1)S(1)}, u32[]{:S(2)}, u32[]{:S(2)}) %collective-permute-start.21) | collective-permute-done | bytes 393248 | tf_op jit(solution)/shard_map/ppermute | solution.py:246
  100.1 0.6 collective-permute-start.28
  100.6 0.1 add_convert_fusion
  100.7 0.1 collective-permute-start.27
  100.8 2.1 %collective-permute-done.23.refs_1_ = bf16[48,4096]{1,0:T(8,128)(2,1)S(1)} collective-permute-done((bf16[48,4096]{1,0:T(8,128)(2,1)S(1)}, bf16[48,4096]{1,0:T(8,128)(2,1)S(1)}, u32[]{:S(2)}, u32[]{:S(2)}) %collective-permute-start.23) | collective-permute-done | bytes 393248 | tf_op jit(solution)/shard_map/ppermute | solution.py:246
  102.9 0.9 collective-permute-start.29
  103.8 16.2 %collective-permute-done.27.refs_2_ = bf16[48,4096]{1,0:T(8,128)(2,1)S(1)} collective-permute-done((bf16[48,4096]{1,0:T(8,128)(2,1)S(1)}, bf16[48,4096]{1,0:T(8,128)(2,1)S(1)}, u32[]{:S(2)}, u32[]{:S(2)}) %collective-permute-start.27) | collective-permute-done | bytes 393248 | tf_op jit(solution)/shard_map/ppermute | solution.py:246
  120.0 0.8 collective-permute-start.30
  120.8 1.3 %collective-permute-done.30.refs_5_ = bf16[48,4096]{1,0:T(8,128)(2,1)S(1)} collective-permute-done((bf16[48,4096]{1,0:T(8,128)(2,1)S(1)}, bf16[48,4096]{1,0:T(8,128)(2,1)S(1)}, u32[]{:S(2)}, u32[]{:S(2)}) %collective-permute-start.30) | collective-permute-done | bytes 393248 | tf_op jit(solution)/shard_map/ppermute | solution.py:252
  122.1 1.7 %merge_rows.1 = (bf16[128,4096]{1,0:T(8,128)(2,1)}, bf16[128,4096]{1,0:T(8,128)(2,1)}) custom-call(bf16[48,4096]{1,0:T(8,128)(2,1)S(1)} %collective-permute-done.21.refs_0_, bf16[48,4096]{1,0:T(8,128)(2,1)S(1)} %collective-permute-done.23.refs_1_, bf16[48,4096]{1,0:T(8,128)(2,1)S(1)} %collective-permute-done.27.refs_2_, ...), custom_call_target="tpu_custom_call" | custom-call | tf_op jit(solution)/shard_map/merge_rows/pallas_call | solution.py:331
  (36 shorter events, 0.3 us)
Async XLA Ops:
  0.6 9.2 %copy-start.1 = (bf16[128,4096]{1,0:T(8,128)(2,1)S(1)}, bf16[128,4096]{1,0:T(8,128)(2,1)}, u32[]{:S(2)}) copy-start(bf16[128,4096]{1,0:T(8,128)(2,1)} %tokens_ref.1) | copy-start | bytes 3145732
  3.6 18.9 %collective-permute-start = (bf16[192,1024]{1,0:T(8,128)(2,1)}, bf16[192,1024]{1,0:T(8,128)(2,1)S(1)}, u32[]{:S(2)}, u32[]{:S(2)}) collective-permute-start(bf16[192,1024]{1,0:T(8,128)(2,1)} %get-tuple-element.31), channel_id=1, source_target_pairs={{0,6},{2,4},{4,2},{6,0},{1,7},{3,5},{5,3},{7,1},{8,14},{10,12},{12... | collective-permute-start | bytes 1179656 | tf_op jit(solution)/shard_map/ppermute | solution.py:246
  5.0 17.5 %collective-permute-start.1 = (bf16[192,1024]{1,0:T(8,128)(2,1)}, bf16[192,1024]{1,0:T(8,128)(2,1)S(1)}, u32[]{:S(2)}, u32[]{:S(2)}) collective-permute-start(bf16[192,1024]{1,0:T(8,128)(2,1)} %get-tuple-element.32.refs_9_), channel_id=1, source_target_pairs={{0,8},{8,0},{16,24},{24,16},{1,9},{9,1},{17,25},{25,17},{2,10},{10... | collective-permute-start | bytes 1179656 | tf_op jit(solution)/shard_map/ppermute | solution.py:249
  6.2 16.3 %collective-permute-start.2 = (bf16[192,1024]{1,0:T(8,128)(2,1)}, bf16[192,1024]{1,0:T(8,128)(2,1)S(1)}, u32[]{:S(2)}, u32[]{:S(2)}) collective-permute-start(bf16[192,1024]{1,0:T(8,128)(2,1)} %get-tuple-element.32.refs_9_), channel_id=1, source_target_pairs={{0,16},{8,24},{16,0},{24,8},{1,17},{9,25},{17,1},{25,9},{2,18},{10... | collective-permute-start | bytes 1179656 | tf_op jit(solution)/shard_map/ppermute | solution.py:249
  7.4 17.5 %collective-permute-start.8 = (bf16[192,1024]{1,0:T(8,128)(2,1)}, bf16[192,1024]{1,0:T(8,128)(2,1)S(1)}, u32[]{:S(2)}, u32[]{:S(2)}) collective-permute-start(bf16[192,1024]{1,0:T(8,128)(2,1)} %get-tuple-element.32.refs_9_), channel_id=1, source_target_pairs={{0,24},{8,16},{16,8},{24,0},{1,25},{9,17},{17,9},{25,1},{2,26},{10... | collective-permute-start | bytes 1179656 | tf_op jit(solution)/shard_map/ppermute | solution.py:249
  7.6 2.2 %copy-start.3 = (s32[128,1]{0,1:T(1,128)S(1)}, s32[128,1]{0,1:T(1,128)}, u32[]{:S(2)}) copy-start(s32[128,1]{0,1:T(1,128)} %param.9) | copy-start | bytes 1540
  7.6 17.3 %collective-permute-start.7 = (bf16[192,1024]{1,0:T(8,128)(2,1)}, bf16[192,1024]{1,0:T(8,128)(2,1)S(1)}, u32[]{:S(2)}, u32[]{:S(2)}) collective-permute-start(bf16[192,1024]{1,0:T(8,128)(2,1)} %get-tuple-element.37), channel_id=1, source_target_pairs={{0,2},{2,0},{4,6},{6,4},{1,3},{3,1},{5,7},{7,5},{8,10},{10,8},{12,... | collective-permute-start | bytes 1179656 | tf_op jit(solution)/shard_map/ppermute | solution.py:246
  9.8 1.2 copy-start.2
  11.0 12.7 %copy-start.4 = (bf16[192,1024]{1,0:T(8,128)(2,1)S(1)}, bf16[192,1024]{1,0:T(8,128)(2,1)}, u32[]{:S(2)}) copy-start(bf16[192,1024]{1,0:T(8,128)(2,1)} %get-tuple-element.36) | copy-start | bytes 1179652
  22.5 7.3 %collective-permute-start.3 = (bf16[192,1024]{1,0:T(8,128)(2,1)S(1)}, bf16[192,1024]{1,0:T(8,128)(2,1)S(1)}, u32[]{:S(2)}, u32[]{:S(2)}) collective-permute-start(bf16[192,1024]{1,0:T(8,128)(2,1)S(1)} %collective-permute-done.refs_0_), channel_id=1, source_target_pairs={{0,8},{8,0},{16,24},{24,16},{1,9},{9,1},{17,25},{25,17},{2,10},{10... | collective-permute-start | bytes 1179656 | tf_op jit(solution)/shard_map/ppermute | solution.py:249
  23.7 15.3 %collective-permute-start.6 = (bf16[192,1024]{1,0:T(8,128)(2,1)S(1)}, bf16[192,1024]{1,0:T(8,128)(2,1)S(1)}, u32[]{:S(2)}, u32[]{:S(2)}) collective-permute-start(bf16[192,1024]{1,0:T(8,128)(2,1)S(1)} %copy-done.4), channel_id=1, source_target_pairs={{0,4},{2,6},{4,0},{6,2},{1,5},{3,7},{5,1},{7,3},{8,12},{10,14},{12... | collective-permute-start | bytes 1179656 | tf_op jit(solution)/shard_map/ppermute | solution.py:246
  23.7 18.4 %collective-permute-start.4 = (bf16[192,1024]{1,0:T(8,128)(2,1)S(1)}, bf16[192,1024]{1,0:T(8,128)(2,1)S(1)}, u32[]{:S(2)}, u32[]{:S(2)}) collective-permute-start(bf16[192,1024]{1,0:T(8,128)(2,1)S(1)} %collective-permute-done.refs_0_), channel_id=1, source_target_pairs={{0,16},{8,24},{16,0},{24,8},{1,17},{9,25},{17,1},{25,9},{2,18},{10... | collective-permute-start | bytes 1179656 | tf_op jit(solution)/shard_map/ppermute | solution.py:249
  25.0 17.8 %collective-permute-start.9 = (bf16[192,1024]{1,0:T(8,128)(2,1)S(1)}, bf16[192,1024]{1,0:T(8,128)(2,1)S(1)}, u32[]{:S(2)}, u32[]{:S(2)}) collective-permute-start(bf16[192,1024]{1,0:T(8,128)(2,1)S(1)} %collective-permute-done.7.refs_13_), channel_id=1, source_target_pairs={{0,8},{8,0},{16,24},{24,16},{1,9},{9,1},{17,25},{25,17},{2,10},{10... | collective-permute-start | bytes 1179656 | tf_op jit(solution)/shard_map/ppermute | solution.py:249
  25.7 17.3 %collective-permute-start.12 = (bf16[192,1024]{1,0:T(8,128)(2,1)S(1)}, bf16[192,1024]{1,0:T(8,128)(2,1)S(1)}, u32[]{:S(2)}, u32[]{:S(2)}) collective-permute-start(bf16[192,1024]{1,0:T(8,128)(2,1)S(1)} %collective-permute-done.7.refs_13_), channel_id=1, source_target_pairs={{0,16},{8,24},{16,0},{24,8},{1,17},{9,25},{17,1},{25,9},{2,18},{10... | collective-permute-start | bytes 1179656 | tf_op jit(solution)/shard_map/ppermute | solution.py:249
  29.8 17.9 %collective-permute-start.5 = (bf16[192,1024]{1,0:T(8,128)(2,1)S(1)}, bf16[192,1024]{1,0:T(8,128)(2,1)S(1)}, u32[]{:S(2)}, u32[]{:S(2)}) collective-permute-start(bf16[192,1024]{1,0:T(8,128)(2,1)S(1)} %collective-permute-done.3.refs_1_), channel_id=1, source_target_pairs={{0,16},{8,24},{16,0},{24,8},{1,17},{9,25},{17,1},{25,9},{2,18},{10... | collective-permute-start | bytes 1179656 | tf_op jit(solution)/shard_map/ppermute | solution.py:249
  39.0 20.2 %collective-permute-start.16 = (bf16[48,4096]{1,0:T(8,128)(2,1)S(1)}, bf16[48,4096]{1,0:T(8,128)(2,1)S(1)}, u32[]{:S(2)}, u32[]{:S(2)}) collective-permute-start(bf16[48,4096]{1,0:T(8,128)(2,1)S(1)} %get-tuple-element.43), channel_id=1, source_target_pairs={{0,4},{2,6},{4,0},{6,2},{1,5},{3,7},{5,1},{7,3},{8,12},{10,14},{12... | collective-permute-start | bytes 1179656 | tf_op jit(solution)/shard_map/ppermute | solution.py:246
  42.1 25.3 %copy-start = (bf16[192,1024]{1,0:T(8,128)(2,1)S(1)}, bf16[192,1024]{1,0:T(8,128)(2,1)}, u32[]{:S(2)}) copy-start(bf16[192,1024]{1,0:T(8,128)(2,1)} %get-tuple-element.32.refs_9_) | copy-start | bytes 1179652
  42.1 17.8 %collective-permute-start.17 = (bf16[48,4096]{1,0:T(8,128)(2,1)S(1)}, bf16[48,4096]{1,0:T(8,128)(2,1)S(1)}, u32[]{:S(2)}, u32[]{:S(2)}) collective-permute-start(bf16[48,4096]{1,0:T(8,128)(2,1)S(1)} %get-tuple-element.45), channel_id=1, source_target_pairs={{0,2},{2,0},{4,6},{6,4},{1,3},{3,1},{5,7},{7,5},{8,10},{10,8},{12,... | collective-permute-start | bytes 1179656 | tf_op jit(solution)/shard_map/ppermute | solution.py:246
  42.7 18.5 %collective-permute-start.10 = (bf16[192,1024]{1,0:T(8,128)(2,1)S(1)}, bf16[192,1024]{1,0:T(8,128)(2,1)S(1)}, u32[]{:S(2)}, u32[]{:S(2)}) collective-permute-start(bf16[192,1024]{1,0:T(8,128)(2,1)S(1)} %collective-permute-done.6.refs_4_), channel_id=1, source_target_pairs={{0,8},{8,0},{16,24},{24,16},{1,9},{9,1},{17,25},{25,17},{2,10},{10... | collective-permute-start | bytes 1179656 | tf_op jit(solution)/shard_map/ppermute | solution.py:249
  43.0 18.2 %collective-permute-start.11 = (bf16[192,1024]{1,0:T(8,128)(2,1)S(1)}, bf16[192,1024]{1,0:T(8,128)(2,1)S(1)}, u32[]{:S(2)}, u32[]{:S(2)}) collective-permute-start(bf16[192,1024]{1,0:T(8,128)(2,1)S(1)} %collective-permute-done.6.refs_4_), channel_id=1, source_target_pairs={{0,16},{8,24},{16,0},{24,8},{1,17},{9,25},{17,1},{25,9},{2,18},{10... | collective-permute-start | bytes 1179656 | tf_op jit(solution)/shard_map/ppermute | solution.py:249
  47.7 13.5 %collective-permute-start.13 = (bf16[192,1024]{1,0:T(8,128)(2,1)S(1)}, bf16[192,1024]{1,0:T(8,128)(2,1)S(1)}, u32[]{:S(2)}, u32[]{:S(2)}) collective-permute-start(bf16[192,1024]{1,0:T(8,128)(2,1)S(1)} %collective-permute-done.12.refs_15_), channel_id=1, source_target_pairs={{0,8},{8,0},{16,24},{24,16},{1,9},{9,1},{17,25},{25,17},{2,10},{10... | collective-permute-start | bytes 1179656 | tf_op jit(solution)/shard_map/ppermute | solution.py:249
  59.2 8.3 %collective-permute-start.18 = (bf16[48,4096]{1,0:T(8,128)(2,1)S(1)}, bf16[48,4096]{1,0:T(8,128)(2,1)S(1)}, u32[]{:S(2)}, u32[]{:S(2)}) collective-permute-start(bf16[48,4096]{1,0:T(8,128)(2,1)S(1)} %collective-permute-done.16.refs_17_), channel_id=1, source_target_pairs={{0,1},{1,0},{2,3},{3,2},{4,5},{5,4},{6,7},{7,6},{8,9},{9,8},{10,11... | collective-permute-start | bytes 1179656 | tf_op jit(solution)/shard_map/ppermute | solution.py:252
  59.9 7.5 %collective-permute-start.19 = (bf16[48,4096]{1,0:T(8,128)(2,1)S(1)}, bf16[48,4096]{1,0:T(8,128)(2,1)S(1)}, u32[]{:S(2)}, u32[]{:S(2)}) collective-permute-start(bf16[48,4096]{1,0:T(8,128)(2,1)S(1)} %collective-permute-done.17.refs_18_), channel_id=1, source_target_pairs={{0,1},{1,0},{2,3},{3,2},{4,5},{5,4},{6,7},{7,6},{8,9},{9,8},{10,11... | collective-permute-start | bytes 1179656 | tf_op jit(solution)/shard_map/ppermute | solution.py:252
  61.2 4.6 %collective-permute-start.14 = (bf16[96,1024]{1,0:T(8,128)(2,1)S(1)}, bf16[96,1024]{1,0:T(8,128)(2,1)S(1)}, u32[]{:S(2)}, u32[]{:S(2)}) collective-permute-start(bf16[96,1024]{1,0:T(8,128)(2,1)S(1)} %slice.6), channel_id=1, source_target_pairs={{0,16},{8,24},{16,0},{24,8},{1,17},{9,25},{17,1},{25,9},{2,18},{10... | collective-permute-start | bytes 589832 | tf_op jit(solution)/shard_map/ppermute | solution.py:249
  62.6 4.9 %collective-permute-start.15 = (bf16[96,1024]{1,0:T(8,128)(2,1)S(1)}, bf16[96,1024]{1,0:T(8,128)(2,1)S(1)}, u32[]{:S(2)}, u32[]{:S(2)}) collective-permute-start(bf16[96,1024]{1,0:T(8,128)(2,1)S(1)} %slice.7), channel_id=1, source_target_pairs={{0,8},{8,0},{16,24},{24,16},{1,9},{9,1},{17,25},{25,17},{2,10},{10... | collective-permute-start | bytes 589832 | tf_op jit(solution)/shard_map/ppermute | solution.py:249
  62.6 17.4 %collective-permute-start.24 = (bf16[48,4096]{1,0:T(8,128)(2,1)S(1)}, bf16[48,4096]{1,0:T(8,128)(2,1)S(1)}, u32[]{:S(2)}, u32[]{:S(2)}) collective-permute-start(bf16[48,4096]{1,0:T(8,128)(2,1)S(1)} %get-tuple-element.51), channel_id=1, source_target_pairs={{0,6},{2,4},{4,2},{6,0},{1,7},{3,5},{5,3},{7,1},{8,14},{10,12},{12... | collective-permute-start | bytes 1179656 | tf_op jit(solution)/shard_map/ppermute | solution.py:246
  71.4 11.3 %collective-permute-start.20 = (bf16[48,4096]{1,0:T(8,128)(2,1)S(1)}, bf16[48,4096]{1,0:T(8,128)(2,1)S(1)}, u32[]{:S(2)}, u32[]{:S(2)}) collective-permute-start(bf16[48,4096]{1,0:T(8,128)(2,1)S(1)} %get-tuple-element.47), channel_id=1, source_target_pairs={{0,1},{1,0},{2,3},{3,2},{4,5},{5,4},{6,7},{7,6},{8,9},{9,8},{10,11... | collective-permute-start | bytes 1179656 | tf_op jit(solution)/shard_map/ppermute | solution.py:252
  75.4 12.9 %collective-permute-start.22 = (bf16[48,4096]{1,0:T(8,128)(2,1)S(1)}, bf16[48,4096]{1,0:T(8,128)(2,1)S(1)}, u32[]{:S(2)}, u32[]{:S(2)}) collective-permute-start(bf16[48,4096]{1,0:T(8,128)(2,1)S(1)} %get-tuple-element.49), channel_id=1, source_target_pairs={{0,1},{1,0},{2,3},{3,2},{4,5},{5,4},{6,7},{7,6},{8,9},{9,8},{10,11... | collective-permute-start | bytes 1179656 | tf_op jit(solution)/shard_map/ppermute | solution.py:252
  80.0 4.0 %collective-permute-start.25 = (bf16[48,4096]{1,0:T(8,128)(2,1)S(1)}, bf16[48,4096]{1,0:T(8,128)(2,1)S(1)}, u32[]{:S(2)}, u32[]{:S(2)}) collective-permute-start(bf16[48,4096]{1,0:T(8,128)(2,1)S(1)} %collective-permute-done.24.refs_17_), channel_id=1, source_target_pairs={{0,1},{1,0},{2,3},{3,2},{4,5},{5,4},{6,7},{7,6},{8,9},{9,8},{10,11... | collective-permute-start | bytes 1179656 | tf_op jit(solution)/shard_map/ppermute | solution.py:252
  82.8 17.3 %collective-permute-start.21 = (bf16[48,4096]{1,0:T(8,128)(2,1)S(1)}, bf16[48,4096]{1,0:T(8,128)(2,1)S(1)}, u32[]{:S(2)}, u32[]{:S(2)}) collective-permute-start(bf16[48,4096]{1,0:T(8,128)(2,1)S(1)} %add_convert_fusion.2), channel_id=1, source_target_pairs={{0,4},{2,6},{4,0},{6,2},{1,5},{3,7},{5,1},{7,3},{8,12},{10,14},{12... | collective-permute-start | bytes 1179656 | tf_op jit(solution)/shard_map/ppermute | solution.py:246
  87.9 12.7 %collective-permute-start.26 = (bf16[48,4096]{1,0:T(8,128)(2,1)S(1)}, bf16[48,4096]{1,0:T(8,128)(2,1)S(1)}, u32[]{:S(2)}, u32[]{:S(2)}) collective-permute-start(bf16[48,4096]{1,0:T(8,128)(2,1)S(1)} %get-tuple-element.55), channel_id=1, source_target_pairs={{0,1},{1,0},{2,3},{3,2},{4,5},{5,4},{6,7},{7,6},{8,9},{9,8},{10,11... | collective-permute-start | bytes 1179656 | tf_op jit(solution)/shard_map/ppermute | solution.py:252
  88.4 14.4 %collective-permute-start.23 = (bf16[48,4096]{1,0:T(8,128)(2,1)S(1)}, bf16[48,4096]{1,0:T(8,128)(2,1)S(1)}, u32[]{:S(2)}, u32[]{:S(2)}) collective-permute-start(bf16[48,4096]{1,0:T(8,128)(2,1)S(1)} %add_convert_fusion.1), channel_id=1, source_target_pairs={{0,2},{2,0},{4,6},{6,4},{1,3},{3,1},{5,7},{7,5},{8,10},{10,8},{12,... | collective-permute-start | bytes 1179656 | tf_op jit(solution)/shard_map/ppermute | solution.py:246
  100.1 2.8 %collective-permute-start.28 = (bf16[48,4096]{1,0:T(8,128)(2,1)S(1)}, bf16[48,4096]{1,0:T(8,128)(2,1)S(1)}, u32[]{:S(2)}, u32[]{:S(2)}) collective-permute-start(bf16[48,4096]{1,0:T(8,128)(2,1)S(1)} %collective-permute-done.21.refs_0_), channel_id=1, source_target_pairs={{0,1},{1,0},{2,3},{3,2},{4,5},{5,4},{6,7},{7,6},{8,9},{9,8},{10,11... | collective-permute-start | bytes 1179656 | tf_op jit(solution)/shard_map/ppermute | solution.py:252
  100.7 19.2 %collective-permute-start.27 = (bf16[48,4096]{1,0:T(8,128)(2,1)S(1)}, bf16[48,4096]{1,0:T(8,128)(2,1)S(1)}, u32[]{:S(2)}, u32[]{:S(2)}) collective-permute-start(bf16[48,4096]{1,0:T(8,128)(2,1)S(1)} %add_convert_fusion), channel_id=1, source_target_pairs={{0,6},{2,4},{4,2},{6,0},{1,7},{3,5},{5,3},{7,1},{8,14},{10,12},{12... | collective-permute-start | bytes 1179656 | tf_op jit(solution)/shard_map/ppermute | solution.py:246
  102.9 17.1 %collective-permute-start.29 = (bf16[48,4096]{1,0:T(8,128)(2,1)S(1)}, bf16[48,4096]{1,0:T(8,128)(2,1)S(1)}, u32[]{:S(2)}, u32[]{:S(2)}) collective-permute-start(bf16[48,4096]{1,0:T(8,128)(2,1)S(1)} %collective-permute-done.23.refs_1_), channel_id=1, source_target_pairs={{0,1},{1,0},{2,3},{3,2},{4,5},{5,4},{6,7},{7,6},{8,9},{9,8},{10,11... | collective-permute-start | bytes 1179656 | tf_op jit(solution)/shard_map/ppermute | solution.py:252
  103.8 16.9 %collective-permute-start.31 = (bf16[96,4096]{1,0:T(8,128)(2,1)S(1)}, bf16[96,4096]{1,0:T(8,128)(2,1)S(1)}, u32[]{:S(2)}, u32[]{:S(2)}) collective-permute-start(bf16[96,4096]{1,0:T(8,128)(2,1)S(1)} %get-tuple-element.58.refs_6_), channel_id=1, source_target_pairs={{0,1},{1,0},{2,3},{3,2},{4,5},{5,4},{6,7},{7,6},{8,9},{9,8},{10,11... | collective-permute-start | bytes 2359304 | tf_op jit(solution)/shard_map/ppermute | solution.py:252
  120.0 2.1 %collective-permute-start.30 = (bf16[48,4096]{1,0:T(8,128)(2,1)S(1)}, bf16[48,4096]{1,0:T(8,128)(2,1)S(1)}, u32[]{:S(2)}, u32[]{:S(2)}) collective-permute-start(bf16[48,4096]{1,0:T(8,128)(2,1)S(1)} %collective-permute-done.27.refs_2_), channel_id=1, source_target_pairs={{0,1},{1,0},{2,3},{3,2},{4,5},{5,4},{6,7},{7,6},{8,9},{9,8},{10,11... | collective-permute-start | bytes 1179656 | tf_op jit(solution)/shard_map/ppermute | solution.py:252

commit v7 on v6

--- a/solution.py
+++ b/solution.py
@@ -326,7 +326,7 @@
         awaited = [other[k]]
 
     order = (2, 1, 3)
-    blocks = 4
+    blocks = 16
     return tuple(
         pl.pallas_call(
             functools.partial(merge_kernel, order, capacity, blocks),

time: 124 us -> 124 us (level)
  no operation moved by 1% of the time
where the time goes in v7:
time: 124 us
  waiting for transfers between devices  78.1 us (63%)
  starting transfers between devices  29.6 us (24%)
  Pallas kernels  13.9 us (11%)
  local copies, waits for them, and re-layouts  1.27 us (1%)
    ppermute x9, waiting for transfers between devices, planes(): return lax.ppermute(chunk, 'expert', flips(n_experts, k))  64.3 us
    ppermute x10, starting transfers between devices, swapped(): return lax.ppermute(chunk, 'tensor', swap)  11.5 us
    ppermute x13, waiting for transfers between devices, spread(): return lax.ppermute(chunk, 'dp', flips(n_dp, step))  11.2 us
    ppermute x13, starting transfers between devices, spread(): return lax.ppermute(chunk, 'dp', flips(n_dp, step))  10.5 us
    pallas_call x2, Pallas kernels, aligned_plan(): pl.pallas_call(functools.partial(expert_kernel, [len(pieces) for pieces i...  7.77 us
    ppermute x9, starting transfers between devices, planes(): return lax.ppermute(chunk, 'expert', flips(n_experts, k))  7.54 us
    pallas_call x1, Pallas kernels, aligned_plan(): pl.pallas_call(functools.partial(select_kernel, n_experts, halves, shards...  2.96 us
    ppermute x10, waiting for transfers between devices, swapped(): return lax.ppermute(chunk, 'tensor', swap)  2.54 us
  transfers between devices with their start and end apart: 32, of which 13 were waited for; matrix products, arithmetic and copies ran while one was open for 0% of the time, Pallas kernels for 7%

profile of v7, /device:TPU:9, one launch (start us, length us, event | category | flops | bytes accessed | tf_op | source)
XLA Modules:
  0.0 123.9 jit_solution(6510587110544846363)
XLA Ops:
  0.6 3.0 %select_rows.1 = (bf16[192,1024]{1,0:T(8,128)(2,1)}, bf16[192,1024]{1,0:T(8,128)(2,1)}, bf16[192,1024]{1,0:T(8,128)(2,1)}, bf16[192,1024]{1,0:T(8,128)(2,1)}) custom-call(s32[4,512]{1,0:T(4,128)} %cluster_hbm.1, bf16[231,1024]{1,0:T(8,128)(2,1)} %gate_hbm.1, bf16[231,1024]{1,0:T(8,128)(2,1)} %up_hbm.1, bf16[231,1024]{1,0:T(8,128)(2,1)} %down_hbm.1), custom_call_target="tpu_custom_call" | custom-call | tf_op jit(solution)/shard_map/select_rows/pallas_call | solution.py:208
  3.6 1.4 %collective-permute-start = (bf16[192,1024]{1,0:T(8,128)(2,1)}, bf16[192,1024]{1,0:T(8,128)(2,1)S(1)}, u32[]{:S(2)}, u32[]{:S(2)}) collective-permute-start(bf16[192,1024]{1,0:T(8,128)(2,1)} %get-tuple-element.31), channel_id=1, source_target_pairs={{0,6},{2,4},{4,2},{6,0},{1,7},{3,5},{5,3},{7,1},{8,14},{10,12},{12... | collective-permute-start | bytes 1179656 | tf_op jit(solution)/shard_map/ppermute | solution.py:246
  5.0 1.2 collective-permute-start.1
  6.2 1.2 %collective-permute-start.2 = (bf16[192,1024]{1,0:T(8,128)(2,1)}, bf16[192,1024]{1,0:T(8,128)(2,1)S(1)}, u32[]{:S(2)}, u32[]{:S(2)}) collective-permute-start(bf16[192,1024]{1,0:T(8,128)(2,1)} %get-tuple-element.32.refs_9_), channel_id=1, source_target_pairs={{0,16},{8,24},{16,0},{24,8},{1,17},{9,25},{17,1},{25,9},{2,18},{10... | collective-permute-start | bytes 1179656 | tf_op jit(solution)/shard_map/ppermute | solution.py:249
  7.4 0.2 collective-permute-start.8
  7.6 2.2 %collective-permute-start.7 = (bf16[192,1024]{1,0:T(8,128)(2,1)}, bf16[192,1024]{1,0:T(8,128)(2,1)S(1)}, u32[]{:S(2)}, u32[]{:S(2)}) collective-permute-start(bf16[192,1024]{1,0:T(8,128)(2,1)} %get-tuple-element.37), channel_id=1, source_target_pairs={{0,2},{2,0},{4,6},{6,4},{1,3},{3,1},{5,7},{7,5},{8,10},{10,8},{12,... | collective-permute-start | bytes 1179656 | tf_op jit(solution)/shard_map/ppermute | solution.py:246
  9.8 1.2 copy-done.2
  11.0 1.4 %dispatch_rows.1 = (bf16[48,4096]{1,0:T(8,128)(2,1)S(1)}, bf16[48,4096]{1,0:T(8,128)(2,1)S(1)}, bf16[48,4096]{1,0:T(8,128)(2,1)S(1)}, bf16[48,4096]{1,0:T(8,128)...) custom-call(s32[1,128]{1,0:T(1,128)S(1)} %bitcast.1, bf16[128,4096]{1,0:T(8,128)(2,1)S(1)} %copy-done.1, ...), custom_call_target="tpu_custom_call" | custom-call | tf_op jit(solution)/shard_map/dispatch_rows/pallas_call | solution.py:226
  12.5 10.0 %collective-permute-done.refs_0_ = bf16[192,1024]{1,0:T(8,128)(2,1)S(1)} collective-permute-done((bf16[192,1024]{1,0:T(8,128)(2,1)}, bf16[192,1024]{1,0:T(8,128)(2,1)S(1)}, u32[]{:S(2)}, u32[]{:S(2)}) %collective-permute-start) | collective-permute-done | bytes 393248 | tf_op jit(solution)/shard_map/ppermute | solution.py:246
  22.5 1.2 collective-permute-start.3
  23.7 1.2 %collective-permute-start.4 = (bf16[192,1024]{1,0:T(8,128)(2,1)S(1)}, bf16[192,1024]{1,0:T(8,128)(2,1)S(1)}, u32[]{:S(2)}, u32[]{:S(2)}) collective-permute-start(bf16[192,1024]{1,0:T(8,128)(2,1)S(1)} %collective-permute-done.refs_0_), channel_id=1, source_target_pairs={{0,16},{8,24},{16,0},{24,8},{1,17},{9,25},{17,1},{25,9},{2,18},{10... | collective-permute-start | bytes 1179656 | tf_op jit(solution)/shard_map/ppermute | solution.py:249
  25.0 0.7 collective-permute-start.9
  25.7 1.2 collective-permute-start.12
  26.9 2.9 %collective-permute-done.3.refs_1_ = bf16[192,1024]{1,0:T(8,128)(2,1)S(1)} collective-permute-done((bf16[192,1024]{1,0:T(8,128)(2,1)S(1)}, bf16[192,1024]{1,0:T(8,128)(2,1)S(1)}, u32[]{:S(2)}, u32[]{:S(2)}) %collective-permute-start.3) | collective-permute-done | bytes 393248 | tf_op jit(solution)/shard_map/ppermute | solution.py:249
  29.8 0.7 collective-permute-start.5
  30.5 8.5 %collective-permute-done.6.refs_4_ = bf16[192,1024]{1,0:T(8,128)(2,1)S(1)} collective-permute-done((bf16[192,1024]{1,0:T(8,128)(2,1)S(1)}, bf16[192,1024]{1,0:T(8,128)(2,1)S(1)}, u32[]{:S(2)}, u32[]{:S(2)}) %collective-permute-start.6) | collective-permute-done | bytes 393248 | tf_op jit(solution)/shard_map/ppermute | solution.py:246
  39.0 3.1 %collective-permute-start.16 = (bf16[48,4096]{1,0:T(8,128)(2,1)S(1)}, bf16[48,4096]{1,0:T(8,128)(2,1)S(1)}, u32[]{:S(2)}, u32[]{:S(2)}) collective-permute-start(bf16[48,4096]{1,0:T(8,128)(2,1)S(1)} %get-tuple-element.43), channel_id=1, source_target_pairs={{0,4},{2,6},{4,0},{6,2},{1,5},{3,7},{5,1},{7,3},{8,12},{10,14},{12... | collective-permute-start | bytes 1179656 | tf_op jit(solution)/shard_map/ppermute | solution.py:246
  42.1 0.6 collective-permute-start.17
  42.7 0.2 collective-permute-start.10
  43.0 1.1 collective-permute-start.11
  44.1 3.6 %collective-permute-done.5.refs_3_ = bf16[192,1024]{1,0:T(8,128)(2,1)S(1)} collective-permute-done((bf16[192,1024]{1,0:T(8,128)(2,1)S(1)}, bf16[192,1024]{1,0:T(8,128)(2,1)S(1)}, u32[]{:S(2)}, u32[]{:S(2)}) %collective-permute-start.5) | collective-permute-done | bytes 393248 | tf_op jit(solution)/shard_map/ppermute | solution.py:249
  47.7 11.5 %collective-permute-done.16.refs_17_ = bf16[48,4096]{1,0:T(8,128)(2,1)S(1)} collective-permute-done((bf16[48,4096]{1,0:T(8,128)(2,1)S(1)}, bf16[48,4096]{1,0:T(8,128)(2,1)S(1)}, u32[]{:S(2)}, u32[]{:S(2)}) %collective-permute-start.16) | collective-permute-done | bytes 393248 | tf_op jit(solution)/shard_map/ppermute | solution.py:246
  59.2 0.7 collective-permute-start.18
  59.9 1.3 %collective-permute-start.19 = (bf16[48,4096]{1,0:T(8,128)(2,1)S(1)}, bf16[48,4096]{1,0:T(8,128)(2,1)S(1)}, u32[]{:S(2)}, u32[]{:S(2)}) collective-permute-start(bf16[48,4096]{1,0:T(8,128)(2,1)S(1)} %collective-permute-done.17.refs_18_), channel_id=1, source_target_pairs={{0,1},{1,0},{2,3},{3,2},{4,5},{5,4},{6,7},{7,6},{8,9},{9,8},{10,11... | collective-permute-start | bytes 1179656 | tf_op jit(solution)/shard_map/ppermute | solution.py:252
  61.2 1.3 %collective-permute-start.14 = (bf16[96,1024]{1,0:T(8,128)(2,1)S(1)}, bf16[96,1024]{1,0:T(8,128)(2,1)S(1)}, u32[]{:S(2)}, u32[]{:S(2)}) collective-permute-start(bf16[96,1024]{1,0:T(8,128)(2,1)S(1)} %slice.6), channel_id=1, source_target_pairs={{0,16},{8,24},{16,0},{24,8},{1,17},{9,25},{17,1},{25,9},{2,18},{10... | collective-permute-start | bytes 589832 | tf_op jit(solution)/shard_map/ppermute | solution.py:249
  62.6 0.1 collective-permute-start.15
  62.7 3.1 %collective-permute-done.14.refs_7_ = bf16[96,1024]{1,0:T(8,128)(2,1)S(1)} collective-permute-done((bf16[96,1024]{1,0:T(8,128)(2,1)S(1)}, bf16[96,1024]{1,0:T(8,128)(2,1)S(1)}, u32[]{:S(2)}, u32[]{:S(2)}) %collective-permute-start.14) | collective-permute-done | bytes 196640 | tf_op jit(solution)/shard_map/ppermute | solution.py:249
  65.8 1.6 %collective-permute-done.15.refs_8_ = bf16[96,1024]{1,0:T(8,128)(2,1)S(1)} collective-permute-done((bf16[96,1024]{1,0:T(8,128)(2,1)S(1)}, bf16[96,1024]{1,0:T(8,128)(2,1)S(1)}, u32[]{:S(2)}, u32[]{:S(2)}) %collective-permute-start.15) | collective-permute-done | bytes 196640 | tf_op jit(solution)/shard_map/ppermute | solution.py:249
  67.5 3.9 %expert_math.2 = (bf16[48,4096]{1,0:T(8,128)(2,1)S(1)}, bf16[48,4096]{1,0:T(8,128)(2,1)S(1)}, bf16[48,4096]{1,0:T(8,128)(2,1)S(1)}, bf16[48,4096]{1,0:T(8,128)(2,1)S(1)}) custom-call(bf16[192,1024]{1,0:T(8,128)(2,1)S(1)} %collective-permute-done.refs_0_, bf16[192,1024]{1,0:T(8,128)(2,1)S(1)} %collective-permute-done.3.refs_1_, ...), custom_call_target="tpu_custom_call" | custom-call | tf_op jit(solution)/shard_map/expert_math/pallas_call | solution.py:295
  71.4 4.1 %collective-permute-start.20 = (bf16[48,4096]{1,0:T(8,128)(2,1)S(1)}, bf16[48,4096]{1,0:T(8,128)(2,1)S(1)}, u32[]{:S(2)}, u32[]{:S(2)}) collective-permute-start(bf16[48,4096]{1,0:T(8,128)(2,1)S(1)} %get-tuple-element.47), channel_id=1, source_target_pairs={{0,1},{1,0},{2,3},{3,2},{4,5},{5,4},{6,7},{7,6},{8,9},{9,8},{10,11... | collective-permute-start | bytes 1179656 | tf_op jit(solution)/shard_map/ppermute | solution.py:252
  75.4 0.1 collective-permute-start.22
  75.5 4.5 %collective-permute-done.24.refs_17_ = bf16[48,4096]{1,0:T(8,128)(2,1)S(1)} collective-permute-done((bf16[48,4096]{1,0:T(8,128)(2,1)S(1)}, bf16[48,4096]{1,0:T(8,128)(2,1)S(1)}, u32[]{:S(2)}, u32[]{:S(2)}) %collective-permute-start.24) | collective-permute-done | bytes 393248 | tf_op jit(solution)/shard_map/ppermute | solution.py:246
  80.0 2.7 %collective-permute-start.25 = (bf16[48,4096]{1,0:T(8,128)(2,1)S(1)}, bf16[48,4096]{1,0:T(8,128)(2,1)S(1)}, u32[]{:S(2)}, u32[]{:S(2)}) collective-permute-start(bf16[48,4096]{1,0:T(8,128)(2,1)S(1)} %collective-permute-done.24.refs_17_), channel_id=1, source_target_pairs={{0,1},{1,0},{2,3},{3,2},{4,5},{5,4},{6,7},{7,6},{8,9},{9,8},{10,11... | collective-permute-start | bytes 1179656 | tf_op jit(solution)/shard_map/ppermute | solution.py:252
  82.7 0.1 add_convert_fusion.2
  82.8 1.2 collective-permute-done.25.refs_19_
  84.0 3.9 %expert_math.3 = (bf16[48,4096]{1,0:T(8,128)(2,1)S(1)}, bf16[48,4096]{1,0:T(8,128)(2,1)S(1)}, bf16[96,4096]{1,0:T(8,128)(2,1)S(1)}) custom-call(bf16[192,1024]{1,0:T(8,128)(2,1)S(1)} %collective-permute-done.refs_0_, bf16[192,1024]{1,0:T(8,128)(2,1)S(1)} %collective-permute-done.3.refs_1_, bf16[192,1024]{1,0:T(8,128)(2,1)S(1)} %collective-permute-done.4.refs_2_, ...), custom_call_target="tpu_custom_call" | custom-call | tf_op jit(solution)/shard_map/expert_math/pallas_call | solution.py:295
  87.9 0.4 collective-permute-start.26
  88.3 0.1 add_convert_fusion.1
  88.5 11.5 %collective-permute-done.21.refs_0_ = bf16[48,4096]{1,0:T(8,128)(2,1)S(1)} collective-permute-done((bf16[48,4096]{1,0:T(8,128)(2,1)S(1)}, bf16[48,4096]{1,0:T(8,128)(2,1)S(1)}, u32[]{:S(2)}, u32[]{:S(2)}) %collective-permute-start.21) | collective-permute-done | bytes 393248 | tf_op jit(solution)/shard_map/ppermute | solution.py:246
  100.1 0.6 collective-permute-start.28
  100.6 0.1 add_convert_fusion
  100.7 0.1 collective-permute-start.27
  100.8 2.1 %collective-permute-done.23.refs_1_ = bf16[48,4096]{1,0:T(8,128)(2,1)S(1)} collective-permute-done((bf16[48,4096]{1,0:T(8,128)(2,1)S(1)}, bf16[48,4096]{1,0:T(8,128)(2,1)S(1)}, u32[]{:S(2)}, u32[]{:S(2)}) %collective-permute-start.23) | collective-permute-done | bytes 393248 | tf_op jit(solution)/shard_map/ppermute | solution.py:246
  102.9 0.9 collective-permute-start.29
  103.8 16.2 %collective-permute-done.27.refs_2_ = bf16[48,4096]{1,0:T(8,128)(2,1)S(1)} collective-permute-done((bf16[48,4096]{1,0:T(8,128)(2,1)S(1)}, bf16[48,4096]{1,0:T(8,128)(2,1)S(1)}, u32[]{:S(2)}, u32[]{:S(2)}) %collective-permute-start.27) | collective-permute-done | bytes 393248 | tf_op jit(solution)/shard_map/ppermute | solution.py:246
  120.0 0.8 collective-permute-start.30
  120.8 1.3 %collective-permute-done.30.refs_5_ = bf16[48,4096]{1,0:T(8,128)(2,1)S(1)} collective-permute-done((bf16[48,4096]{1,0:T(8,128)(2,1)S(1)}, bf16[48,4096]{1,0:T(8,128)(2,1)S(1)}, u32[]{:S(2)}, u32[]{:S(2)}) %collective-permute-start.30) | collective-permute-done | bytes 393248 | tf_op jit(solution)/shard_map/ppermute | solution.py:252
  122.1 1.8 %merge_rows.1 = (bf16[128,4096]{1,0:T(8,128)(2,1)}, bf16[128,4096]{1,0:T(8,128)(2,1)}) custom-call(bf16[48,4096]{1,0:T(8,128)(2,1)S(1)} %collective-permute-done.21.refs_0_, bf16[48,4096]{1,0:T(8,128)(2,1)S(1)} %collective-permute-done.23.refs_1_, bf16[48,4096]{1,0:T(8,128)(2,1)S(1)} %collective-permute-done.27.refs_2_, ...), custom_call_target="tpu_custom_call" | custom-call | tf_op jit(solution)/shard_map/merge_rows/pallas_call | solution.py:331
  (36 shorter events, 0.3 us)
Async XLA Ops:
  0.6 9.2 %copy-start.1 = (bf16[128,4096]{1,0:T(8,128)(2,1)S(1)}, bf16[128,4096]{1,0:T(8,128)(2,1)}, u32[]{:S(2)}) copy-start(bf16[128,4096]{1,0:T(8,128)(2,1)} %tokens_ref.1) | copy-start | bytes 3145732
  3.6 18.9 %collective-permute-start = (bf16[192,1024]{1,0:T(8,128)(2,1)}, bf16[192,1024]{1,0:T(8,128)(2,1)S(1)}, u32[]{:S(2)}, u32[]{:S(2)}) collective-permute-start(bf16[192,1024]{1,0:T(8,128)(2,1)} %get-tuple-element.31), channel_id=1, source_target_pairs={{0,6},{2,4},{4,2},{6,0},{1,7},{3,5},{5,3},{7,1},{8,14},{10,12},{12... | collective-permute-start | bytes 1179656 | tf_op jit(solution)/shard_map/ppermute | solution.py:246
  5.0 17.5 %collective-permute-start.1 = (bf16[192,1024]{1,0:T(8,128)(2,1)}, bf16[192,1024]{1,0:T(8,128)(2,1)S(1)}, u32[]{:S(2)}, u32[]{:S(2)}) collective-permute-start(bf16[192,1024]{1,0:T(8,128)(2,1)} %get-tuple-element.32.refs_9_), channel_id=1, source_target_pairs={{0,8},{8,0},{16,24},{24,16},{1,9},{9,1},{17,25},{25,17},{2,10},{10... | collective-permute-start | bytes 1179656 | tf_op jit(solution)/shard_map/ppermute | solution.py:249
  6.2 16.3 %collective-permute-start.2 = (bf16[192,1024]{1,0:T(8,128)(2,1)}, bf16[192,1024]{1,0:T(8,128)(2,1)S(1)}, u32[]{:S(2)}, u32[]{:S(2)}) collective-permute-start(bf16[192,1024]{1,0:T(8,128)(2,1)} %get-tuple-element.32.refs_9_), channel_id=1, source_target_pairs={{0,16},{8,24},{16,0},{24,8},{1,17},{9,25},{17,1},{25,9},{2,18},{10... | collective-permute-start | bytes 1179656 | tf_op jit(solution)/shard_map/ppermute | solution.py:249
  7.4 17.5 %collective-permute-start.8 = (bf16[192,1024]{1,0:T(8,128)(2,1)}, bf16[192,1024]{1,0:T(8,128)(2,1)S(1)}, u32[]{:S(2)}, u32[]{:S(2)}) collective-permute-start(bf16[192,1024]{1,0:T(8,128)(2,1)} %get-tuple-element.32.refs_9_), channel_id=1, source_target_pairs={{0,24},{8,16},{16,8},{24,0},{1,25},{9,17},{17,9},{25,1},{2,26},{10... | collective-permute-start | bytes 1179656 | tf_op jit(solution)/shard_map/ppermute | solution.py:249
  7.6 2.2 %copy-start.3 = (s32[128,1]{0,1:T(1,128)S(1)}, s32[128,1]{0,1:T(1,128)}, u32[]{:S(2)}) copy-start(s32[128,1]{0,1:T(1,128)} %param.9) | copy-start | bytes 1540
  7.6 17.3 %collective-permute-start.7 = (bf16[192,1024]{1,0:T(8,128)(2,1)}, bf16[192,1024]{1,0:T(8,128)(2,1)S(1)}, u32[]{:S(2)}, u32[]{:S(2)}) collective-permute-start(bf16[192,1024]{1,0:T(8,128)(2,1)} %get-tuple-element.37), channel_id=1, source_target_pairs={{0,2},{2,0},{4,6},{6,4},{1,3},{3,1},{5,7},{7,5},{8,10},{10,8},{12,... | collective-permute-start | bytes 1179656 | tf_op jit(solution)/shard_map/ppermute | solution.py:246
  9.8 1.2 copy-start.2
  11.0 12.7 %copy-start.4 = (bf16[192,1024]{1,0:T(8,128)(2,1)S(1)}, bf16[192,1024]{1,0:T(8,128)(2,1)}, u32[]{:S(2)}) copy-start(bf16[192,1024]{1,0:T(8,128)(2,1)} %get-tuple-element.36) | copy-start | bytes 1179652
  22.5 7.3 %collective-permute-start.3 = (bf16[192,1024]{1,0:T(8,128)(2,1)S(1)}, bf16[192,1024]{1,0:T(8,128)(2,1)S(1)}, u32[]{:S(2)}, u32[]{:S(2)}) collective-permute-start(bf16[192,1024]{1,0:T(8,128)(2,1)S(1)} %collective-permute-done.refs_0_), channel_id=1, source_target_pairs={{0,8},{8,0},{16,24},{24,16},{1,9},{9,1},{17,25},{25,17},{2,10},{10... | collective-permute-start | bytes 1179656 | tf_op jit(solution)/shard_map/ppermute | solution.py:249
  23.7 15.3 %collective-permute-start.6 = (bf16[192,1024]{1,0:T(8,128)(2,1)S(1)}, bf16[192,1024]{1,0:T(8,128)(2,1)S(1)}, u32[]{:S(2)}, u32[]{:S(2)}) collective-permute-start(bf16[192,1024]{1,0:T(8,128)(2,1)S(1)} %copy-done.4), channel_id=1, source_target_pairs={{0,4},{2,6},{4,0},{6,2},{1,5},{3,7},{5,1},{7,3},{8,12},{10,14},{12... | collective-permute-start | bytes 1179656 | tf_op jit(solution)/shard_map/ppermute | solution.py:246
  23.7 18.4 %collective-permute-start.4 = (bf16[192,1024]{1,0:T(8,128)(2,1)S(1)}, bf16[192,1024]{1,0:T(8,128)(2,1)S(1)}, u32[]{:S(2)}, u32[]{:S(2)}) collective-permute-start(bf16[192,1024]{1,0:T(8,128)(2,1)S(1)} %collective-permute-done.refs_0_), channel_id=1, source_target_pairs={{0,16},{8,24},{16,0},{24,8},{1,17},{9,25},{17,1},{25,9},{2,18},{10... | collective-permute-start | bytes 1179656 | tf_op jit(solution)/shard_map/ppermute | solution.py:249
  25.0 17.8 %collective-permute-start.9 = (bf16[192,1024]{1,0:T(8,128)(2,1)S(1)}, bf16[192,1024]{1,0:T(8,128)(2,1)S(1)}, u32[]{:S(2)}, u32[]{:S(2)}) collective-permute-start(bf16[192,1024]{1,0:T(8,128)(2,1)S(1)} %collective-permute-done.7.refs_13_), channel_id=1, source_target_pairs={{0,8},{8,0},{16,24},{24,16},{1,9},{9,1},{17,25},{25,17},{2,10},{10... | collective-permute-start | bytes 1179656 | tf_op jit(solution)/shard_map/ppermute | solution.py:249
  25.7 17.3 %collective-permute-start.12 = (bf16[192,1024]{1,0:T(8,128)(2,1)S(1)}, bf16[192,1024]{1,0:T(8,128)(2,1)S(1)}, u32[]{:S(2)}, u32[]{:S(2)}) collective-permute-start(bf16[192,1024]{1,0:T(8,128)(2,1)S(1)} %collective-permute-done.7.refs_13_), channel_id=1, source_target_pairs={{0,16},{8,24},{16,0},{24,8},{1,17},{9,25},{17,1},{25,9},{2,18},{10... | collective-permute-start | bytes 1179656 | tf_op jit(solution)/shard_map/ppermute | solution.py:249
  29.8 17.9 %collective-permute-start.5 = (bf16[192,1024]{1,0:T(8,128)(2,1)S(1)}, bf16[192,1024]{1,0:T(8,128)(2,1)S(1)}, u32[]{:S(2)}, u32[]{:S(2)}) collective-permute-start(bf16[192,1024]{1,0:T(8,128)(2,1)S(1)} %collective-permute-done.3.refs_1_), channel_id=1, source_target_pairs={{0,16},{8,24},{16,0},{24,8},{1,17},{9,25},{17,1},{25,9},{2,18},{10... | collective-permute-start | bytes 1179656 | tf_op jit(solution)/shard_map/ppermute | solution.py:249
  39.0 20.2 %collective-permute-start.16 = (bf16[48,4096]{1,0:T(8,128)(2,1)S(1)}, bf16[48,4096]{1,0:T(8,128)(2,1)S(1)}, u32[]{:S(2)}, u32[]{:S(2)}) collective-permute-start(bf16[48,4096]{1,0:T(8,128)(2,1)S(1)} %get-tuple-element.43), channel_id=1, source_target_pairs={{0,4},{2,6},{4,0},{6,2},{1,5},{3,7},{5,1},{7,3},{8,12},{10,14},{12... | collective-permute-start | bytes 1179656 | tf_op jit(solution)/shard_map/ppermute | solution.py:246
  42.1 25.3 %copy-start = (bf16[192,1024]{1,0:T(8,128)(2,1)S(1)}, bf16[192,1024]{1,0:T(8,128)(2,1)}, u32[]{:S(2)}) copy-start(bf16[192,1024]{1,0:T(8,128)(2,1)} %get-tuple-element.32.refs_9_) | copy-start | bytes 1179652
  42.1 17.8 %collective-permute-start.17 = (bf16[48,4096]{1,0:T(8,128)(2,1)S(1)}, bf16[48,4096]{1,0:T(8,128)(2,1)S(1)}, u32[]{:S(2)}, u32[]{:S(2)}) collective-permute-start(bf16[48,4096]{1,0:T(8,128)(2,1)S(1)} %get-tuple-element.45), channel_id=1, source_target_pairs={{0,2},{2,0},{4,6},{6,4},{1,3},{3,1},{5,7},{7,5},{8,10},{10,8},{12,... | collective-permute-start | bytes 1179656 | tf_op jit(solution)/shard_map/ppermute | solution.py:246
  42.7 18.5 %collective-permute-start.10 = (bf16[192,1024]{1,0:T(8,128)(2,1)S(1)}, bf16[192,1024]{1,0:T(8,128)(2,1)S(1)}, u32[]{:S(2)}, u32[]{:S(2)}) collective-permute-start(bf16[192,1024]{1,0:T(8,128)(2,1)S(1)} %collective-permute-done.6.refs_4_), channel_id=1, source_target_pairs={{0,8},{8,0},{16,24},{24,16},{1,9},{9,1},{17,25},{25,17},{2,10},{10... | collective-permute-start | bytes 1179656 | tf_op jit(solution)/shard_map/ppermute | solution.py:249
  43.0 18.2 %collective-permute-start.11 = (bf16[192,1024]{1,0:T(8,128)(2,1)S(1)}, bf16[192,1024]{1,0:T(8,128)(2,1)S(1)}, u32[]{:S(2)}, u32[]{:S(2)}) collective-permute-start(bf16[192,1024]{1,0:T(8,128)(2,1)S(1)} %collective-permute-done.6.refs_4_), channel_id=1, source_target_pairs={{0,16},{8,24},{16,0},{24,8},{1,17},{9,25},{17,1},{25,9},{2,18},{10... | collective-permute-start | bytes 1179656 | tf_op jit(solution)/shard_map/ppermute | solution.py:249
  47.7 13.5 %collective-permute-start.13 = (bf16[192,1024]{1,0:T(8,128)(2,1)S(1)}, bf16[192,1024]{1,0:T(8,128)(2,1)S(1)}, u32[]{:S(2)}, u32[]{:S(2)}) collective-permute-start(bf16[192,1024]{1,0:T(8,128)(2,1)S(1)} %collective-permute-done.12.refs_15_), channel_id=1, source_target_pairs={{0,8},{8,0},{16,24},{24,16},{1,9},{9,1},{17,25},{25,17},{2,10},{10... | collective-permute-start | bytes 1179656 | tf_op jit(solution)/shard_map/ppermute | solution.py:249
  59.2 8.3 %collective-permute-start.18 = (bf16[48,4096]{1,0:T(8,128)(2,1)S(1)}, bf16[48,4096]{1,0:T(8,128)(2,1)S(1)}, u32[]{:S(2)}, u32[]{:S(2)}) collective-permute-start(bf16[48,4096]{1,0:T(8,128)(2,1)S(1)} %collective-permute-done.16.refs_17_), channel_id=1, source_target_pairs={{0,1},{1,0},{2,3},{3,2},{4,5},{5,4},{6,7},{7,6},{8,9},{9,8},{10,11... | collective-permute-start | bytes 1179656 | tf_op jit(solution)/shard_map/ppermute | solution.py:252
  59.9 7.5 %collective-permute-start.19 = (bf16[48,4096]{1,0:T(8,128)(2,1)S(1)}, bf16[48,4096]{1,0:T(8,128)(2,1)S(1)}, u32[]{:S(2)}, u32[]{:S(2)}) collective-permute-start(bf16[48,4096]{1,0:T(8,128)(2,1)S(1)} %collective-permute-done.17.refs_18_), channel_id=1, source_target_pairs={{0,1},{1,0},{2,3},{3,2},{4,5},{5,4},{6,7},{7,6},{8,9},{9,8},{10,11... | collective-permute-start | bytes 1179656 | tf_op jit(solution)/shard_map/ppermute | solution.py:252
  61.2 4.6 %collective-permute-start.14 = (bf16[96,1024]{1,0:T(8,128)(2,1)S(1)}, bf16[96,1024]{1,0:T(8,128)(2,1)S(1)}, u32[]{:S(2)}, u32[]{:S(2)}) collective-permute-start(bf16[96,1024]{1,0:T(8,128)(2,1)S(1)} %slice.6), channel_id=1, source_target_pairs={{0,16},{8,24},{16,0},{24,8},{1,17},{9,25},{17,1},{25,9},{2,18},{10... | collective-permute-start | bytes 589832 | tf_op jit(solution)/shard_map/ppermute | solution.py:249
  62.6 4.9 %collective-permute-start.15 = (bf16[96,1024]{1,0:T(8,128)(2,1)S(1)}, bf16[96,1024]{1,0:T(8,128)(2,1)S(1)}, u32[]{:S(2)}, u32[]{:S(2)}) collective-permute-start(bf16[96,1024]{1,0:T(8,128)(2,1)S(1)} %slice.7), channel_id=1, source_target_pairs={{0,8},{8,0},{16,24},{24,16},{1,9},{9,1},{17,25},{25,17},{2,10},{10... | collective-permute-start | bytes 589832 | tf_op jit(solution)/shard_map/ppermute | solution.py:249
  62.6 17.4 %collective-permute-start.24 = (bf16[48,4096]{1,0:T(8,128)(2,1)S(1)}, bf16[48,4096]{1,0:T(8,128)(2,1)S(1)}, u32[]{:S(2)}, u32[]{:S(2)}) collective-permute-start(bf16[48,4096]{1,0:T(8,128)(2,1)S(1)} %get-tuple-element.51), channel_id=1, source_target_pairs={{0,6},{2,4},{4,2},{6,0},{1,7},{3,5},{5,3},{7,1},{8,14},{10,12},{12... | collective-permute-start | bytes 1179656 | tf_op jit(solution)/shard_map/ppermute | solution.py:246
  71.4 11.3 %collective-permute-start.20 = (bf16[48,4096]{1,0:T(8,128)(2,1)S(1)}, bf16[48,4096]{1,0:T(8,128)(2,1)S(1)}, u32[]{:S(2)}, u32[]{:S(2)}) collective-permute-start(bf16[48,4096]{1,0:T(8,128)(2,1)S(1)} %get-tuple-element.47), channel_id=1, source_target_pairs={{0,1},{1,0},{2,3},{3,2},{4,5},{5,4},{6,7},{7,6},{8,9},{9,8},{10,11... | collective-permute-start | bytes 1179656 | tf_op jit(solution)/shard_map/ppermute | solution.py:252
  75.4 12.9 %collective-permute-start.22 = (bf16[48,4096]{1,0:T(8,128)(2,1)S(1)}, bf16[48,4096]{1,0:T(8,128)(2,1)S(1)}, u32[]{:S(2)}, u32[]{:S(2)}) collective-permute-start(bf16[48,4096]{1,0:T(8,128)(2,1)S(1)} %get-tuple-element.49), channel_id=1, source_target_pairs={{0,1},{1,0},{2,3},{3,2},{4,5},{5,4},{6,7},{7,6},{8,9},{9,8},{10,11... | collective-permute-start | bytes 1179656 | tf_op jit(solution)/shard_map/ppermute | solution.py:252
  80.0 4.0 %collective-permute-start.25 = (bf16[48,4096]{1,0:T(8,128)(2,1)S(1)}, bf16[48,4096]{1,0:T(8,128)(2,1)S(1)}, u32[]{:S(2)}, u32[]{:S(2)}) collective-permute-start(bf16[48,4096]{1,0:T(8,128)(2,1)S(1)} %collective-permute-done.24.refs_17_), channel_id=1, source_target_pairs={{0,1},{1,0},{2,3},{3,2},{4,5},{5,4},{6,7},{7,6},{8,9},{9,8},{10,11... | collective-permute-start | bytes 1179656 | tf_op jit(solution)/shard_map/ppermute | solution.py:252
  82.8 17.3 %collective-permute-start.21 = (bf16[48,4096]{1,0:T(8,128)(2,1)S(1)}, bf16[48,4096]{1,0:T(8,128)(2,1)S(1)}, u32[]{:S(2)}, u32[]{:S(2)}) collective-permute-start(bf16[48,4096]{1,0:T(8,128)(2,1)S(1)} %add_convert_fusion.2), channel_id=1, source_target_pairs={{0,4},{2,6},{4,0},{6,2},{1,5},{3,7},{5,1},{7,3},{8,12},{10,14},{12... | collective-permute-start | bytes 1179656 | tf_op jit(solution)/shard_map/ppermute | solution.py:246
  87.9 12.7 %collective-permute-start.26 = (bf16[48,4096]{1,0:T(8,128)(2,1)S(1)}, bf16[48,4096]{1,0:T(8,128)(2,1)S(1)}, u32[]{:S(2)}, u32[]{:S(2)}) collective-permute-start(bf16[48,4096]{1,0:T(8,128)(2,1)S(1)} %get-tuple-element.55), channel_id=1, source_target_pairs={{0,1},{1,0},{2,3},{3,2},{4,5},{5,4},{6,7},{7,6},{8,9},{9,8},{10,11... | collective-permute-start | bytes 1179656 | tf_op jit(solution)/shard_map/ppermute | solution.py:252
  88.4 14.4 %collective-permute-start.23 = (bf16[48,4096]{1,0:T(8,128)(2,1)S(1)}, bf16[48,4096]{1,0:T(8,128)(2,1)S(1)}, u32[]{:S(2)}, u32[]{:S(2)}) collective-permute-start(bf16[48,4096]{1,0:T(8,128)(2,1)S(1)} %add_convert_fusion.1), channel_id=1, source_target_pairs={{0,2},{2,0},{4,6},{6,4},{1,3},{3,1},{5,7},{7,5},{8,10},{10,8},{12,... | collective-permute-start | bytes 1179656 | tf_op jit(solution)/shard_map/ppermute | solution.py:246
  100.1 2.8 %collective-permute-start.28 = (bf16[48,4096]{1,0:T(8,128)(2,1)S(1)}, bf16[48,4096]{1,0:T(8,128)(2,1)S(1)}, u32[]{:S(2)}, u32[]{:S(2)}) collective-permute-start(bf16[48,4096]{1,0:T(8,128)(2,1)S(1)} %collective-permute-done.21.refs_0_), channel_id=1, source_target_pairs={{0,1},{1,0},{2,3},{3,2},{4,5},{5,4},{6,7},{7,6},{8,9},{9,8},{10,11... | collective-permute-start | bytes 1179656 | tf_op jit(solution)/shard_map/ppermute | solution.py:252
  100.7 19.2 %collective-permute-start.27 = (bf16[48,4096]{1,0:T(8,128)(2,1)S(1)}, bf16[48,4096]{1,0:T(8,128)(2,1)S(1)}, u32[]{:S(2)}, u32[]{:S(2)}) collective-permute-start(bf16[48,4096]{1,0:T(8,128)(2,1)S(1)} %add_convert_fusion), channel_id=1, source_target_pairs={{0,6},{2,4},{4,2},{6,0},{1,7},{3,5},{5,3},{7,1},{8,14},{10,12},{12... | collective-permute-start | bytes 1179656 | tf_op jit(solution)/shard_map/ppermute | solution.py:246
  102.9 17.1 %collective-permute-start.29 = (bf16[48,4096]{1,0:T(8,128)(2,1)S(1)}, bf16[48,4096]{1,0:T(8,128)(2,1)S(1)}, u32[]{:S(2)}, u32[]{:S(2)}) collective-permute-start(bf16[48,4096]{1,0:T(8,128)(2,1)S(1)} %collective-permute-done.23.refs_1_), channel_id=1, source_target_pairs={{0,1},{1,0},{2,3},{3,2},{4,5},{5,4},{6,7},{7,6},{8,9},{9,8},{10,11... | collective-permute-start | bytes 1179656 | tf_op jit(solution)/shard_map/ppermute | solution.py:252
  103.8 16.9 %collective-permute-start.31 = (bf16[96,4096]{1,0:T(8,128)(2,1)S(1)}, bf16[96,4096]{1,0:T(8,128)(2,1)S(1)}, u32[]{:S(2)}, u32[]{:S(2)}) collective-permute-start(bf16[96,4096]{1,0:T(8,128)(2,1)S(1)} %get-tuple-element.58.refs_6_), channel_id=1, source_target_pairs={{0,1},{1,0},{2,3},{3,2},{4,5},{5,4},{6,7},{7,6},{8,9},{9,8},{10,11... | collective-permute-start | bytes 2359304 | tf_op jit(solution)/shard_map/ppermute | solution.py:252
  120.0 2.1 %collective-permute-start.30 = (bf16[48,4096]{1,0:T(8,128)(2,1)S(1)}, bf16[48,4096]{1,0:T(8,128)(2,1)S(1)}, u32[]{:S(2)}, u32[]{:S(2)}) collective-permute-start(bf16[48,4096]{1,0:T(8,128)(2,1)S(1)} %collective-permute-done.27.refs_2_), channel_id=1, source_target_pairs={{0,1},{1,0},{2,3},{3,2},{4,5},{5,4},{6,7},{7,6},{8,9},{9,8},{10,11... | collective-permute-start | bytes 1179656 | tf_op jit(solution)/shard_map/ppermute | solution.py:252
